TPU v7x, 32 devices: a whole 2x2x4 slice. The times are simulated.
32 devices in a mesh: win: 8 (over z, y), ch: 4 (over x, core).
Axes of the slice: x: 2, y: 2, z: 4, core: 2. Of those that a mesh axis runs over, the one named last changes fastest.
Arguments:
- tokens: bfloat16 [2, 64, 196, 384], P(None, ('win', 'ch')), may hold values from -6 to 6
- valid_rows: int32 [2, 64], P(None, ('win', 'ch')), may hold values from 7 to 14
- valid_cols: int32 [2, 64], P(None, ('win', 'ch')), may hold values from 7 to 14
- partner: int32 [2, 64], P(None, ('win', 'ch')), may hold values from 0 to 63
- mix_level: int32 [2, 64], P(None, ('win', 'ch')), may hold values from 1 to 15
- labels: int32 [2, 64], replicated, may hold values from 0 to 999
- w_qkv: float32 [2, 384, 1152], P(None, 'win', 'ch'), may hold values from -0.3125 to 0.3125
- m_qkv: float32 [2, 384, 1152], P(None, 'win', 'ch'), may hold values from -0.00036621094 to 0.00036621094
- v_qkv: float32 [2, 384, 1152], P(None, 'win', 'ch'), may hold values from 6.348181e-10 to 2.5392723e-09
- w_proj: float32 [2, 384, 384], P(None, 'win', 'ch'), may hold values from -0.875 to 0.875
- m_proj: float32 [2, 384, 384], P(None, 'win', 'ch'), may hold values from -0.00036621094 to 0.00036621094
- v_proj: float32 [2, 384, 384], P(None, 'win', 'ch'), may hold values from 6.348181e-10 to 2.5392723e-09
- w_fc1: float32 [2, 384, 1536], P(None, 'win', 'ch'), may hold values from -0.3125 to 0.3125
- m_fc1: float32 [2, 384, 1536], P(None, 'win', 'ch'), may hold values from -0.00036621094 to 0.00036621094
- v_fc1: float32 [2, 384, 1536], P(None, 'win', 'ch'), may hold values from 6.348181e-10 to 2.5392723e-09
- w_fc2: float32 [2, 1536, 384], P(None, 'ch', 'win'), may hold values from -0.15625 to 0.15625
- m_fc2: float32 [2, 1536, 384], P(None, 'ch', 'win'), may hold values from -0.00036621094 to 0.00036621094
- v_fc2: float32 [2, 1536, 384], P(None, 'ch', 'win'), may hold values from 6.348181e-10 to 2.5392723e-09
- w_head: float32 [384, 1000], P('win', 'ch'), may hold values from -0.3125 to 0.3125
- m_head: float32 [384, 1000], P('win', 'ch'), may hold values from -0.00036621094 to 0.00036621094
- v_head: float32 [384, 1000], P('win', 'ch'), may hold values from 6.348181e-10 to 2.5392723e-09
- vectors: float32 [29, 384], replicated, as said below
- m_vec: float32 [29, 384], replicated, may hold values from -0.00036621094 to 0.00036621094
- v_vec: float32 [29, 384], replicated, may hold values from 6.348181e-10 to 2.5392723e-09
- rel_table: float32 [2, 169, 12], replicated, may hold values from -3 to 3
- m_rel: float32 [2, 169, 12], replicated, may hold values from -2.2888184e-05 to 2.2888184e-05
- v_rel: float32 [2, 169, 12], replicated, may hold values from 1.015709e-12 to 4.062836e-12
Outputs:
- loss_total: float32 [], replicated
- grad_norm: float32 [], replicated
- qkv_first: float32 [2, 384, 1152], P(None, 'win', 'ch')
- qkv_second: float32 [2, 384, 1152], P(None, 'win', 'ch')
- qkv_weight: float32 [2, 384, 1152], P(None, 'win', 'ch')
- proj_first: float32 [2, 384, 384], P(None, 'win', 'ch')
- proj_second: float32 [2, 384, 384], P(None, 'win', 'ch')
- proj_weight: float32 [2, 384, 384], P(None, 'win', 'ch')
- expand_first: float32 [2, 384, 1536], P(None, 'win', 'ch')
- expand_second: float32 [2, 384, 1536], P(None, 'win', 'ch')
- expand_weight: float32 [2, 384, 1536], P(None, 'win', 'ch')
- reduce_first: float32 [2, 1536, 384], P(None, 'ch', 'win')
- reduce_second: float32 [2, 1536, 384], P(None, 'ch', 'win')
- reduce_weight: float32 [2, 1536, 384], P(None, 'ch', 'win')
- head_first: float32 [384, 1000], P('win', 'ch')
- head_second: float32 [384, 1000], P('win', 'ch')
- head_weight: float32 [384, 1000], P('win', 'ch')
- vector_first: float32 [29, 384], replicated
- vector_second: float32 [29, 384], replicated
- vector_weight: float32 [29, 384], replicated
- table_first: float32 [2, 169, 12], replicated
- table_second: float32 [2, 169, 12], replicated
- table_weight: float32 [2, 169, 12], replicated
Inputs may be any that keep to these rules, and one draw needn't show every extreme that they name: `valid_rows`: padding rows are the image's last ones. `valid_cols`: padding columns are the image's last ones. `vectors`: gains lie near one, biases near zero.
All inputs are finite; a program needn't handle non-finite values.
Results may differ from a plain program's by a relative error of at most 0.024.
Values may be sent and summed in bfloat16 or wider, within the bound.
No kernel may reach another device: no remote copies, remote signals or barrier semaphores. Data moves between devices by JAX's collectives and lax.ppermute only.
A program may use at most 256 MiB of HBM per device.

v0:
```python
import functools

import jax
import jax.numpy as jnp
import numpy as np
from jax import lax
from jax.experimental import pallas as pl
from jax.experimental.pallas import tpu as pltpu
from jax.sharding import PartitionSpec as P

C = 384
HID = 1536
CLASSES = 1000
CLASS_PAD = 1024
WSIDE = 7
GRID = 14
STEP = 10
HEADS = 12
PER_LAYER = 8 + HID // C
DEPTH = 32
CELLS = GRID * GRID
ROWS = 208
AREA = WSIDE * WSIDE
SLOT = 64
NWIN = 4
NGRP = 3
PACK = 4
WROWS = NWIN * SLOT
LANES = PACK * SLOT

NORM_EPS = 1e-05
CLIP_NORM = 0.05
LEARN_RATE = 0.04
SMALL_RATE = 0.2
DECAY_RATE = 0.05
ADAM_EPS = 1e-08
MASKED = -1e30
SCALE = DEPTH ** (-0.5)
F32 = jnp.float32
BF16 = jnp.bfloat16
NN = (((1,), (0,)), ((), ()))
NT = (((1,), (1,)), ((), ()))
TN = (((0,), (0,)), ((), ()))
VMEM_LIMIT = 24 * 1024 * 1024
GROUP = 2
CHUNK = 512


def dot(a, b, dims=NN):
    return lax.dot_general(a, b, dims, preferred_element_type=F32)


@functools.lru_cache(None)
def window_tables(shifted):
    perm = np.zeros((WROWS, ROWS), np.float32)
    row_limit = np.full((NWIN, SLOT, 2 * SLOT), 99, np.int32)
    col_limit = np.full((NWIN, SLOT, 2 * SLOT), 99, np.int32)
    shift = WSIDE // 2 if shifted else 0

    def band(v):
        return 0 if v < GRID - WSIDE else (1 if v < GRID - WSIDE // 2 else 2)

    for window in range(NWIN):
        wr, wc = divmod(window, GRID // WSIDE)
        place = []
        for j in range(AREA):
            r, c = wr * WSIDE + j // WSIDE, wc * WSIDE + j % WSIDE
            region = 3 * band(r) + band(c) if shifted else 0
            source = ((r + shift) % GRID, (c + shift) % GRID)
            place.append((region, source))
            perm[window * SLOT + j, source[0] * GRID + source[1]] = 1
        for j in range(SLOT):
            for i in range(SLOT):
                if i == j:
                    pair = (-1, -1)
                elif i < AREA and j < AREA and place[i][0] == place[j][0]:
                    pair = place[j][1]
                else:
                    pair = (99, 99)
                row_limit[window, j, i::SLOT] = pair[0]
                col_limit[window, j, i::SLOT] = pair[1]
    return perm, row_limit, col_limit


@functools.lru_cache(None)
def relative_onehot():
    span = 2 * WSIDE - 1
    onehot = np.zeros((span * span, SLOT, SLOT), np.float32)
    for i in range(AREA):
        for j in range(AREA):
            row, col = i // WSIDE - j // WSIDE, i % WSIDE - j % WSIDE
            onehot[(row + WSIDE - 1) * span + col + WSIDE - 1, j, i] = 1
    return onehot.reshape(span * span, SLOT * SLOT)


def norm_parts(field):
    average = jnp.mean(field, -1, keepdims=True)
    centered = field - average
    spread = jnp.mean(centered * centered, -1, keepdims=True)
    rate = lax.rsqrt(spread + NORM_EPS)
    return centered * rate, rate


def norm_back(grad, hat, rate, gain):
    scaled = grad * gain
    return rate * (
        scaled
        - jnp.mean(scaled, -1, keepdims=True)
        - hat * jnp.mean(scaled * hat, -1, keepdims=True)
    )


def col_sum(field):
    return jnp.sum(field, 0, keepdims=True)


def head_masks(dtype):
    lane = lax.broadcasted_iota(jnp.int32, (SLOT, 128), 1)
    return [((lane // DEPTH) == h).astype(F32).astype(dtype) for h in range(PACK)]


def spread_heads(block, masks):
    return jnp.concatenate([block * m for m in masks], 0)


def relative_owners(bits):
    owners = []
    for index in range(1 << len(bits)):
        offset = 0
        for n, (_, bit) in enumerate(bits):
            offset |= ((index >> (len(bits) - 1 - n)) & 1) << bit
        owners.append(offset)
    return owners


def owner_part(ref, owner, width, start, size):
    if len(ref.shape) == 3:
        return ref.at[owner, :, start : start + size]
    return ref.at[:, pl.ds(pl.multiple_of(owner * width + start, 128), size)]


def load_blocks(pieces, target, width, sem, me_ref):
    for ref, owners, cut in pieces:
        if owners is None:
            pltpu.make_async_copy(ref, target, sem).start()
            continue
        source, size, start = cut
        for n, owner in enumerate(owners):
            pltpu.make_async_copy(
                ref.at[n, :, source : source + size],
                owner_part(target, me_ref[1] ^ owner, width, start, size),
                sem,
            ).start()


def wait_all(ref, sem):
    pltpu.make_async_copy(ref, ref, sem).wait()


def store_blocks(source, outs, width, sems, me_ref):
    for number, (ref, owners, start, source_start, size) in enumerate(outs):
        if owners is None:
            copy = pltpu.make_async_copy(source, ref, sems.at[number])
            copy.start()
            copy.wait()
            continue
        for n, owner in enumerate(owners):
            pltpu.make_async_copy(
                owner_part(source, me_ref[1] ^ owner, width, source_start, size),
                ref.at[n, :, start : start + size],
                sems.at[number],
            ).start()


def wait_blocks(outs, sems):
    for number, (ref, owners, *_) in enumerate(outs):
        if owners is not None:
            wait_all(ref, sems.at[number])


def join_attention(stage, w_qkv, w_proj):
    owners = stage.shape[0]
    wide, narrow = 3 * C // owners, C // owners
    w_qkv[...] = jnp.concatenate([stage[n, :, :wide] for n in range(owners)], 1)
    w_proj[...] = jnp.concatenate([stage[n, :, wide : wide + narrow] for n in range(owners)], 1)


def pick_heads(first, second):
    lane = lax.broadcasted_iota(jnp.int32, (DEPTH, 128), 1)
    parts = []
    for h in range(PACK):
        at = (slice(h * DEPTH, (h + 1) * DEPTH), slice(h // 2 * 128, (h // 2 + 1) * 128))
        one, two = first[at], second[at]
        if h % 2:
            one = pltpu.roll(one, SLOT, 1)
        else:
            two = pltpu.roll(two, SLOT, 1)
        parts.append(jnp.where(lane < SLOT, one, two))
    return jnp.concatenate(parts, 0)


def apply_pair(rows_ref, cut, eye, first, second):
    turned = dot(eye, rows_ref[cut], NT).astype(BF16)
    empty = jnp.zeros_like(first)
    full = dot(
        turned,
        jnp.concatenate(
            [jnp.concatenate([first, empty], 1), jnp.concatenate([empty, second], 1)], 0
        ),
    )
    return pick_heads(full[:, :LANES], full[:, LANES:])


def identity():
    shape = (128, 128)
    same = lax.broadcasted_iota(jnp.int32, shape, 0) == lax.broadcasted_iota(jnp.int32, shape, 1)
    return same.astype(F32).astype(BF16)


def pipelined(units, first, second, third):
    ones, twos = {}, {}
    count = len(units)
    for n in range(count + 2):
        if n < count:
            ones[n] = first(*units[n])
        if 1 <= n <= count:
            twos[n - 1] = second(*units[n - 1], ones.pop(n - 1))
        if n >= 2:
            third(*units[n - 2], twos.pop(n - 2))


def each_image(images, body, unrolled):
    lax.fori_loop(0, images, body, 0, unroll=images if unrolled else 1)


def forward_attention(
    field, sizes, w_qkv, w_proj, perm, perm_t, row_limit, col_limit, bias, small, qkv_bias,
    qkv_ref, prob_ref, windowed_ref, mixed_ref, attended_ref, unrolled,
):
    hat, _ = norm_parts(field)
    normed = (hat * small[0:1] + small[1:2]).astype(BF16)
    images = len(sizes)
    for b in range(images):
        windowed_ref[b] = dot(perm[...], normed[b * ROWS : (b + 1) * ROWS]).astype(BF16)
    flat = windowed_ref[...].reshape(images * WROWS, C)
    qkv = (dot(flat, w_qkv[...]) + qkv_bias).astype(BF16)
    qkv_ref[...] = qkv.reshape(images, WROWS, 3 * C)
    low_masks = head_masks(BF16)
    eye = identity()
    def one_image(b, carry):
        rows, cols = sizes[0]
        for n in range(1, images):
            rows = jnp.where(b == n, sizes[n][0], rows)
            cols = jnp.where(b == n, sizes[n][1], cols)
        blocks = {}
        for w in range(NWIN):
            allowed = (row_limit[w] < rows) & (col_limit[w] < cols)
            blocks[w] = jnp.where(allowed, 0.0, MASKED).astype(F32)
        attend(b, blocks)
        return carry

    def attend(b, blocks):
        units = [(b, pair, g, blocks) for pair in range(NWIN // 2) for g in range(NGRP)]
        pipelined(units, raw_scores, softmax, apply)

    def raw_scores(b, pair, g, blocks):
        results = []
        for w in (2 * pair, 2 * pair + 1):
            at = slice(w * SLOT, (w + 1) * SLOT)
            query = qkv_ref[b, at, g * 128 : (g + 1) * 128]
            key = qkv_ref[b, at, C + g * 128 : C + (g + 1) * 128]
            results.append(dot(key, spread_heads(query, low_masks), NT))
        return results

    def softmax(b, pair, g, blocks, raw):
        probs = []
        for n, score in enumerate(raw):
            w = 2 * pair + n
            block = jnp.concatenate([blocks[w]] * 2, 1)
            score = score * SCALE + (bias[g] + block)
            top = jnp.max(score, 0, keepdims=True)
            expo = jnp.exp(score - top)
            prob = (expo * (1.0 / jnp.sum(expo, 0, keepdims=True))).astype(BF16)
            prob_ref[b, w, g] = prob
            probs.append(prob)
        return probs

    def apply(b, pair, g, blocks, probs):
        both = slice(pair * 2 * SLOT, (pair + 1) * 2 * SLOT)
        value = (b, both, slice(2 * C + g * 128, 2 * C + (g + 1) * 128))
        mixed_ref[b, g * 128 : (g + 1) * 128, both] = apply_pair(qkv_ref, value, eye, *probs).astype(BF16)

    each_image(images, one_image, unrolled)
    for b in range(images):
        attended_ref[b] = dot(perm_t[...], mixed_ref[b], NT).astype(BF16)
    attended = attended_ref[...].reshape(images * ROWS, C)
    middle = field + dot(attended, w_proj[...]) + small[4:5]
    return normed, middle


def forward_mlp(middle, w_up, w_down, small, up_bias, active_ref, slope_ref):
    hat, _ = norm_parts(middle)
    mlp_in = (hat * small[5:6] + small[6:7]).astype(BF16)
    branch = jnp.zeros(middle.shape, F32)
    width = CHUNK
    for part in range(HID // width):
        at = slice(part * width, (part + 1) * width)
        pre = dot(mlp_in, w_up[:, at]) + up_bias[:, at]
        half = 0.5 * (1.0 + lax.erf(pre * (0.5**0.5)))
        active = (pre * half).astype(BF16)
        slope = half + pre * (jnp.exp(-0.5 * pre * pre) * ((2.0 * np.pi) ** -0.5))
        active_ref[..., at] = active.reshape(active_ref.shape[:-1] + (width,))
        slope_ref[..., at] = slope.astype(BF16).reshape(slope_ref.shape[:-1] + (width,))
        branch = branch + dot(active, w_down[:, at], NT)
    return mlp_in, middle + branch + small[7:8]


def backward_mlp(
    grad, middle, slope_ref, w_up, w_down, small, low_ref, pre_ref, rows_ref, up_rows_ref, place
):
    low = grad.astype(BF16)
    low_ref[place, :] = low
    rows_ref[7:8, :] += col_sum(low.astype(F32))
    normed_grad = jnp.zeros(grad.shape, F32)
    width = CHUNK
    for part in range(HID // width):
        at = slice(part * width, (part + 1) * width)
        slope = slope_ref[..., at].reshape(-1, width).astype(F32)
        pre = (dot(low, w_down[:, at]) * slope).astype(BF16)
        pre_ref[place, at] = pre
        up_rows_ref[:, at] += col_sum(pre.astype(F32))
        normed_grad = normed_grad + dot(pre, w_up[:, at], NT)
    hat, rate = norm_parts(middle)
    rows_ref[5:6, :] += col_sum(normed_grad * hat)
    rows_ref[6:7, :] += col_sum(normed_grad)
    return norm_back(normed_grad, hat, rate, small[5:6]) + grad


def backward_attention(
    grad_mid, field, qkv_ref, prob_ref, w_qkv, w_proj, perm, perm_t, small,
    spread_ref, dq_ref, dkv_ref, attn_ref, joined_ref, rows_ref, qkv_rows_ref, bias_grad_ref, start,
    need_grad, unrolled,
):
    images = qkv_ref.shape[0]
    place = pl.ds(start, images * ROWS)
    attn = grad_mid.astype(BF16)
    attn_ref[place, :] = attn
    rows_ref[4:5, :] += col_sum(attn.astype(F32))
    joined = dot(attn, w_proj[...], NT).astype(BF16)
    for b in range(images):
        joined_ref[b] = dot(perm[...], joined[b * ROWS : (b + 1) * ROWS]).astype(BF16)
    low_masks = head_masks(BF16)
    eye = identity()

    def cut(n, g):
        return slice(n * C + g * 128, n * C + (g + 1) * 128)

    def prob_grads(b, pair, g):
        results = []
        for w in (2 * pair, 2 * pair + 1):
            at = slice(w * SLOT, (w + 1) * SLOT)
            out = spread_heads(joined_ref[b, at, cut(0, g)], low_masks)
            results.append(dot(qkv_ref[b, at, cut(2, g)], out, NT))
            dkv_ref[b, at, cut(1, g)] = dot(prob_ref[b, 2 * pair + len(results) - 1, g], out).astype(BF16)
        return results

    def score_grads(b, pair, g, grads):
        results = []
        for n, prob_grad in enumerate(grads):
            wide = prob_ref[b, 2 * pair + n, g].astype(F32)
            weighted = wide * prob_grad
            score = weighted - wide * jnp.sum(weighted, 0, keepdims=True)
            bias_grad_ref[g] += score
            results.append(score.astype(BF16))
        return results

    def products(b, pair, g, scores):
        both = slice(pair * 2 * SLOT, (pair + 1) * 2 * SLOT)
        for n, score in enumerate(scores):
            w = 2 * pair + n
            at = slice(w * SLOT, (w + 1) * SLOT)
            query = spread_heads(qkv_ref[b, at, cut(0, g)], low_masks)
            dkv_ref[b, at, cut(0, g)] = (dot(score, query) * SCALE).astype(BF16)
        dq_ref[b, cut(0, g), both] = (
            apply_pair(qkv_ref, (b, both, cut(1, g)), eye, *scores) * SCALE
        ).astype(BF16)

    def one_image(b, carry):
        units = [(b, pair, g) for pair in range(NWIN // 2) for g in range(NGRP)]
        pipelined(units, prob_grads, score_grads, products)
        return carry

    each_image(images, one_image, unrolled)
    for b in range(images):
        rows = pl.ds(pl.multiple_of(start + b * ROWS, 16), ROWS)
        spread_ref[rows, :C] = dot(perm_t[...], dq_ref[b], NT).astype(BF16)
        spread_ref[rows, C:] = dot(perm_t[...], dkv_ref[b]).astype(BF16)
    back = spread_ref[place, :]
    qkv_rows_ref[:, :C] += col_sum(back[:, :C].astype(F32))
    qkv_rows_ref[:, 2 * C :] += col_sum(back[:, 2 * C :].astype(F32))
    normed_grad = dot(back, w_qkv[...], NT)
    hat, rate = norm_parts(field)
    rows_ref[0:1, :] += col_sum(normed_grad * hat)
    rows_ref[1:2, :] += col_sum(normed_grad)
    if not need_grad:
        return None
    return norm_back(normed_grad, hat, rate, small[0:1]) + grad_mid


def image_place():
    return pl.ds(pl.multiple_of(pl.program_id(0) * GROUP * ROWS, 16), GROUP * ROWS)


def flat(ref):
    return ref[...].reshape(-1, ref.shape[-1])


def rows_in(k, name):
    if hasattr(k, name):
        return flat(getattr(k, name))
    rows = flat(getattr(k, name + "0"))
    number = 1
    while hasattr(k, f"{name}{number}"):
        rows = jnp.where(pl.program_id(0) == number, flat(getattr(k, f"{name}{number}")), rows)
        number += 1
    return rows


def put_rows(ref, value):
    ref[...] = value.reshape(ref.shape)


def is_first():
    return pl.program_id(0) == 0


def is_last():
    return pl.program_id(0) == pl.num_programs(0) - 1


def clear(*refs):
    @pl.when(is_first())
    def _():
        for ref in refs:
            ref[...] = jnp.zeros(ref.shape, ref.dtype)


class Names:
    def __init__(self, **refs):
        self.__dict__.update(refs)


def fetch_attention(k, plan):
    if not plan.sources:
        return

    @pl.when(is_first())
    def _():
        load_blocks(plan.pieces(k, "attn"), k.stage, plan.widths["attn"], k.load_sem.at[0], k.me)
        wait_all(k.stage, k.load_sem.at[0])
        join_attention(k.stage, k.w_qkv, k.w_proj)
        for n, (source, target) in enumerate(((k.w_qkv, k.qkv_out), (k.w_proj, k.proj_out))):
            pltpu.make_async_copy(source, target, k.out_sem.at[n]).start()


def fetch_mlp(k, plan):
    @pl.when(is_first())
    def _():
        load_blocks(plan.pieces(k, "down"), k.w_down, plan.widths["down"], k.load_sem.at[1], k.me)
        load_blocks(plan.pieces(k, "up"), k.w_up, plan.widths["up"], k.load_sem.at[2], k.me)
        wait_all(k.w_down, k.load_sem.at[1])
        wait_all(k.w_up, k.load_sem.at[2])


def group_images(k, group=0):
    images = k.rows.shape[1]
    first = (pl.program_id(0) + group) * GROUP
    return [((first + b) // images, (first + b) % images) for b in range(GROUP)]


def group_sizes(k, group=0):
    return [(k.rows[m, n], k.cols[m, n]) for m, n in group_images(k, group)]


def small_rows(k, plan):
    return k.vec[plan.layer * PER_LAYER : plan.layer * PER_LAYER + 8]


def joined_rows(k, start, end):
    return jnp.concatenate([k.vec[n : n + 1] for n in range(start, end)], 1)


def up_bias_row(k, plan):
    return joined_rows(k, plan.layer * PER_LAYER + 8, (plan.layer + 1) * PER_LAYER)


def attention_forward_kernel(k, plan):
    fetch_attention(k, plan)
    small = small_rows(k, plan)
    qkv_bias = jnp.concatenate([small[2:3], jnp.zeros((1, C), F32), small[3:4]], 1)
    normed, middle = forward_attention(
        flat(k.field).astype(F32), group_sizes(k, plan.group), k.w_qkv, k.w_proj, k.perm, k.perm_t,
        k.row_limit, k.col_limit, k.bias, small, qkv_bias, k.qkv, k.prob, k.windowed,
        k.mixed, k.attended, plan.layer > 0,
    )
    put_rows(k.normed, normed)
    put_rows(k.middle, middle)
    if not plan.sources:
        return

    @pl.when(is_last())
    def _():
        wait_all(k.w_qkv, k.out_sem.at[0])
        wait_all(k.w_proj, k.out_sem.at[1])


def first_mlp_kernel(k, plan):
    fetch_mlp(k, plan)

    @pl.when(is_first())
    def _():
        for n, (source, target) in enumerate(((k.w_down, k.down_out), (k.w_up, k.up_out))):
            pltpu.make_async_copy(source, target, k.out_sem.at[n]).start()

    mlp_in, result = forward_mlp(
        rows_in(k, "middle"), k.w_up, k.w_down, small_rows(k, plan), up_bias_row(k, plan), k.active,
        k.slope,
    )
    put_rows(k.mlp_in, mlp_in)
    put_rows(k.result, result)

    @pl.when(is_last())
    def _():
        wait_all(k.w_down, k.out_sem.at[0])
        wait_all(k.w_up, k.out_sem.at[1])


def store_mlp_grads(k, plan):
    for at in range(0, HID, CHUNK):
        k.up_grad[:, at : at + CHUNK] = dot(k.mlp_all[...], k.pre_all[:, at : at + CHUNK], TN).astype(BF16)
    store_blocks(k.up_grad, plan.outs(k, "up"), plan.widths["up"], k.sem_x, k.me)
    for at in range(0, HID, CHUNK):
        k.down_grad[:, at : at + CHUNK] = dot(k.low_all[...], k.active_all[:, at : at + CHUNK], TN).astype(BF16)
    store_blocks(k.down_grad, plan.outs(k, "down"), plan.widths["down"], k.sem_y, k.me)


def wait_mlp_grads(k, plan):
    wait_blocks(plan.outs(k, "up"), k.sem_x)
    wait_blocks(plan.outs(k, "down"), k.sem_y)


def head_pass(k, plan, result, sizes, total_images):
    first = pl.program_id(0) * GROUP
    base = plan.layers * PER_LAYER
    gain = k.vec[base : base + 1]
    hat, rate = norm_parts(result)
    final = hat * gain + k.vec[base + 1 : base + 2]
    places = group_images(k)
    owners, _, width = k.w_head.shape
    row = lax.broadcasted_iota(jnp.int32, (16, 1), 0)
    pooled = jnp.zeros((16, C), F32)
    own = other = jnp.full((16, 1), -1, jnp.int32)
    mixing = jnp.zeros((16, 1), F32)
    shares = []
    for b, (rows, cols) in enumerate(sizes):
        inside = ((k.cell_row[...] < rows) & (k.cell_col[...] < cols)).astype(F32)
        count = (rows * cols).astype(F32)
        mean = col_sum(final[b * ROWS : (b + 1) * ROWS] * inside) / count
        shares.append(inside / count)
        pooled = jnp.where(row == b, mean, pooled)
        m, n = places[b]
        mine = (k.me[0] * owners + k.me[1]) * k.rows.shape[1] + n
        own = jnp.where(row == b, k.labels[m, mine], own)
        other = jnp.where(row == b, k.labels[m, k.partner[m, n]], other)
        mixing = jnp.where(row == b, k.mix[m, n].astype(F32) / 16.0, mixing)
    pooled = pooled.astype(BF16)
    classes = owners * width
    real = CLASSES // owners
    bias = joined_rows(k, base + 2, base + 2 - (-CLASSES // C))
    empty = jnp.full((1, width - real), MASKED, F32)
    bias = jnp.concatenate(
        [part for n in range(owners) for part in (bias[:, n * real : (n + 1) * real], empty)], 1
    )
    logits = jnp.concatenate([dot(pooled, k.w_head[n]) for n in range(owners)], 1)
    logits = logits + bias
    top = jnp.max(logits, -1, keepdims=True)
    expo = jnp.exp(logits - top)
    log_probs = logits - top - jnp.log(jnp.sum(expo, -1, keepdims=True))
    lane = lax.broadcasted_iota(jnp.int32, (16, classes), 1)
    label = lane // width * real + lane % width
    label = jnp.where(lane % width < real, label, -2)
    target = jnp.where(label == own, mixing, 0.0)
    target = target + jnp.where(label == other, 1.0 - mixing, 0.0)
    loss = jnp.where(target > 0.0, target * log_probs, 0.0)
    loss = jnp.sum(jnp.sum(loss, -1, keepdims=True), 0, keepdims=True)
    k.loss[...] -= jnp.broadcast_to(loss, k.loss.shape)
    logit_grad = jnp.where(row < GROUP, (jnp.exp(log_probs) - target) / total_images, 0.0)
    logit_low = logit_grad.astype(BF16)
    wide = logit_low.astype(F32)
    k.head_rows[...] += col_sum(wide)
    for b in range(GROUP):
        k.pooled_all[pl.ds(first + b, 1), :] = pooled[b : b + 1].astype(F32)
        k.logit_all[pl.ds(first + b, 1), :] = wide[b : b + 1]
    pooled_grad = jnp.zeros((16, C), F32)
    for n in range(owners):
        pooled_grad += dot(logit_low[:, n * width : (n + 1) * width], k.w_head[n], NT)
    final_grad = jnp.concatenate(
        [pooled_grad[b : b + 1] * share for b, share in enumerate(shares)], 0
    )
    k.final_rows[0:1, :] += col_sum(final_grad * hat)
    k.final_rows[1:2, :] += col_sum(final_grad)
    return norm_back(final_grad, hat, rate, gain)


def last_mlp_kernel(k, plan, total_images):
    place = image_place()

    @pl.when(is_first())
    def _():
        load_blocks(plan.pieces(k, "head"), k.w_head, plan.widths["head"], k.load_sem.at[3], k.me)

    fetch_mlp(k, plan)

    @pl.when(is_first())
    def _():
        wait_all(k.w_head, k.load_sem.at[3])

    clear(k.row_sums, k.up_rows, k.final_rows, k.head_rows, k.loss, k.pooled_all, k.logit_all)
    middle = flat(k.middle)
    mlp_in, result = forward_mlp(
        middle, k.w_up, k.w_down, small_rows(k, plan), up_bias_row(k, plan), k.active_all.at[place], k.slope
    )
    k.mlp_all[place, :] = mlp_in
    grad = head_pass(k, plan, result, group_sizes(k), total_images)
    put_rows(k.grad_mid, backward_mlp(
        grad, flat(k.middle), k.slope, k.w_up, k.w_down, small_rows(k, plan), k.low_all, k.pre_all,
        k.row_sums, k.up_rows, place,
    ))

    @pl.when(is_last())
    def _():
        store_mlp_grads(k, plan)
        total = dot(k.pooled_all[...].astype(BF16), k.logit_all[...].astype(BF16), TN).astype(BF16)
        owners, _, width = k.head_grad.shape
        for n in range(owners):
            k.head_grad[n] = total[:, n * width : (n + 1) * width]
        store_blocks(k.head_grad, plan.outs(k, "head"), plan.widths["head"], k.sem_x, k.me)
        wait_mlp_grads(k, plan)


def backward_mlp_kernel(k, plan):
    clear(k.row_sums, k.up_rows)
    place = image_place()
    k.mlp_all[place, :] = flat(k.mlp_in)
    k.active_all[place, :] = flat(k.active)
    put_rows(k.grad_mid, backward_mlp(
        flat(k.grad), rows_in(k, "middle"), k.slope, k.w_up, k.w_down, small_rows(k, plan), k.low_all, k.pre_all,
        k.row_sums, k.up_rows, place,
    ))

    @pl.when(is_last())
    def _():
        store_mlp_grads(k, plan)
        wait_mlp_grads(k, plan)


def backward_attention_kernel(k, plan, earlier, need_grad):
    sums = ("row_sums", "qkv_rows", "bias_grad")
    if earlier:
        @pl.when(is_first())
        def _():
            for name in sums:
                getattr(k, name)[...] = getattr(k, name + "_in")[...]
    else:
        clear(*[getattr(k, name) for name in sums])
    start = pl.multiple_of(earlier * ROWS + pl.program_id(0) * GROUP * ROWS, 16)
    grad = backward_attention(
        flat(k.grad_mid), flat(k.field).astype(F32), k.qkv, k.prob, k.w_qkv, k.w_proj, k.perm,
        k.perm_t, small_rows(k, plan), k.spread_all, k.dq, k.dkv, k.attn_all, k.joined, k.row_sums,
        k.qkv_rows, k.bias_grad, start, need_grad, True,
    )
    if need_grad:
        put_rows(k.grad, grad)
    if "attn" not in plan.targets:
        return
    place = pl.ds(start, GROUP * ROWS)
    k.normed_all[place, :] = flat(k.normed)
    k.attended_all[place, :] = flat(k.attended)

    @pl.when(is_last())
    def _():
        if earlier:
            before = slice(0, earlier * ROWS)
            k.normed_all[before, :] = flat(k.normed_in)
            k.attended_all[before, :] = flat(k.attended_in)
            k.spread_all[before, :] = k.spread_in[...]
            k.attn_all[before, :] = k.attn_in[...]
        owners, _, _ = k.attn_grad.shape
        wide, narrow = 3 * C // owners, C // owners
        if plan.collect is not None:
            layers, head_real, loss_at, near = plan.collect
            own = [k.row_sums, k.qkv_rows, k.mlp_rows0, k.up_rows0, k.bias_grad]
            collect_rows(
                layers, head_real, loss_at,
                own + [k.row_sums1, k.qkv_rows1, k.mlp_rows1, k.up_rows1, k.bias_grad1]
                + [k.final_rows, k.head_rows, k.loss],
                k.small_rows, k.spread_table,
            )
            pair_rows(k.small_rows, owners, near, k.me, k.pairs)
            for flip, (ref, *_) in enumerate(plan.outs(k, "attn")[2:]):
                width = ref.shape[2]
                pltpu.make_async_copy(
                    k.pairs.at[flip], ref.at[:, :, width - 128 : width], k.sem_a.at[2 + flip]
                ).start()
        total = dot(k.normed_all[...], k.spread_all[...], TN).astype(BF16)
        for n in range(owners):
            k.attn_grad[n, :, :wide] = total[:, n * wide : (n + 1) * wide]
        total = dot(k.attended_all[...], k.attn_all[...], TN).astype(BF16)
        for n in range(owners):
            k.attn_grad[n, :, wide:] = total[:, n * narrow : (n + 1) * narrow]
        store_blocks(k.attn_grad, plan.outs(k, "attn"), plan.widths["attn"], k.sem_a, k.me)
        wait_blocks(plan.outs(k, "attn"), k.sem_a)


class Plan:
    def __init__(self, widths, layer, layers):
        self.widths, self.layer, self.layers = widths, layer, layers
        self.sources = {}
        self.targets = {}
        self.collect = None
        self.group = 0

    def pieces(self, k, name):
        return [(getattr(k, ref), owners, cut) for ref, owners, cut in self.sources[name]]

    def outs(self, k, name):
        return [(getattr(k, ref), *rest) for ref, *rest in self.targets[name]]


def whole(shape):
    return pl.BlockSpec(shape, lambda i: (0,) * len(shape))


def per_image(*shape, first=0):
    return pl.BlockSpec((GROUP,) + shape, lambda i: (i + first,) + (0,) * len(shape))


SCALARS = pl.BlockSpec(memory_space=pltpu.SMEM)
FAR = pl.BlockSpec(memory_space=pl.ANY)
NEAR = pl.BlockSpec(memory_space=pltpu.VMEM)


def call(body, name, groups, ins, outs, scratch, flops):
    def kernel(*refs):
        body(Names(**dict(zip(list(ins) + list(outs) + list(scratch), refs))))

    moved = sum(a.size * a.dtype.itemsize for _, a in ins.values())
    results = pl.pallas_call(
        kernel,
        grid=(groups,),
        in_specs=[spec for spec, _ in ins.values()],
        out_specs=[spec for spec, _, _ in outs.values()],
        out_shape=[jax.ShapeDtypeStruct(dims, dtype) for _, dims, dtype in outs.values()],
        scratch_shapes=list(scratch.values()),
        compiler_params=pltpu.CompilerParams(
            dimension_semantics=("arbitrary",), vmem_limit_bytes=VMEM_LIMIT
        ),
        cost_estimate=pl.CostEstimate(flops=int(flops), bytes_accessed=int(moved), transcendentals=0),
        name=name,
    )(*[array for _, array in ins.values()])
    return dict(zip(outs, results))


def exchange(array, step):
    axis, bit = step
    size = lax.axis_size(axis)
    return lax.ppermute(array, axis, [(i, i ^ (1 << bit)) for i in range(size)])


class Held:
    def __init__(self, array, dims=()):
        self.array, self.dims = array, list(dims)


def stack_blocks(parts, me, name, cuts=None):
    cuts = cuts or [None] * len(parts)
    args, outs, results = [], [], []
    for (held, received, step), cut in zip(parts, cuts):
        count, rows, columns = held.array.shape
        args += [held.array, received]
        axis, bit = step
        place = sum(d[0] == "win" and d[1] < bit for d in held.dims) if axis == "win" else len(held.dims)
        at = len(held.dims) - place
        dims = held.dims[:at] + [step] + held.dims[at:]
        bounds = [0, *(cut or ()), columns]
        pieces = list(zip(bounds, bounds[1:]))
        outs += [((2 * count, rows, end - start), BF16) for start, end in pieces]
        results.append((place, axis, bit, pieces, dims))

    def kernel(me_ref, *refs):
        ins, targets = list(refs[: len(args)]), list(refs[len(args) :])
        for place, axis, bit, pieces, _ in results:
            held, received = ins.pop(0), ins.pop(0)
            mine = (me_ref[0] >> bit) & 1 if axis == "win" else 0
            for start, end in pieces:
                out = targets.pop(0)
                for n in range(held.shape[0]):
                    base = (n >> place << (place + 1)) + (n & ((1 << place) - 1))
                    out[base + (mine << place)] = held[n, :, start:end]
                    out[base + ((1 - mine) << place)] = received[n, :, start:end]

    arrays = list(small_call(kernel, name, [me] + args, outs, scalars=1))
    return [
        [Held(arrays.pop(0), dims) for _ in pieces] for _, _, _, pieces, dims in results
    ]


def tie(*values):
    return lax.optimization_barrier(values)


def small_call(kernel, name, args, outs, stream=False, scratch=(), scalars=0, limit=24):
    def spec(dims):
        return whole(dims) if stream else pl.BlockSpec(memory_space=pltpu.VMEM)

    return pl.pallas_call(
        kernel,
        grid=(1,) if stream else (),
        out_shape=[jax.ShapeDtypeStruct(dims, dtype) for dims, dtype in outs],
        in_specs=[SCALARS] * scalars + [spec(a.shape) for a in args[scalars:]],
        out_specs=[spec(dims) for dims, _ in outs],
        scratch_shapes=list(scratch),
        compiler_params=pltpu.CompilerParams(
            vmem_limit_bytes=limit * 1024 * 1024
        ),
        cost_estimate=pl.CostEstimate(flops=1, bytes_accessed=1, transcendentals=0),
        name=name,
    )(*args)


class Chain:
    def __init__(self, keep, send, dims, steps, pair_at=None):
        self.keep, self.send, self.dims, self.steps = keep, send, list(dims), list(steps)
        self.pair_at = pair_at

    def start(self):
        self.received = exchange(self.send, self.steps.pop(0))


def add_blocks(keep, received, pair_at):
    total = keep.astype(F32) + received.astype(F32)
    if pair_at is None:
        return total.astype(BF16)
    pair = total[:16, pair_at:] + total[16:32, pair_at:]
    high = pair.astype(BF16)
    tail = jnp.zeros((total.shape[0] - 32, pair.shape[1]), BF16)
    parts = [jnp.concatenate([high, (pair - high.astype(F32)).astype(BF16), tail], 0)]
    if pair_at:
        parts = [total[:, :pair_at].astype(BF16)] + parts
    return jnp.concatenate(parts, 1)


def combine(groups, me, name):
    args, outs = [], []
    for group in groups:
        for chain in group:
            args += [chain.keep, chain.received]
        count, rows, _ = group[0].keep.shape
        width = sum(chain.keep.shape[2] for chain in group)
        outs += [((count // 2, rows, width), BF16)] * 2

    def kernel(me_ref, *refs):
        ins, results = list(refs[: len(args)]), list(refs[len(args) :])
        for group in groups:
            keep_out, send_out = results.pop(0), results.pop(0)
            start = 0
            for chain in group:
                keep, received = ins.pop(0), ins.pop(0)
                width = keep.shape[2]
                axis, bit = chain.steps[0]
                place = len(chain.dims) - 1 - chain.dims.index((axis, bit))
                mine = (me_ref[0] >> bit) & 1 if axis == "win" else 0
                for n in range(keep_out.shape[0]):
                    base = (n >> place << (place + 1)) + (n & ((1 << place) - 1))
                    for out, at in (
                        (keep_out, base + (mine << place)), (send_out, base + ((1 - mine) << place))
                    ):
                        out[n, :, start : start + width] = add_blocks(
                            keep[at], received[at], chain.pair_at
                        )
                start += width

    results = small_call(kernel, name, [me] + args, outs, scalars=1)
    chains = []
    for n, group in enumerate(groups):
        step = group[0].steps[0]
        at, pair_at = 0, None
        for chain in group:
            if chain.pair_at is not None:
                pair_at = at + chain.pair_at
            at += chain.keep.shape[2]
        dims = [d for d in group[0].dims if d != step]
        chains.append(Chain(results[2 * n], results[2 * n + 1], dims, group[0].steps, pair_at))
    return chains


def finish(chain, name):
    _, rows, width = chain.keep.shape

    def kernel(keep, received, own, square):
        total = keep[0].astype(F32) + received[0].astype(F32)
        own[...] = total
        square[...] = jnp.broadcast_to(jnp.sum(total * total), (1, 128))

    return small_call(
        kernel, name, [chain.keep, chain.received], [((rows, width), F32), ((1, 128), F32)]
    )


def finish_pair(chain, squares, devices, share, name):
    _, rows, width = chain.keep.shape
    at = chain.pair_at

    def kernel(keep, received, *refs):
        total = keep[0].astype(F32) + received[0].astype(F32)
        own, message = refs[-2:]
        own[...] = total[:, :at]
        pair = total[:16, at:] + total[16:32, at:]
        square = jnp.sum(total[:, :at] * total[:, :at])
        square = jnp.broadcast_to(square, (1, 128))
        for ref in refs[:-2]:
            square = square + ref[...]
        row = [pair[n : n + 1] for n in range(share // 128)] + [square]
        message[...] = jnp.broadcast_to(jnp.concatenate(row, 1), message.shape)

    return small_call(
        kernel, name, [chain.keep, chain.received] + squares,
        [((rows, at), F32), ((devices, share + 128), F32)],
    )


def adam_step(weight, grad, first, second, rate):
    new_first = 0.5 * first + 0.5 * grad
    new_second = 0.5 * second + 0.5 * grad * grad
    fix = 1.0 - 0.5**STEP
    update = new_first / fix / (jnp.sqrt(new_second / fix) + ADAM_EPS)
    return (new_first, new_second, weight - rate * (update + DECAY_RATE * weight))


def update_kernel(starts, widths, layout, *refs):
    own, message, rest = refs[:3], refs[3], list(refs[4:])
    groups = [rest[3 * n : 3 * n + 3] for n in range(7)]
    loss_ref, norm_ref = rest[21], rest[22]
    outs = [rest[23 + 3 * n : 26 + 3 * n] for n in range(7)]
    vector_rows, table_rows, offsets, square_at, loss_at = layout
    vector_grad = message[:vector_rows, :C]
    table_grad = message[:table_rows, C : C + offsets]
    total = (
        jnp.sum(message[:, square_at : square_at + 1])
        + jnp.sum(vector_grad * vector_grad)
        + jnp.sum(table_grad * table_grad)
    )
    norm = jnp.sqrt(jnp.broadcast_to(total, (1, 1)))
    factor = CLIP_NORM / jnp.maximum(norm, CLIP_NORM)
    norm_ref[...] = norm
    loss_ref[...] = message[0:1, loss_at : loss_at + 1]

    def put(number, layer, grad, rate):
        weight, first, second = groups[number]
        index = (Ellipsis,) if layer is None else (layer, Ellipsis)
        if number == 6:
            index = (slice(None), layer, slice(None))
        results = adam_step(weight[index], factor * grad, first[index], second[index], rate)
        for ref, value in zip(outs[number], results):
            ref[index] = value

    layers = len(starts)
    for l in range(layers):
        qkv_width = outs[0][0].shape[2]
        part, at = starts[l]["attn"]
        put(0, l, own[part][:, at : at + qkv_width], LEARN_RATE)
        put(1, l, own[part][:, at + qkv_width : at + widths["attn"]], LEARN_RATE)
        part, at = starts[l]["up"]
        put(2, l, own[part][:, at : at + widths["up"]], LEARN_RATE)
        part, at = starts[l]["down"]
        put(3, l, own[part][:, at : at + widths["down"]], LEARN_RATE)
        heads = table_rows // layers
        put(6, l, table_grad[l * heads : (l + 1) * heads], SMALL_RATE)
    part, at = starts[-1]["head"]
    put(4, None, own[part][:, at : at + outs[4][0].shape[1]], LEARN_RATE)
    put(5, None, vector_grad, SMALL_RATE)


def collect_rows(layers, head_real, loss_at, ins, out, spread):
    out[...] = jnp.zeros(out.shape, F32)
    row_of_slot = lax.broadcasted_iota(jnp.int32, (SLOT, 128), 0)
    lane = lax.broadcasted_iota(jnp.int32, (SLOT, 128), 1)
    target = row_of_slot // WSIDE * (2 * WSIDE - 1) + row_of_slot % WSIDE
    spreader = ((lane == target) & (row_of_slot < AREA)).astype(F32).astype(BF16)
    row = 0
    for l in range(layers):
        attn_rows, qkv_rows, mlp_rows, up_rows, bias_grad = ins[5 * l : 5 * l + 5]
        parts = [
            attn_rows[0:2], qkv_rows[:, :C], qkv_rows[:, 2 * C :], attn_rows[4:5], mlp_rows[5:8],
        ] + [up_rows[:, n * C : (n + 1) * C] for n in range(HID // C)]
        for part in parts:
            out[row : row + part.shape[0], :C] = part
            row += part.shape[0]
        for head in range(HEADS):
            g, h = divmod(head, PACK)
            left = bias_grad[g, :, h * SLOT : (h + 1) * SLOT]
            total = jnp.zeros((SLOT, 128), F32)
            for _ in range(3):
                low = left.astype(BF16)
                total = total + dot(low, spreader)
                left = left - low.astype(F32)
            spread[head * SLOT : (head + 1) * SLOT, :] = total
        table = jnp.zeros((HEADS, 256), F32)
        span = 2 * WSIDE - 1
        for j in range(AREA):
            wide = jnp.concatenate(
                [spread[pl.ds(j, HEADS, stride=SLOT), :], jnp.zeros((HEADS, 128), F32)], 1
            )
            shift = (WSIDE - 1 - j // WSIDE) * span + WSIDE - 1 - j % WSIDE
            table = table + (pltpu.roll(wide, shift, 1) if shift else wide)
        width = out.shape[1] - C
        out[l * HEADS : (l + 1) * HEADS, C:] = table[:, :width]
    final_rows, head_rows, loss = ins[5 * layers :]
    out[row : row + 2, :C] = final_rows[...]
    row += 2
    cuts = CLASSES // head_real
    width = head_rows.shape[1] // cuts
    classes = jnp.concatenate(
        [head_rows[:, n * width : n * width + head_real] for n in range(cuts)]
        + [jnp.zeros((1, -CLASSES % C), F32)], 1
    )
    for n in range(classes.shape[1] // C):
        out[row + n : row + n + 1, :C] = classes[:, n * C : (n + 1) * C]
    out[0:1, loss_at : loss_at + 1] = loss[:, 0:1]


def pair_rows(rows, ch_count, owners, me_ref, pairs):
    count = rows.shape[1] // 128
    wins = rows.shape[0] // ch_count
    high_rows = pairs.shape[2] // wins
    for flip in range(2):
        for n, owner in enumerate(owners):
            for win in range(wins):
                values = rows[pl.ds(win * ch_count + (me_ref[1] ^ (owner ^ flip)), 1), :]
                values = jnp.concatenate(
                    [values[:, m * 128 : (m + 1) * 128] for m in range(count)]
                    + [jnp.zeros((16 - count, 128), F32)], 0
                )
                high = values.astype(BF16)
                at = win * high_rows
                pairs[flip, n, at : at + 16] = high
                pairs[flip, n, at + 16 : at + 32] = (values - high.astype(F32)).astype(BF16)
                pairs[flip, n, at + 32 : at + high_rows] = jnp.zeros((high_rows - 32, 128), BF16)


def pack_kernel(head_width, qkv, proj, down, up, head, attn0, mlp0, all1):
    attn0[...] = jnp.concatenate([qkv[0], proj[0]], 1).astype(BF16)
    mlp0[...] = jnp.concatenate([down[0], up[0]], 1).astype(BF16)
    parts = [qkv[1], proj[1], down[1], up[1], head[...]]
    pad = head_width - head.shape[1]
    if pad:
        parts.append(jnp.zeros((head.shape[0], pad), F32))
    all1[...] = jnp.concatenate(parts, 1).astype(BF16)


def per_device(
    tokens, valid_rows, valid_cols, partner, mix_level, labels,
    w_qkv, m_qkv, v_qkv, w_proj, m_proj, v_proj, w_fc1, m_fc1, v_fc1, w_fc2, m_fc2, v_fc2,
    w_head, m_head, v_head, vectors, m_vec, v_vec, rel_table, m_rel, v_rel,
):
    micro, images, cells, chans = tokens.shape
    layers = rel_table.shape[0]
    per_layer = 8 + HID // C
    base = layers * per_layer
    head_rows = vectors.shape[0] - base - 2
    all_images = labels.shape[1]
    total_images = micro * all_images
    local = micro * images
    groups = local // GROUP
    sizes = {axis: lax.axis_size(axis) for axis in ("win", "ch")}
    win_count, ch_count = sizes["win"], sizes["ch"]
    device_count = win_count * ch_count
    win_index, ch_index = lax.axis_index("win"), lax.axis_index("ch")
    me = jnp.stack([win_index, ch_index]).astype(jnp.int32)
    block_rows = C // win_count
    widths = {"attn": 4 * C // ch_count, "down": HID // ch_count, "up": HID // ch_count}
    head_real = CLASSES // ch_count
    widths["head"] = -(-head_real // 128) * 128
    head_classes = widths["head"] * ch_count
    direct = block_rows % 16 == 0 and block_rows >= 32 and all(w % 128 == 0 for w in widths.values())

    core = ("ch", 0)
    ch_high = [("ch", b) for b in range(1, ch_count.bit_length() - 1)]
    win_low = [("win", 0)]
    win_high = [("win", b) for b in range(1, win_count.bit_length() - 1)]

    def low(v):
        return v.astype(BF16)

    packed = small_call(
        functools.partial(pack_kernel, widths["head"]), "pack",
        [w_qkv, w_proj, w_fc2.transpose(0, 2, 1), w_fc1, w_head],
        [((block_rows, sum(widths[n] for n in names)), BF16) for names in (
            ("attn",), ("down", "up"), ("attn", "down", "up", "head"))],
        stream=True,
        limit=56,
    )
    names = [["attn", "down", "up"], ["attn", "down", "up", "head"]]
    onehot = jnp.asarray(relative_onehot(), BF16)
    offsets = rel_table.shape[1]
    table_width = -(-(offsets + 1) // 128) * 128
    share = C + table_width
    tables = [window_tables(l % 2 == 1) for l in range(layers)]
    perms = [jnp.asarray(t[0], BF16) for t in tables]
    perms_t = [jnp.asarray(t[0].T, BF16) for t in tables]
    row_limits = [jnp.asarray(t[1]) for t in tables]
    col_limits = [jnp.asarray(t[2]) for t in tables]

    def bias_of(table):
        table = table.transpose(0, 2, 1).reshape(layers * HEADS, offsets)
        table_parts = []
        for _ in range(3):
            table_parts.append(low(table))
            table = table - table_parts[-1].astype(F32)
        bias = dot(jnp.concatenate(table_parts, 0), onehot).reshape(3, layers, HEADS, SLOT * SLOT)
        bias = (bias[0] + bias[1]) + bias[2]
        return (
            bias.reshape(layers, NGRP, PACK, SLOT, SLOT)
            .transpose(0, 1, 3, 2, 4)
            .reshape(layers, NGRP, SLOT, LANES)
        )

    padded = jnp.pad(tokens.reshape(local, cells, chans), ((0, 0), (0, ROWS - cells), (0, 0)))

    def stage(number, *moves, cuts=None, more=()):
        received = [exchange(part.array, step) for part, step in moves]
        tied = tie(*received, *more)
        received, more = tied[: len(moves)], tied[len(moves) :]
        stacked = stack_blocks(
            [(part, got, step) for (part, step), got in zip(moves, received)],
            me, f"stack{number}", cuts,
        )
        return (stacked, *more)

    def wait_for(value, *parts):
        value, *arrays = tie(value, *[part.array for part in parts])
        for part, array in zip(parts, arrays):
            part.array = array
        return value

    far = [Held(block[None]) for block in packed]
    edges = [
        [0, widths["attn"] * 2 // 3, widths["attn"], widths["attn"] + widths["down"],
         widths["attn"] + widths["down"] + widths["up"]],
        [0, widths["attn"], widths["attn"] + widths["down"] + widths["up"] * 2 // 3,
         sum(widths[name] for name in ("attn", "down", "up", "head"))],
    ]
    staged = win_count == 8 and ch_count == 4
    if staged:
        zh, zl, y, x = ("win", 2), ("win", 1), ("win", 0), ("ch", 1)
        ((attn,),), mlp, padded = stage(0, (far[0], zh), more=(far[1].array, padded))
        (attn, (mlp,)), all1, bias = stage(
            1, (attn, zl), (Held(mlp), zh), cuts=[edges[0][1:2], None],
            more=(packed[2], bias_of(rel_table)),
        )
        floating = exchange(all1[None], zh)
        ((one,), (two,), mlp), = stage(
            2, (attn[0], y), (attn[1], x), (mlp, zl), cuts=[None, None, [widths["down"]]]
        )
        (((all1,),),) = [stack_blocks([(Held(all1[None]), floating, zh)], me, "stack10")]
        mlp[0].array, mlp[1].array, all1.array = tie(mlp[0].array, mlp[1].array, all1.array)
        near = [(one, x), (two, y), (mlp[0], x), (mlp[1], y)]
        received = [exchange(part.array, step) for part, step in near]
        floating = exchange(all1.array, zl)
        *received, floating = tie(*received, floating)
        ((one,), (two,), (down,), (up,)) = stack_blocks(
            [(part, got, step) for (part, step), got in zip(near, received)], me, "stack3"
        )
        held = [[one, two]]
        *got, floating = tie(*[exchange(part.array, core) for part in held[0]], floating)
        other = [got]
        (parts1,) = stack_blocks([(all1, floating, zl)], me, "stack11", [edges[1][1:-1]])
        padded = wait_for(padded, *parts1)
    else:
        bias = bias_of(rel_table)
        bits = win_high[::-1] + win_low + ch_high[::-1]
        held, other = [[], []], []
        for number, part in enumerate(far):
            for n, step in enumerate(bits):
                ((part,),), = stage(10 * number + n, (part, step))
            layer = number // 2
            base = 0 if number != 1 else widths["attn"]
            for start, end in zip(edges[layer], edges[layer][1:]):
                if start >= base and end - base <= part.array.shape[-1]:
                    held[layer].append(Held(part.array[..., start - base : end - base], part.dims))
        other.append([exchange(part.array, core) for part in held[0]])

    def weight_inputs(layer, wanted):
        plan = Plan(widths, layer, layers)
        ins = {}
        starts, at = {}, 0
        for name in names[layer]:
            starts[name] = at
            at += widths[name]
        bounds = list(zip(edges[layer], edges[layer][1:]))
        blocks = []
        for group, part in enumerate(held[layer]):
            if group >= len(other[layer]):
                break
            owners = relative_owners([d for d in part.dims if d[0] == "ch"])
            for number, array in enumerate((part.array, other[layer][group])):
                flat_array = array.reshape(-1, C, array.shape[-1])
                blocks.append((group, [owner ^ number for owner in owners], flat_array))
        for name in wanted:
            plan.sources[name] = []
            columns = []
            for number, (group, owners, array) in enumerate(blocks):
                begin = max(starts[name], bounds[group][0])
                end = min(starts[name] + widths[name], bounds[group][1])
                if begin >= end:
                    continue
                cut = (begin - bounds[group][0], end - begin, begin - starts[name])
                if direct:
                    ref = f"blocks{number}"
                    ins[ref] = (FAR, array)
                    plan.sources[name].append((ref, owners, cut))
                elif number % 2 == 0:
                    table = np.argsort(np.asarray(owners + blocks[number + 1][1]))
                    both = jnp.concatenate([array, blocks[number + 1][2]])
                    index = jnp.asarray(table)[jnp.arange(ch_count) ^ ch_index]
                    columns.append(jnp.take(both, index, axis=0)[..., cut[0] : cut[0] + cut[1]])
            if not direct:
                full = jnp.concatenate(columns, -1)
                if name in ("up", "down"):
                    full = full.transpose(1, 0, 2).reshape(C, -1)
                ins[f"staged_{name}"] = (FAR, full)
                plan.sources[name] = [(f"staged_{name}", None, None)]
        ins["me"] = (SCALARS, me)
        return ins, plan

    orders = {
        "x": ch_high + win_low + win_high, "a": ch_high + win_low + win_high,
        "y": win_low + ch_high + win_high, "b": win_low + ch_high + win_high,
    }
    block_dims = ch_high + [("win", b) for b in reversed(range(win_count.bit_length() - 1))]
    owners = relative_owners(ch_high)
    regular = direct and len(ch_high) == 1

    def grad_outputs(plan, **members):
        outs = {}
        for group, wanted in members.items():
            if not direct:
                for name in wanted:
                    plan.targets[name] = [(f"full_{name}", None, 0, 0, widths[name])]
                    dims = (C, HID) if name in ("up", "down") else (ch_count, C, widths[name])
                    outs[f"full_{name}"] = (FAR, dims, BF16)
                continue
            starts = np.cumsum([0] + [widths[name] for name in wanted])
            refs = [
                (f"keep_{group}", owners), (f"send_{group}", [owner ^ 1 for owner in owners])
            ]
            for ref, _ in refs:
                outs[ref] = (FAR, (len(owners), C, int(starts[-1])), BF16)
            for name, start in zip(wanted, starts):
                plan.targets[name] = [(ref, at, int(start), 0, widths[name]) for ref, at in refs]
        return outs

    def cut_attention_outputs(plan):
        cut = widths["attn"] * 2 // 3
        outs, plan.targets["attn"] = {}, []
        for group, start, size, extra in (("a", 0, cut, 0), ("b", cut, widths["attn"] - cut, 128)):
            for kind, flip in (("keep", 0), ("send", 1)):
                ref = f"{kind}_{group}"
                outs[ref] = (NEAR, (len(owners), C, size + extra), BF16)
                plan.targets["attn"].append(
                    (ref, [owner ^ flip for owner in owners], 0, start, size)
                )
        return outs

    def chain_of(results, group, *members, pair_at=None):
        if direct:
            keep, send = results[f"keep_{group}"], results[f"send_{group}"]
        else:
            full = []
            for name in members:
                part = results[f"full_{name}"]
                if name in ("up", "down"):
                    part = part.reshape(C, ch_count, -1).transpose(1, 0, 2)
                full.append(part)
            full = jnp.concatenate(full, -1)
            keep, send = [
                jnp.take(full, np.asarray(owners) ^ flip ^ ch_index, axis=0) for flip in (0, 1)
            ]
        dims = (-1, block_rows, keep.shape[-1])
        return Chain(
            keep.reshape(dims), send.reshape(dims), block_dims, [core] + orders[group], pair_at
        )

    def start(*chains):
        for chain in chains:
            chain.start()

    def meet(value, *chains):
        value, *got = tie(value, *[chain.received for chain in chains])
        for chain, array in zip(chains, got):
            chain.received = array
        return value

    def after(value, *chains):
        held_back = [array for chain in chains for array in (chain.keep, chain.send)]
        value, *held_back = tie(value, *held_back)
        for n, chain in enumerate(chains):
            chain.keep, chain.send = held_back[2 * n], held_back[2 * n + 1]
        return value

    def attention_consts(l, forward):
        ins = {
            "perm": (whole((WROWS, ROWS)), perms[l]),
            "perm_t": (whole((ROWS, WROWS)), perms_t[l]),
            "vec": (whole(vectors.shape), vectors),
        }
        if forward:
            ins["rows"] = (SCALARS, valid_rows)
            ins["cols"] = (SCALARS, valid_cols)
            ins["row_limit"] = (whole((NWIN, SLOT, 128)), row_limits[l])
            ins["col_limit"] = (whole((NWIN, SLOT, 128)), col_limits[l])
            ins["bias"] = (
                pl.BlockSpec((None, NGRP, SLOT, LANES), lambda i, l=l: (l, 0, 0, 0)), bias
            )
        return ins

    def vmem(*dims, dtype=BF16):
        return pltpu.VMEM(dims, dtype)

    attn_weights = {
        "stage": vmem(ch_count, C, widths["attn"]),
        "w_qkv": vmem(C, 3 * C),
        "w_proj": vmem(C, C),
        "load_sem": pltpu.SemaphoreType.DMA((4,)),
    }
    mlp_weights = {
        "w_down": vmem(C, HID),
        "w_up": vmem(C, HID),
        "load_sem": pltpu.SemaphoreType.DMA((4,)),
    }
    all_rows = local * ROWS
    mlp_rows = {
        "mlp_all": vmem(all_rows, C), "active_all": vmem(all_rows, HID),
        "pre_all": vmem(all_rows, HID), "low_all": vmem(all_rows, C),
        "up_grad": vmem(C, HID), "down_grad": vmem(C, HID),
        "sem_x": pltpu.SemaphoreType.DMA((2,)), "sem_y": pltpu.SemaphoreType.DMA((2,)),
    }
    wide = (per_image(ROWS, C), (local, ROWS, C), F32)
    thin = (per_image(ROWS, C), (local, ROWS, C), BF16)
    hidden = (per_image(ROWS, HID), (local, ROWS, HID), BF16)
    attn_saved = {
        "normed": thin,
        "qkv": (per_image(WROWS, 3 * C), (local, WROWS, 3 * C), BF16),
        "prob": (per_image(NWIN, NGRP, SLOT, LANES), (local, NWIN, NGRP, SLOT, LANES), BF16),
        "attended": thin,
    }
    sums = {"row_sums": (whole((8, C)), (8, C), F32)}
    up_sums = {**sums, "up_rows": (whole((1, HID)), (1, HID), F32)}
    attn_sums = {
        **sums,
        "qkv_rows": (whole((1, 3 * C)), (1, 3 * C), F32),
        "bias_grad": (whole((NGRP, SLOT, LANES)), (NGRP, SLOT, LANES), F32),
    }

    def given(spec, array):
        return (spec[0], array)

    mlp_flops = 2 * all_rows * C * HID * 2
    attn_flops = 2 * all_rows * C * C * 8

    def attention_forward(l, field, first=0, count=groups, before=None):
        ins, plan = weight_inputs(l, ["attn"]) if before is None else ({}, Plan(widths, l, layers))
        plan.group = first
        ins["field"] = (per_image(*field.shape[1:], first=first), field)
        ins.update(attention_consts(l, True))
        outs = {
            name: (spec, (count * GROUP,) + dims[1:], dtype)
            for name, (spec, dims, dtype) in {"middle": wide, **attn_saved}.items()
        }
        scratch = {"mixed": vmem(GROUP, C, WROWS), "windowed": vmem(GROUP, WROWS, C)}
        if before is None:
            outs["qkv_out"] = (FAR, (C, 3 * C), BF16)
            outs["proj_out"] = (FAR, (C, C), BF16)
            scratch.update(attn_weights)
            scratch["out_sem"] = pltpu.SemaphoreType.DMA((2,))
        else:
            ins["w_qkv"] = (whole((C, 3 * C)), before["qkv_out"])
            ins["w_proj"] = (whole((C, C)), before["proj_out"])
        results = call(
            functools.partial(attention_forward_kernel, plan=plan), f"attention_forward{l}_{first}",
            count, ins, outs, scratch, attn_flops * count // groups,
        )
        return results if before is None else {**before, **results}

    def rows_of(name, arrays):
        if len(arrays) == 1:
            return {name: given(wide, arrays[0])}
        return {f"{name}{n}": (whole(array.shape), array) for n, array in enumerate(arrays)}

    def begin(*moves):
        return [(part, step, exchange(part.array, step)) for part, step in moves]

    def arrive(number, value, moves):
        value, *received = tie(value, *[got for _, _, got in moves])
        stacked = stack_blocks(
            [(part, got, step) for (part, step, _), got in zip(moves, received)], me, f"stack{number}"
        )
        return value, [parts[0] for parts in stacked]

    if staged:
        moves = begin((down, y), (up, x), (parts1[0], y), (parts1[1], x), (parts1[2], y))
        early0 = attention_forward(0, padded, 0, groups - 1)
        early0["proj_out"], (down, up, *parts1) = arrive(4, early0["proj_out"], moves)
        early0["proj_out"] = wait_for(early0["proj_out"], down, up, *parts1)
        held[0] += [down, up]
        got = [exchange(part.array, core) for part in (down, up)]
        moves = begin((parts1[0], x), (parts1[1], y), (parts1[2], x))
        saved0 = attention_forward(0, padded, groups - 1, 1, early0)
        saved0["middle"], *got = tie(saved0["middle"], *got)
        other[0] = list(other[0]) + got
        saved0["middle"], parts1 = arrive(5, saved0["middle"], moves[:1])
        middle0 = [early0["middle"], wait_for(saved0["middle"], *parts1)]
        held.append(parts1)
    else:
        saved0 = early0 = attention_forward(0, padded)
        middle0 = [saved0["middle"]]
    ins, plan = weight_inputs(0, ["down", "up"])
    ins.update(rows_of("middle", middle0))
    ins["vec"] = (whole(vectors.shape), vectors)
    mlp0 = call(
        functools.partial(first_mlp_kernel, plan=plan), "first_mlp", groups, ins,
        {
            "result": wide, "mlp_in": thin, "active": hidden, "slope": hidden,
            "down_out": (FAR, (C, HID), BF16),
            "up_out": (FAR, (C, HID), BF16),
        },
        {**mlp_weights, "out_sem": pltpu.SemaphoreType.DMA((2,))},
        mlp_flops,
    )
    result0 = mlp0["result"]
    got = [exchange(part.array, core) for part in held[1]]
    result0, *got = tie(result0, *got)
    other.append(got)
    if staged:
        result0, late1 = arrive(6, result0, moves[1:])
        result0 = wait_for(result0, *late1)
        late_got = [exchange(part.array, core) for part in late1]

    saved1 = attention_forward(1, result0)
    if staged:
        saved1["middle"], *late_got = tie(saved1["middle"], *late_got)
        held[1] = held[1] + late1
        other[1] = other[1] + late_got
    ins, plan = weight_inputs(1, ["down", "up", "head"])
    ins["middle"] = given(wide, saved1["middle"])
    ins["vec"] = (whole(vectors.shape), vectors)
    ins["rows"] = (SCALARS, valid_rows)
    ins["cols"] = (SCALARS, valid_cols)
    ins["labels"] = (SCALARS, labels)
    ins["partner"] = (SCALARS, partner)
    ins["mix"] = (SCALARS, mix_level)
    cell = np.arange(ROWS)
    for name, place in (("cell_row", cell // GRID), ("cell_col", cell % GRID)):
        place = np.where(cell < CELLS, place, 99)[:, None].astype(np.int32)
        ins[name] = (whole((ROWS, 1)), jnp.asarray(place))
    outs = {
        "grad_mid": wide, **up_sums,
        "final_rows": (whole((2, C)), (2, C), F32),
        "head_rows": (whole((1, head_classes)), (1, head_classes), F32),
        "loss": (whole((1, 128)), (1, 128), F32),
        **grad_outputs(plan, x=["up", "head"], y=["down"]),
    }
    last = call(
        functools.partial(last_mlp_kernel, plan=plan, total_images=float(total_images)),
        "last_mlp", groups, ins, outs,
        {
            "slope": vmem(GROUP * ROWS, HID), "w_head": vmem(ch_count, C, widths["head"]),
            **mlp_weights, **mlp_rows,
            "pooled_all": vmem(16, C, dtype=F32), "logit_all": vmem(16, head_classes, dtype=F32),
            "head_grad": vmem(ch_count, C, widths["head"]),
        },
        3 * mlp_flops,
    )

    def attention_backward(l, grad_mid, field, saved, first, count, before=None, before_saved=None, store=True, collect=None):
        plan = Plan(widths, l, layers)
        ins = {
            "me": (SCALARS, me), "w_qkv": (whole((C, 3 * C)), saved["qkv_out"]),
            "w_proj": (whole((C, C)), saved["proj_out"]),
        }
        ins.update(attention_consts(l, False))
        wanted = ["qkv", "prob"] + (["normed", "attended"] if store else [])
        for name, array in [("grad_mid", grad_mid), ("field", field)] + [
            (name, saved[name]) for name in wanted
        ]:
            skip = first if array.shape[0] == local else 0
            ins[name] = (per_image(*array.shape[1:], first=skip), array)
        if before is not None:
            for name, (spec, _, _) in attn_sums.items():
                ins[name + "_in"] = (spec, before[name])
            for name in ("normed", "attended"):
                ins[name + "_in"] = (whole((first * GROUP, ROWS, C)), before_saved[name])
            for name in ("spread", "attn"):
                array = before[name + "_all"]
                ins[name + "_in"] = (whole(array.shape), array)
        rows_here = count * GROUP * ROWS
        outs = dict(attn_sums)
        scratch = {
            "dq": vmem(GROUP, C, WROWS), "dkv": vmem(GROUP, WROWS, 2 * C),
            "joined": vmem(GROUP, WROWS, C),
        }
        need_grad = l > 0
        if need_grad:
            outs["grad"] = wide
        if store:
            if collect is None:
                outs.update(grad_outputs(plan, a=["attn"]))
            else:
                outs.update(cut_attention_outputs(plan))
                plan.collect = (layers, head_real, share - 1, owners)
                ins.update({name: (whole(array.shape), array) for name, array in collect.items()})
                scratch["small_rows"] = vmem(device_count, share, dtype=F32)
                scratch["spread_table"] = vmem(HEADS * SLOT, 128, dtype=F32)
                scratch["pairs"] = vmem(2, len(owners), C, 128)
            scratch.update({
                "normed_all": vmem(all_rows, C), "attended_all": vmem(all_rows, C),
                "spread_all": vmem(all_rows, 3 * C), "attn_all": vmem(all_rows, C),
                "attn_grad": vmem(ch_count, C, widths["attn"]),
                "sem_a": pltpu.SemaphoreType.DMA((4,)),
            })
        else:
            outs["spread_all"] = (whole((rows_here, 3 * C)), (rows_here, 3 * C), BF16)
            outs["attn_all"] = (whole((rows_here, C)), (rows_here, C), BF16)
        return call(
            functools.partial(
                backward_attention_kernel, plan=plan,
                earlier=0 if before is None else first * GROUP, need_grad=need_grad,
            ),
            f"attention_backward{l}_{first}", count, ins, outs, scratch,
            2 * attn_flops * count // groups,
        )

    x1, y1 = chain_of(last, "x", "up", "head"), chain_of(last, "y", "down")
    if regular:
        start(x1, y1)
    back1 = attention_backward(1, last["grad_mid"], mlp0["result"], saved1, 0, groups)
    a1 = chain_of(back1, "a", "attn")
    grad = back1["grad"]
    if regular:
        grad = meet(grad, x1, y1)
        x1, y1 = combine([[x1], [y1]], me, "sum1")
        grad = after(grad, x1, y1)
        start(x1, y1, a1)

    plan = Plan(widths, 0, layers)
    ins = {
        "me": (SCALARS, me),
        "w_down": (whole((C, HID)), mlp0["down_out"]),
        "w_up": (whole((C, HID)), mlp0["up_out"]),
    }
    ins["grad"] = given(wide, grad)
    ins.update(rows_of("middle", middle0))
    ins["mlp_in"] = given(thin, mlp0["mlp_in"])
    ins["active"] = given(hidden, mlp0["active"])
    ins["slope"] = given(hidden, mlp0["slope"])
    ins["vec"] = (whole(vectors.shape), vectors)
    first = call(
        functools.partial(backward_mlp_kernel, plan=plan), "mlp_backward0", groups, ins,
        {"grad_mid": wide, **up_sums, **grad_outputs(plan, x=["up"], y=["down"])},
        dict(mlp_rows), 2 * mlp_flops,
    )
    x0, y0 = chain_of(first, "x", "up"), chain_of(first, "y", "down")
    grad_mid = first["grad_mid"]
    if regular:
        grad_mid = meet(grad_mid, x1, y1, a1)
        x1, y1, a1 = combine([[x1], [y1], [a1]], me, "sum2")
        grad_mid = after(grad_mid, x1, y1, a1)
        start(x1, y1, a1, x0, y0)
    before0 = attention_backward(0, grad_mid, padded, early0, 0, groups - 1, store=False)
    if regular:
        before0["row_sums"] = meet(before0["row_sums"], a1, x0, y0, x1, y1)
        a1, x0, y0, z1 = combine([[a1], [x0], [y0], [x1, y1]], me, "sum3")
        grad_mid = after(grad_mid, a1, x0, y0, z1)
        start(a1, x0, y0, z1)
    small_parts = None
    if regular:
        small_parts = {
            "mlp_rows0": first["row_sums"], "up_rows0": first["up_rows"],
            "row_sums1": back1["row_sums"], "qkv_rows1": back1["qkv_rows"],
            "mlp_rows1": last["row_sums"], "up_rows1": last["up_rows"],
            "bias_grad1": back1["bias_grad"], "final_rows": last["final_rows"],
            "head_rows": last["head_rows"], "loss": last["loss"],
        }
    back0 = attention_backward(
        0, grad_mid, padded, saved0, groups - 1, 1, before0, early0, collect=small_parts
    )
    a0 = chain_of(back0, "a", "attn")
    if regular:
        b0 = chain_of(back0, "b", pair_at=widths["attn"] - widths["attn"] * 2 // 3)
        waiting = (a1, x0, y0, z1)
        a0.send, b0.send, *got = tie(a0.send, b0.send, *[chain.received for chain in waiting])
        for chain, array in zip(waiting, got):
            chain.received = array

    if regular:
        start(a0, b0)
        z1, x0, y0 = combine([[z1], [x0], [y0]], me, "sum5")
        start(z1, x0, y0)
        a0.received, b0.received, x0.keep = tie(a0.received, b0.received, x0.keep)
        a0, b0 = combine([[a0], [b0]], me, "sum6")
        start(a0, b0)
        x0.received, y0.received, z1.received = tie(x0.received, y0.received, z1.received)
        (z0,) = combine([[x0, y0, a1]], me, "sum7")
        start(z0)
        a0, b0 = combine([[a0], [b0]], me, "sum8")
        start(a0, b0)
        (z0,) = combine([[z0]], me, "sum9")
        start(z0)
        own1, square1 = finish(z1, "own1")
        (a0,) = combine([[a0, b0]], me, "sum10")
        start(a0)
        own0, square0 = finish(z0, "own0")
        (a0,) = combine([[a0]], me, "sum11")
        start(a0)
        own_attn, message = finish_pair(a0, [square0, square1], device_count, share, "own_attn")
    else:
        square, own_parts = jnp.zeros((1, 128), F32), []
        for chain in (a0, x0, y0, a1, x1, y1):
            start(chain)
            while chain.steps:
                (chain,) = combine([[chain]], me, "sum")
                start(chain)
            part, part_square = finish(chain, "own")
            square = square + part_square
            own_parts.append(part)
        own_attn = own_parts[0]
        own0, own1 = jnp.concatenate(own_parts[1:4], 1), jnp.concatenate(own_parts[4:], 1)
        (rows_all,) = small_call(
            lambda *refs: collect_rows(
                layers, head_real, share - 1, refs[:-2], refs[-2], refs[-1]
            ),
            "collect",
            [part[name] for part in ((first, back0), (last, back1))
             for part, name in (
                 (part[1], "row_sums"), (part[1], "qkv_rows"), (part[0], "row_sums"),
                 (part[0], "up_rows"), (part[1], "bias_grad"))]
            + [last["final_rows"], last["head_rows"], last["loss"]],
            [((device_count, share), F32)],
            stream=True,
            scratch=[pltpu.VMEM((HEADS * SLOT, 128), F32)],
        )
        rows_all = lax.all_to_all(rows_all, ("win", "ch"), 0, 0, tiled=True)
        message = jnp.concatenate([jnp.sum(rows_all, 0, keepdims=True), square], 1)
        message = jnp.broadcast_to(message, (device_count, share + 128))
    message = lax.all_to_all(message, ("win", "ch"), 0, 0, tiled=True)
    starts = [
        {"attn": (1, 0), "up": (2, 0), "down": (2, widths["up"])},
        {
            "attn": (2, widths["up"] + widths["down"]), "up": (0, 0), "head": (0, widths["up"]),
            "down": (0, widths["up"] + widths["head"]),
        },
    ]
    arrays = [
        [w_qkv, m_qkv, v_qkv], [w_proj, m_proj, v_proj], [w_fc1, m_fc1, v_fc1],
        [w_fc2, m_fc2, v_fc2], [w_head, m_head, v_head], [vectors, m_vec, v_vec],
        [rel_table, m_rel, v_rel],
    ]
    turns = {3: (0, 2, 1), 6: (2, 0, 1)}
    turned = [
        a.transpose(turns[n]) if n in turns else a for n, group in enumerate(arrays) for a in group
    ]
    results = small_call(
        functools.partial(
            update_kernel, starts, widths,
            (vectors.shape[0], layers * HEADS, offsets, share, share - 1),
        ),
        "update",
        [own1, own_attn, own0, message] + turned,
        [((1, 1), F32)] * 2 + [(a.shape, F32) for a in turned],
        stream=True,
    )
    loss_total, grad_norm, *results = results
    outs = [loss_total[0, 0], grad_norm[0, 0]]
    for n in range(0, len(results), 3):
        back = {3: (0, 2, 1), 6: (1, 2, 0)}.get(n // 3)
        outs += [r if back is None else r.transpose(back) for r in results[n : n + 3]]
    return tuple(outs)


def solution(mesh):
    cut = P(None, "win", "ch")
    down = P(None, "ch", "win")
    head = P("win", "ch")
    rows = P(None, ("win", "ch"))
    in_specs = (
        (P(None, ("win", "ch"), None, None),) + (rows,) * 4 + (P(),)
        + (cut,) * 9 + (down,) * 3 + (head,) * 3 + (P(),) * 6
    )
    out_specs = (P(),) * 2 + (cut,) * 9 + (down,) * 3 + (head,) * 3 + (P(),) * 6
    return jax.shard_map(
        per_device, mesh=mesh, in_specs=in_specs, out_specs=out_specs, check_vma=False
    )
```

profile of v0, /device:TPU:0, one launch (start us, length us, event | category | flops | bytes accessed | tf_op | source)
XLA Modules:
  0.0 206.2 jit_solution(7888584511026868316)
XLA Ops:
  2.5 4.0 %collective-permute-start = (bf16[1,48,384]{2,1,0:T(8,128)(2,1)}, bf16[1,48,384]{2,1,0:T(8,128)(2,1)S(1)}, u32[]{:S(2)}, u32[]{:S(2)}) collective-permute-start(bf16[1,48,384]{2,1,0:T(8,128)(2,1)} %bitcast.77), channel_id=1, source_target_pairs={{0,16},{4,20},{8,24},{12,28},{16,0},{20,4},{24,8},{28,12},{1,17},{... | collective-permute-start | bytes 110600 | tf_op jit(solution)/shard_map/ppermute | solution.py:777
  15.5 2.5 %collective-permute-done.2.refs_3_ = bf16[1,48,768]{2,1,0:T(8,128)(2,1)S(1)} collective-permute-done((bf16[1,48,768]{2,1,0:T(8,128)(2,1)S(1)}, bf16[1,48,768]{2,1,0:T(8,128)(2,1)S(1)}, u32[]{:S(2)}, u32[]{:S(2)}) %collective-permute-start.2) | collective-permute-done | bytes 73760 | tf_op jit(solution)/shard_map/ppermute | solution.py:777
  23.2 3.0 %collective-permute-done.8.refs_1_ = bf16[1,48,1408]{2,1,0:T(8,128)(2,1)S(1)} collective-permute-done((bf16[1,48,1408]{2,1,0:T(8,128)(2,1)S(1)}, bf16[1,48,1408]{2,1,0:T(8,128)(2,1)S(1)}, u32[]{:S(2)}, u32[]{:S(2)}) %collective-permute-start.8) | collective-permute-done | bytes 135200 | tf_op jit(solution)/shard_map/ppermute | solution.py:777
  32.3 4.2 %collective-permute-done.7.refs_3_ = bf16[8,48,128]{2,1,0:T(8,128)(2,1)S(1)} collective-permute-done((bf16[8,48,128]{2,1,0:T(8,128)(2,1)S(1)}, bf16[8,48,128]{2,1,0:T(8,128)(2,1)S(1)}, u32[]{:S(2)}, u32[]{:S(2)}) %collective-permute-start.7) | collective-permute-done | bytes 98336 | tf_op jit(solution)/shard_map/ppermute | solution.py:777
  43.8 6.3 %attention_forward0_0.1 = (f32[2,208,384]{2,1,0:T(8,128)S(1)}, bf16[2,208,384]{2,1,0:T(8,128)(2,1)S(1)}, bf16[2,256,1152]{2,1,0:T(8,128)(2,1)S(1)}, bf16[2,4,3,6...) custom-call(bf16[2,384,256]{2,1,0:T(8,128)(2,1)S(1)} %bitcast.97, ...), custom_call_target="tpu_custom_call" | custom-call | flops 981467136 | bytes 2731560 | tf_op jit(solution)/shard_map/attention_forward0_0/pallas_call | solution.py:758
  50.8 2.3 %collective-permute-done.18.refs_9_ = bf16[4,48,384]{2,1,0:T(8,128)(2,1)S(1)} collective-permute-done((bf16[4,48,384]{2,1,0:T(8,128)(2,1)S(1)}, bf16[4,48,384]{2,1,0:T(8,128)(2,1)S(1)}, u32[]{:S(2)}, u32[]{:S(2)}) %collective-permute-start.18) | collective-permute-done | bytes 147488 | tf_op jit(solution)/shard_map/ppermute | solution.py:777
  55.9 5.2 %attention_forward0_1.1 = (f32[2,208,384]{2,1,0:T(8,128)S(1)}, bf16[2,208,384]{2,1,0:T(8,128)(2,1)S(1)}, bf16[2,256,1152]{2,1,0:T(8,128)(2,1)S(1)}, bf16[2,4,3,6...) custom-call(bf16[4,208,384]{2,1,0:T(8,128)(2,1)S(1)} %pad.4.refs_5_.refs_0_.refs_7_, bf16[256,208]{1,0:T(8,128)(2,1)S(1)} %copy-done.13, ...), custom_call_target="tpu_custom_call" | custom-call | flops 981467136 | bytes 2731552 | tf_op jit(solution)/shard_map/attention_forward0_1/pallas_call | solution.py:758
  61.1 2.2 %collective-permute-done.21.refs_1_ = bf16[8,48,384]{2,1,0:T(8,128)(2,1)S(1)} collective-permute-done((bf16[8,48,384]{2,1,0:T(8,128)(2,1)S(1)}, bf16[8,48,384]{2,1,0:T(8,128)(2,1)S(1)}, u32[]{:S(2)}, u32[]{:S(2)}) %collective-permute-start.21) | collective-permute-done | bytes 294944 | tf_op jit(solution)/shard_map/ppermute | solution.py:777
  66.9 6.0 %first_mlp.1 = (f32[4,208,384]{2,1,0:T(8,128)S(1)}, bf16[4,208,384]{2,1,0:T(8,128)(2,1)S(1)}, bf16[4,208,1536]{2,1,0:T(8,128)(2,1)S(1)}, bf16[4,208,1536]{2,1,0:...) custom-call(bf16[2,384,384]{2,1,0:T(8,128)(2,1)S(1)} %bitcast.87, ...), custom_call_target="tpu_custom_call" | custom-call | flops 1962934272 | bytes 3681800 | tf_op jit(solution)/shard_map/first_mlp/pallas_call | solution.py:758
  74.5 3.2 %collective-permute-done.23.refs_1_ = bf16[8,48,640]{2,1,0:T(8,128)(2,1)S(1)} collective-permute-done((bf16[8,48,640]{2,1,0:T(8,128)(2,1)S(1)}, bf16[8,48,640]{2,1,0:T(8,128)(2,1)S(1)}, u32[]{:S(2)}, u32[]{:S(2)}) %collective-permute-start.23) | collective-permute-done | bytes 491552 | tf_op jit(solution)/shard_map/ppermute | solution.py:777
  79.0 10.3 %attention_forward1_0.1 = (f32[4,208,384]{2,1,0:T(8,128)S(1)}, bf16[4,208,384]{2,1,0:T(8,128)(2,1)S(1)}, bf16[4,256,1152]{2,1,0:T(8,128)(2,1)S(1)}, bf16[4,4,3,6...) custom-call(bf16[2,384,384]{2,1,0:T(8,128)(2,1)S(1)} %bitcast.60, ...), custom_call_target="tpu_custom_call" | custom-call | flops 1962934272 | bytes 3370536 | tf_op jit(solution)/shard_map/attention_forward1_0/pallas_call | solution.py:758
  89.4 14.6 %last_mlp.1 = (f32[4,208,384]{2,1,0:T(8,128)S(1)}, f32[8,384]{1,0:T(8,128)S(1)}, f32[1,1536]{1,0:T(1,128)S(1)}, f32[2,384]{1,0:T(2,128)S(1)}, f32[1,1024]{1,0:T(...) custom-call(bf16[2,384,640]{2,1,0:T(8,128)(2,1)S(1)} %bitcast.82, ...), custom_call_target="tpu_custom_call" | custom-call | flops 5888802816 | bytes 4470472 | tf_op jit(solution)/shard_map/last_mlp/pallas_call | solution.py:758
  104.5 12.6 %attention_backward1_0.1 = (f32[8,384]{1,0:T(8,128)S(1)}, f32[1,1152]{1,0:T(1,128)S(1)}, f32[3,64,256]{2,1,0:T(8,128)S(1)}, f32[4,208,384]{2,1,0:T(8,128)S(1)}, ...) custom-call(s32[2]{0:T(128)S(1)} %pad_add_fusion.me_ref.refs_4_.refs_2_.refs_0_, ...), custom_call_target="tpu_custom_call" | custom-call | flops 3925868544 | bytes 9203208 | tf_op jit(solution)/shard_map/attention_backward1_0/pallas_call | solution.py:758
  121.1 7.7 %mlp_backward0.1 = (f32[4,208,384]{2,1,0:T(8,128)S(1)}, f32[8,384]{1,0:T(8,128)S(1)}, f32[1,1536]{1,0:T(1,128)S(1)}, bf16[2,384,384]{2,1,0:T(8,128)(2,1)S(1)}, b...) custom-call(s32[2]{0:T(128)S(1)} %pad_add_fusion.me_ref.refs_4_.refs_2_.refs_0_, ...), custom_call_target="tpu_custom_call" | custom-call | flops 3925868544 | bytes 10710536 | tf_op jit(solution)/shard_map/mlp_backward0/pallas_call | solution.py:758
  129.3 3.5 %collective-permute-done.29.refs_1_ = bf16[8,48,640]{2,1,0:T(8,128)(2,1)S(1)} collective-permute-done((bf16[8,48,640]{2,1,0:T(8,128)(2,1)S(1)}, bf16[8,48,640]{2,1,0:T(8,128)(2,1)S(1)}, u32[]{:S(2)}, u32[]{:S(2)}) %collective-permute-start.29) | collective-permute-done | bytes 491552 | tf_op jit(solution)/shard_map/ppermute | solution.py:777
  136.6 5.1 %attention_backward0_0.1 = (f32[8,384]{1,0:T(8,128)S(1)}, f32[1,1152]{1,0:T(1,128)S(1)}, f32[3,64,256]{2,1,0:T(8,128)S(1)}, bf16[416,1152]{1,0:T(8,128)(2,1)S(1)}, bf16[416,384]{1,0:T(8,128)(2,1)S(1)}) custom-call(s32[2]{0:T(128)S(1)} %pad_add_fusion.me_ref.refs_4_.refs_2_.refs_0_, bf16[384,1152]{1,0:T(8,128)(2,1)S(1)} %get-tuple-element.329.refs_9_.refs_1_, ...), custom_call_target="tpu_custom_call" | custom-call | flops 1962934272 | bytes 5320200 | tf_op jit(solution)/shard_map/attention_backward0_0/pallas_call | solution.py:758
  141.7 3.5 %collective-permute-done.36.refs_9_ = bf16[4,48,384]{2,1,0:T(8,128)(2,1)S(1)} collective-permute-done((bf16[4,48,384]{2,1,0:T(8,128)(2,1)S(1)}, bf16[4,48,384]{2,1,0:T(8,128)(2,1)S(1)}, u32[]{:S(2)}, u32[]{:S(2)}) %collective-permute-start.36) | collective-permute-done | bytes 147488 | tf_op jit(solution)/shard_map/ppermute | solution.py:777
  151.4 8.6 %attention_backward0_1.1 = (f32[8,384]{1,0:T(8,128)}, f32[1,1152]{1,0:T(1,128)}, f32[3,64,256]{2,1,0:T(8,128)}, bf16[2,384,256]{2,1,0:T(8,128)(2,1)S(1)}, bf16[2...) custom-call(s32[2]{0:T(128)S(1)} %pad_add_fusion.me_ref.refs_4_.refs_2_.refs_0_, ...), custom_call_target="tpu_custom_call" | custom-call | flops 1962934272 | bytes 8347656 | tf_op jit(solution)/shard_map/attention_backward0_1/pallas_call | solution.py:758
  167.5 5.4 %collective-permute-done.43.received = bf16[1,48,1024]{2,1,0:T(8,128)(2,1)S(1)} collective-permute-done((bf16[1,48,1024]{2,1,0:T(8,128)(2,1)S(1)}, bf16[1,48,1024]{2,1,0:T(8,128)(2,1)S(1)}, u32[]{:S(2)}, u32[]{:S(2)}) %collective-permute-start.43) | collective-permute-done | bytes 98336 | tf_op jit(solution)/shard_map/ppermute | solution.py:777
  176.2 3.0 %collective-permute-done.48.refs_1_ = bf16[4,48,256]{2,1,0:T(8,128)(2,1)S(1)} collective-permute-done((bf16[4,48,256]{2,1,0:T(8,128)(2,1)S(1)}, bf16[4,48,256]{2,1,0:T(8,128)(2,1)S(1)}, u32[]{:S(2)}, u32[]{:S(2)}) %collective-permute-start.48) | collective-permute-done | bytes 98336 | tf_op jit(solution)/shard_map/ppermute | solution.py:777
  180.5 2.1 collective-permute-start.50
  184.0 2.9 %collective-permute-done.50.refs_1_ = bf16[2,48,512]{2,1,0:T(8,128)(2,1)S(1)} collective-permute-done((bf16[2,48,512]{2,1,0:T(8,128)(2,1)S(1)}, bf16[2,48,512]{2,1,0:T(8,128)(2,1)S(1)}, u32[]{:S(2)}, u32[]{:S(2)}) %collective-permute-start.50) | collective-permute-done | bytes 98336 | tf_op jit(solution)/shard_map/ppermute | solution.py:777
  190.4 2.5 %collective-permute-done.51.received = bf16[1,48,512]{2,1,0:T(8,128)(2,1)S(1)} collective-permute-done((bf16[1,48,512]{2,1,0:T(8,128)(2,1)S(1)}, bf16[1,48,512]{2,1,0:T(8,128)(2,1)S(1)}, u32[]{:S(2)}, u32[]{:S(2)}) %collective-permute-start.51) | collective-permute-done | bytes 49184 | tf_op jit(solution)/shard_map/ppermute | solution.py:777
  193.2 10.8 %all_to_all.11 = f32[32,1,768]{2,1,0:T(1,128)S(1)} all-to-all(f32[32,1,768]{2,1,0:T(1,128)S(1)} %copy.69), channel_id=1, replica_groups=mesh['win'=8,'ch'=4] {'win','ch'}, dimensions={0} | all-to-all | bytes 196608 | tf_op jit(solution)/shard_map/all_to_all | solution.py:1665
  (211 shorter events, 72.6 us)
Async XLA Ops:
  37.8 12.3 %collective-permute-start.14 = (bf16[8,48,384]{2,1,0:T(8,128)(2,1)S(1)}, bf16[8,48,384]{2,1,0:T(8,128)(2,1)S(1)}, u32[]{:S(2)}, u32[]{:S(2)}) collective-permute-start(bf16[8,48,384]{2,1,0:T(8,128)(2,1)S(1)} %get-tuple-element.312.refs_0_), channel_id=1, source_target_pairs={{0,4},{4,0},{8,12},{12,8},{16,20},{20,16},{24,28},{28,24},{1,5},{5... | collective-permute-start | bytes 884744 | tf_op jit(solution)/shard_map/ppermute | solution.py:777
  39.0 11.1 %collective-permute-start.15 = (bf16[8,48,384]{2,1,0:T(8,128)(2,1)S(1)}, bf16[8,48,384]{2,1,0:T(8,128)(2,1)S(1)}, u32[]{:S(2)}, u32[]{:S(2)}) collective-permute-start(bf16[8,48,384]{2,1,0:T(8,128)(2,1)S(1)} %get-tuple-element.313.refs_2_), channel_id=1, source_target_pairs={{0,2},{1,3},{2,0},{3,1},{4,6},{5,7},{6,4},{7,5},{8,10},{9,11},{10,... | collective-permute-start | bytes 884744 | tf_op jit(solution)/shard_map/ppermute | solution.py:777
  41.1 12.0 %collective-permute-start.17 = (bf16[4,48,640]{2,1,0:T(8,128)(2,1)S(1)}, bf16[4,48,640]{2,1,0:T(8,128)(2,1)S(1)}, u32[]{:S(2)}, u32[]{:S(2)}) collective-permute-start(bf16[4,48,640]{2,1,0:T(8,128)(2,1)S(1)} %get-tuple-element.315.refs_6_), channel_id=1, source_target_pairs={{0,2},{1,3},{2,0},{3,1},{4,6},{5,7},{6,4},{7,5},{8,10},{9,11},{10,... | collective-permute-start | bytes 737288 | tf_op jit(solution)/shard_map/ppermute | solution.py:777
  42.7 10.4 %collective-permute-start.18 = (bf16[4,48,384]{2,1,0:T(8,128)(2,1)S(1)}, bf16[4,48,384]{2,1,0:T(8,128)(2,1)S(1)}, u32[]{:S(2)}, u32[]{:S(2)}) collective-permute-start(bf16[4,48,384]{2,1,0:T(8,128)(2,1)S(1)} %get-tuple-element.316.refs_8_), channel_id=1, source_target_pairs={{0,4},{4,0},{8,12},{12,8},{16,20},{20,16},{24,28},{28,24},{1,5},{5... | collective-permute-start | bytes 442376 | tf_op jit(solution)/shard_map/ppermute | solution.py:777
  64.1 13.6 %collective-permute-start.23 = (bf16[8,48,640]{2,1,0:T(8,128)(2,1)S(1)}, bf16[8,48,640]{2,1,0:T(8,128)(2,1)S(1)}, u32[]{:S(2)}, u32[]{:S(2)}) collective-permute-start(bf16[8,48,640]{2,1,0:T(8,128)(2,1)S(1)} %get-tuple-element.347.refs_0_), channel_id=1, source_target_pairs={{0,4},{4,0},{8,12},{12,8},{16,20},{20,16},{24,28},{28,24},{1,5},{5... | collective-permute-start | bytes 1474568 | tf_op jit(solution)/shard_map/ppermute | solution.py:777
  78.4 11.0 %collective-permute-start.25 = (bf16[16,48,640]{2,1,0:T(8,128)(2,1)S(1)}, bf16[16,48,640]{2,1,0:T(8,128)(2,1)S(1)}, u32[]{:S(2)}, u32[]{:S(2)}) collective-permute-start(bf16[16,48,640]{2,1,0:T(8,128)(2,1)S(1)} %get-tuple-element.357), channel_id=1, source_target_pairs={{0,1},{1,0},{2,3},{3,2},{4,5},{5,4},{6,7},{7,6},{8,9},{9,8},{10,11... | collective-permute-start | bytes 2949128 | tf_op jit(solution)/shard_map/ppermute | solution.py:777
  78.5 10.9 %collective-permute-start.26 = (bf16[16,48,384]{2,1,0:T(8,128)(2,1)S(1)}, bf16[16,48,384]{2,1,0:T(8,128)(2,1)S(1)}, u32[]{:S(2)}, u32[]{:S(2)}) collective-permute-start(bf16[16,48,384]{2,1,0:T(8,128)(2,1)S(1)} %get-tuple-element.359), channel_id=1, source_target_pairs={{0,1},{1,0},{2,3},{3,2},{4,5},{5,4},{6,7},{7,6},{8,9},{9,8},{10,11... | collective-permute-start | bytes 1769480 | tf_op jit(solution)/shard_map/ppermute | solution.py:777
  104.0 13.4 %collective-permute-start.27 = (bf16[16,48,640]{2,1,0:T(8,128)(2,1)S(1)}, bf16[16,48,640]{2,1,0:T(8,128)(2,1)S(1)}, u32[]{:S(2)}, u32[]{:S(2)}) collective-permute-start(bf16[16,48,640]{2,1,0:T(8,128)(2,1)S(1)} %bitcast.81), channel_id=1, source_target_pairs={{0,1},{1,0},{2,3},{3,2},{4,5},{5,4},{6,7},{7,6},{8,9},{9,8},{10,11... | collective-permute-start | bytes 2949128 | tf_op jit(solution)/shard_map/ppermute | solution.py:777
  104.1 13.2 %collective-permute-start.28 = (bf16[16,48,384]{2,1,0:T(8,128)(2,1)S(1)}, bf16[16,48,384]{2,1,0:T(8,128)(2,1)S(1)}, u32[]{:S(2)}, u32[]{:S(2)}) collective-permute-start(bf16[16,48,384]{2,1,0:T(8,128)(2,1)S(1)} %bitcast.93), channel_id=1, source_target_pairs={{0,1},{1,0},{2,3},{3,2},{4,5},{5,4},{6,7},{7,6},{8,9},{9,8},{10,11... | collective-permute-start | bytes 1769480 | tf_op jit(solution)/shard_map/ppermute | solution.py:777
  117.2 12.2 %collective-permute-start.31 = (bf16[16,48,384]{2,1,0:T(8,128)(2,1)S(1)}, bf16[16,48,384]{2,1,0:T(8,128)(2,1)S(1)}, u32[]{:S(2)}, u32[]{:S(2)}) collective-permute-start(bf16[16,48,384]{2,1,0:T(8,128)(2,1)S(1)} %bitcast.85), channel_id=1, source_target_pairs={{0,1},{1,0},{2,3},{3,2},{4,5},{5,4},{6,7},{7,6},{8,9},{9,8},{10,11... | collective-permute-start | bytes 1769480 | tf_op jit(solution)/shard_map/ppermute | solution.py:777
  118.3 11.1 %collective-permute-start.30 = (bf16[8,48,384]{2,1,0:T(8,128)(2,1)S(1)}, bf16[8,48,384]{2,1,0:T(8,128)(2,1)S(1)}, u32[]{:S(2)}, u32[]{:S(2)}) collective-permute-start(bf16[8,48,384]{2,1,0:T(8,128)(2,1)S(1)} %get-tuple-element.386), channel_id=1, source_target_pairs={{0,4},{4,0},{8,12},{12,8},{16,20},{20,16},{24,28},{28,24},{1,5},{5... | collective-permute-start | bytes 884744 | tf_op jit(solution)/shard_map/ppermute | solution.py:777
  119.6 13.3 %collective-permute-start.29 = (bf16[8,48,640]{2,1,0:T(8,128)(2,1)S(1)}, bf16[8,48,640]{2,1,0:T(8,128)(2,1)S(1)}, u32[]{:S(2)}, u32[]{:S(2)}) collective-permute-start(bf16[8,48,640]{2,1,0:T(8,128)(2,1)S(1)} %get-tuple-element.385), channel_id=1, source_target_pairs={{0,2},{1,3},{2,0},{3,1},{4,6},{5,7},{6,4},{7,5},{8,10},{9,11},{10,... | collective-permute-start | bytes 1474568 | tf_op jit(solution)/shard_map/ppermute | solution.py:777
  128.8 12.9 %collective-permute-start.33 = (bf16[16,48,384]{2,1,0:T(8,128)(2,1)S(1)}, bf16[16,48,384]{2,1,0:T(8,128)(2,1)S(1)}, u32[]{:S(2)}, u32[]{:S(2)}) collective-permute-start(bf16[16,48,384]{2,1,0:T(8,128)(2,1)S(1)} %bitcast.86), channel_id=1, source_target_pairs={{0,1},{1,0},{2,3},{3,2},{4,5},{5,4},{6,7},{7,6},{8,9},{9,8},{10,11... | collective-permute-start | bytes 1769480 | tf_op jit(solution)/shard_map/ppermute | solution.py:777
  128.8 12.9 %collective-permute-start.34 = (bf16[16,48,384]{2,1,0:T(8,128)(2,1)S(1)}, bf16[16,48,384]{2,1,0:T(8,128)(2,1)S(1)}, u32[]{:S(2)}, u32[]{:S(2)}) collective-permute-start(bf16[16,48,384]{2,1,0:T(8,128)(2,1)S(1)} %bitcast.84), channel_id=1, source_target_pairs={{0,1},{1,0},{2,3},{3,2},{4,5},{5,4},{6,7},{7,6},{8,9},{9,8},{10,11... | collective-permute-start | bytes 1769480 | tf_op jit(solution)/shard_map/ppermute | solution.py:777
  133.7 11.5 %collective-permute-start.32 = (bf16[8,48,384]{2,1,0:T(8,128)(2,1)S(1)}, bf16[8,48,384]{2,1,0:T(8,128)(2,1)S(1)}, u32[]{:S(2)}, u32[]{:S(2)}) collective-permute-start(bf16[8,48,384]{2,1,0:T(8,128)(2,1)S(1)} %get-tuple-element.406), channel_id=1, source_target_pairs={{0,2},{1,3},{2,0},{3,1},{4,6},{5,7},{6,4},{7,5},{8,10},{9,11},{10,... | collective-permute-start | bytes 884744 | tf_op jit(solution)/shard_map/ppermute | solution.py:777
  135.3 9.9 %collective-permute-start.35 = (bf16[4,48,640]{2,1,0:T(8,128)(2,1)S(1)}, bf16[4,48,640]{2,1,0:T(8,128)(2,1)S(1)}, u32[]{:S(2)}, u32[]{:S(2)}) collective-permute-start(bf16[4,48,640]{2,1,0:T(8,128)(2,1)S(1)} %get-tuple-element.409), channel_id=1, source_target_pairs={{0,4},{4,0},{8,12},{12,8},{16,20},{20,16},{24,28},{28,24},{1,5},{5... | collective-permute-start | bytes 737288 | tf_op jit(solution)/shard_map/ppermute | solution.py:777
  136.1 9.1 %collective-permute-start.36 = (bf16[4,48,384]{2,1,0:T(8,128)(2,1)S(1)}, bf16[4,48,384]{2,1,0:T(8,128)(2,1)S(1)}, u32[]{:S(2)}, u32[]{:S(2)}) collective-permute-start(bf16[4,48,384]{2,1,0:T(8,128)(2,1)S(1)} %get-tuple-element.410), channel_id=1, source_target_pairs={{0,2},{1,3},{2,0},{3,1},{4,6},{5,7},{6,4},{7,5},{8,10},{9,11},{10,... | collective-permute-start | bytes 442376 | tf_op jit(solution)/shard_map/ppermute | solution.py:777
  146.2 13.8 %collective-permute-start.38 = (bf16[8,48,384]{2,1,0:T(8,128)(2,1)S(1)}, bf16[8,48,384]{2,1,0:T(8,128)(2,1)S(1)}, u32[]{:S(2)}, u32[]{:S(2)}) collective-permute-start(bf16[8,48,384]{2,1,0:T(8,128)(2,1)S(1)} %get-tuple-element.454), channel_id=1, source_target_pairs={{0,2},{1,3},{2,0},{3,1},{4,6},{5,7},{6,4},{7,5},{8,10},{9,11},{10,... | collective-permute-start | bytes 884744 | tf_op jit(solution)/shard_map/ppermute | solution.py:777
  147.8 12.3 %collective-permute-start.39 = (bf16[8,48,384]{2,1,0:T(8,128)(2,1)S(1)}, bf16[8,48,384]{2,1,0:T(8,128)(2,1)S(1)}, u32[]{:S(2)}, u32[]{:S(2)}) collective-permute-start(bf16[8,48,384]{2,1,0:T(8,128)(2,1)S(1)} %get-tuple-element.455), channel_id=1, source_target_pairs={{0,4},{4,0},{8,12},{12,8},{16,20},{20,16},{24,28},{28,24},{1,5},{5... | collective-permute-start | bytes 884744 | tf_op jit(solution)/shard_map/ppermute | solution.py:777
  148.5 11.5 %collective-permute-start.40 = (bf16[2,48,1024]{2,1,0:T(8,128)(2,1)S(1)}, bf16[2,48,1024]{2,1,0:T(8,128)(2,1)S(1)}, u32[]{:S(2)}, u32[]{:S(2)}) collective-permute-start(bf16[2,48,1024]{2,1,0:T(8,128)(2,1)S(1)} %get-tuple-element.456), channel_id=1, source_target_pairs={{0,8},{4,12},{8,0},{12,4},{16,24},{20,28},{24,16},{28,20},{1,9},{5... | collective-permute-start | bytes 589832 | tf_op jit(solution)/shard_map/ppermute | solution.py:777
  150.0 10.0 %collective-permute-start.37 = (bf16[4,48,384]{2,1,0:T(8,128)(2,1)S(1)}, bf16[4,48,384]{2,1,0:T(8,128)(2,1)S(1)}, u32[]{:S(2)}, u32[]{:S(2)}) collective-permute-start(bf16[4,48,384]{2,1,0:T(8,128)(2,1)S(1)} %get-tuple-element.453), channel_id=1, source_target_pairs={{0,4},{4,0},{8,12},{12,8},{16,20},{20,16},{24,28},{28,24},{1,5},{5... | collective-permute-start | bytes 442376 | tf_op jit(solution)/shard_map/ppermute | solution.py:777
  161.4 11.5 %collective-permute-start.41 = (bf16[4,48,384]{2,1,0:T(8,128)(2,1)S(1)}, bf16[4,48,384]{2,1,0:T(8,128)(2,1)S(1)}, u32[]{:S(2)}, u32[]{:S(2)}) collective-permute-start(bf16[4,48,384]{2,1,0:T(8,128)(2,1)S(1)} %get-tuple-element.463), channel_id=1, source_target_pairs={{0,4},{4,0},{8,12},{12,8},{16,20},{20,16},{24,28},{28,24},{1,5},{5... | collective-permute-start | bytes 442376 | tf_op jit(solution)/shard_map/ppermute | solution.py:777
  162.1 10.8 %collective-permute-start.42 = (bf16[4,48,384]{2,1,0:T(8,128)(2,1)S(1)}, bf16[4,48,384]{2,1,0:T(8,128)(2,1)S(1)}, u32[]{:S(2)}, u32[]{:S(2)}) collective-permute-start(bf16[4,48,384]{2,1,0:T(8,128)(2,1)S(1)} %get-tuple-element.464), channel_id=1, source_target_pairs={{0,2},{1,3},{2,0},{3,1},{4,6},{5,7},{6,4},{7,5},{8,10},{9,11},{10,... | collective-permute-start | bytes 442376 | tf_op jit(solution)/shard_map/ppermute | solution.py:777
  163.4 10.3 %collective-permute-start.46 = (bf16[8,48,256]{2,1,0:T(8,128)(2,1)S(1)}, bf16[8,48,256]{2,1,0:T(8,128)(2,1)S(1)}, u32[]{:S(2)}, u32[]{:S(2)}) collective-permute-start(bf16[8,48,256]{2,1,0:T(8,128)(2,1)S(1)} %get-tuple-element.476), channel_id=1, source_target_pairs={{0,2},{1,3},{2,0},{3,1},{4,6},{5,7},{6,4},{7,5},{8,10},{9,11},{10,... | collective-permute-start | bytes 589832 | tf_op jit(solution)/shard_map/ppermute | solution.py:777
  (70 other events, 993.5 us)
where the time goes:
time: 210 us; the launch traced here: 206 us
  Pallas kernels  93.3 us (44%)
  starting transfers between devices  52.7 us (25%)
  waiting for transfers between devices  42.4 us (20%)
  blocking collectives  10.8 us (5%)
  local copies, waits for them, and re-layouts  3.05 us (1%)
    pallas_call x9, Pallas kernels, call(): pl.pallas_call(kernel, grid=(groups,), in_specs=[spec for spec, _ in ins....  76.4 us
    ppermute x54, starting transfers between devices, exchange(): return lax.ppermute(array, axis, [(i, i ^ 1 << bit) for i in range(size)])  52.7 us
    ppermute x54, waiting for transfers between devices, exchange(): return lax.ppermute(array, axis, [(i, i ^ 1 << bit) for i in range(size)])  42.4 us
    pallas_call x24, Pallas kernels, small_call(): pl.pallas_call(kernel, grid=(1,) if stream else (), out_shape=[jax.ShapeD...  16.9 us
    all_to_all x1, blocking collectives, per_device(): message = lax.all_to_all(message, ('win', 'ch'), 0, 0, tiled=True)  10.8 us
  transfers between devices with their start and end apart: 54, of which 16 were waited for; matrix products, arithmetic and copies ran while one was open for 2% of the time, Pallas kernels for 34%

commit v1 on v0

--- a/solution.py
+++ b/solution.py
@@ -501,7 +501,7 @@
     normed, middle = forward_attention(
         flat(k.field).astype(F32), group_sizes(k, plan.group), k.w_qkv, k.w_proj, k.perm, k.perm_t,
         k.row_limit, k.col_limit, k.bias, small, qkv_bias, k.qkv, k.prob, k.windowed,
-        k.mixed, k.attended, plan.layer > 0,
+        k.mixed, k.attended, False,
     )
     put_rows(k.normed, normed)
     put_rows(k.middle, middle)
@@ -626,14 +626,14 @@
         wait_all(k.w_head, k.load_sem.at[3])
 
     clear(k.row_sums, k.up_rows, k.final_rows, k.head_rows, k.loss, k.pooled_all, k.logit_all)
-    middle = flat(k.middle)
+    middle = rows_in(k, "middle")
     mlp_in, result = forward_mlp(
         middle, k.w_up, k.w_down, small_rows(k, plan), up_bias_row(k, plan), k.active_all.at[place], k.slope
     )
     k.mlp_all[place, :] = mlp_in
     grad = head_pass(k, plan, result, group_sizes(k), total_images)
     put_rows(k.grad_mid, backward_mlp(
-        grad, flat(k.middle), k.slope, k.w_up, k.w_down, small_rows(k, plan), k.low_all, k.pre_all,
+        grad, rows_in(k, "middle"), k.slope, k.w_up, k.w_down, small_rows(k, plan), k.low_all, k.pre_all,
         k.row_sums, k.up_rows, place,
     ))
 
@@ -654,7 +654,7 @@
     k.mlp_all[place, :] = flat(k.mlp_in)
     k.active_all[place, :] = flat(k.active)
     put_rows(k.grad_mid, backward_mlp(
-        flat(k.grad), rows_in(k, "middle"), k.slope, k.w_up, k.w_down, small_rows(k, plan), k.low_all, k.pre_all,
+        rows_in(k, "grad"), rows_in(k, "middle"), k.slope, k.w_up, k.w_down, small_rows(k, plan), k.low_all, k.pre_all,
         k.row_sums, k.up_rows, place,
     ))
 
@@ -765,7 +765,7 @@
         compiler_params=pltpu.CompilerParams(
             dimension_semantics=("arbitrary",), vmem_limit_bytes=VMEM_LIMIT
         ),
-        cost_estimate=pl.CostEstimate(flops=int(flops), bytes_accessed=int(moved), transcendentals=0),
+        cost_estimate=pl.CostEstimate(flops=int(8 * flops), bytes_accessed=int(moved), transcendentals=0),
         name=name,
     )(*[array for _, array in ins.values()])
     return dict(zip(outs, results))
@@ -1451,18 +1451,22 @@
     got = [exchange(part.array, core) for part in held[1]]
     result0, *got = tie(result0, *got)
     other.append(got)
+
     if staged:
-        result0, late1 = arrive(6, result0, moves[1:])
-        result0 = wait_for(result0, *late1)
-        late_got = [exchange(part.array, core) for part in late1]
-
-    saved1 = attention_forward(1, result0)
-    if staged:
-        saved1["middle"], *late_got = tie(saved1["middle"], *late_got)
+        early1 = attention_forward(1, result0, 0, groups - 1)
+        early1["proj_out"], late1 = arrive(6, early1["proj_out"], moves[1:])
+        early1["proj_out"] = wait_for(early1["proj_out"], *late1)
+        got = [exchange(part.array, core) for part in late1]
+        saved1 = attention_forward(1, result0, groups - 1, 1, early1)
+        saved1["middle"], *got = tie(saved1["middle"], *got)
         held[1] = held[1] + late1
-        other[1] = other[1] + late_got
+        other[1] = other[1] + got
+        middle1 = [early1["middle"], saved1["middle"]]
+    else:
+        saved1 = early1 = attention_forward(1, result0)
+        middle1 = [saved1["middle"]]
     ins, plan = weight_inputs(1, ["down", "up", "head"])
-    ins["middle"] = given(wide, saved1["middle"])
+    ins.update(rows_of("middle", middle1))
     ins["vec"] = (whole(vectors.shape), vectors)
     ins["rows"] = (SCALARS, valid_rows)
     ins["cols"] = (SCALARS, valid_cols)
@@ -1521,7 +1525,7 @@
         }
         need_grad = l > 0
         if need_grad:
-            outs["grad"] = wide
+            outs["grad"] = (wide[0], (count * GROUP, ROWS, C), F32)
         if store:
             if collect is None:
                 outs.update(grad_outputs(plan, a=["attn"]))
@@ -1553,7 +1557,16 @@
     x1, y1 = chain_of(last, "x", "up", "head"), chain_of(last, "y", "down")
     if regular:
         start(x1, y1)
-    back1 = attention_backward(1, last["grad_mid"], mlp0["result"], saved1, 0, groups)
+    grad_mid = last["grad_mid"]
+    before1 = attention_backward(1, grad_mid, mlp0["result"], early1, 0, groups - 1, store=False)
+    if regular:
+        before1["row_sums"] = meet(before1["row_sums"], x1, y1)
+        x1, y1 = combine([[x1], [y1]], me, "sum0")
+        grad_mid = after(grad_mid, x1, y1)
+        start(x1, y1)
+    back1 = attention_backward(
+        1, grad_mid, mlp0["result"], saved1, groups - 1, 1, before1, early1
+    )
     a1 = chain_of(back1, "a", "attn")
     grad = back1["grad"]
     if regular:
@@ -1568,7 +1581,7 @@
         "w_down": (whole((C, HID)), mlp0["down_out"]),
         "w_up": (whole((C, HID)), mlp0["up_out"]),
     }
-    ins["grad"] = given(wide, grad)
+    ins.update(rows_of("grad", [before1["grad"], grad]))
     ins.update(rows_of("middle", middle0))
     ins["mlp_in"] = given(thin, mlp0["mlp_in"])
     ins["active"] = given(hidden, mlp0["active"])
@@ -1583,13 +1596,13 @@
     grad_mid = first["grad_mid"]
     if regular:
         grad_mid = meet(grad_mid, x1, y1, a1)
-        x1, y1, a1 = combine([[x1], [y1], [a1]], me, "sum2")
-        grad_mid = after(grad_mid, x1, y1, a1)
-        start(x1, y1, a1, x0, y0)
+        a1, z1 = combine([[a1], [x1, y1]], me, "sum2")
+        grad_mid = after(grad_mid, a1, z1)
+        start(a1, z1, x0, y0)
     before0 = attention_backward(0, grad_mid, padded, early0, 0, groups - 1, store=False)
     if regular:
-        before0["row_sums"] = meet(before0["row_sums"], a1, x0, y0, x1, y1)
-        a1, x0, y0, z1 = combine([[a1], [x0], [y0], [x1, y1]], me, "sum3")
+        before0["row_sums"] = meet(before0["row_sums"], a1, x0, y0, z1)
+        a1, x0, y0, z1 = combine([[a1], [x0], [y0], [z1]], me, "sum3")
         grad_mid = after(grad_mid, a1, x0, y0, z1)
         start(a1, x0, y0, z1)
     small_parts = None
@@ -1614,12 +1627,11 @@
 
     if regular:
         start(a0, b0)
-        z1, x0, y0 = combine([[z1], [x0], [y0]], me, "sum5")
-        start(z1, x0, y0)
+        x0, y0 = combine([[x0], [y0]], me, "sum5")
+        start(x0, y0)
         a0.received, b0.received, x0.keep = tie(a0.received, b0.received, x0.keep)
         a0, b0 = combine([[a0], [b0]], me, "sum6")
         start(a0, b0)
-        x0.received, y0.received, z1.received = tie(x0.received, y0.received, z1.received)
         (z0,) = combine([[x0, y0, a1]], me, "sum7")
         start(z0)
         a0, b0 = combine([[a0], [b0]], me, "sum8")

time: 210 us -> 204 us (0.971)
  waiting for transfers between devices: 42.4 us -> 36.9 us
  Pallas kernels: 93.3 us -> 95.5 us
    ppermute x54, waiting for transfers between devices: 42.4 us -> 36.9 us  [exchange(): return lax.ppermute(array, axis, [(i, i ^ 1 << bit) for i in range(size)])]
    pallas_call x9 -> x11, Pallas kernels: 76.4 us -> 78 us  [call(): pl.pallas_call(kernel, grid=(groups,), in_specs=[spec for spec, _ in ins....]
    pallas_call x24 -> x25, Pallas kernels: 16.9 us -> 17.5 us  [small_call(): pl.pallas_call(kernel, grid=(1,) if stream else (), out_shape=[jax.ShapeD...]
  transfers between devices with their start and end apart: 54 -> 54, of which waited for: 16 -> 16; matrix products, arithmetic and copies ran while one was open for 2% -> 2% of each run, Pallas kernels for 34% -> 36%
where the time goes in v1:
time: 204 us; the launch traced here: 201 us
  Pallas kernels  95.5 us (47%)
  starting transfers between devices  51.1 us (25%)
  waiting for transfers between devices  36.9 us (18%)
  blocking collectives  10.1 us (5%)
  local copies, waits for them, and re-layouts  3.03 us (1%)
    pallas_call x11, Pallas kernels, call(): pl.pallas_call(kernel, grid=(groups,), in_specs=[spec for spec, _ in ins....  78 us
    ppermute x54, starting transfers between devices, exchange(): return lax.ppermute(array, axis, [(i, i ^ 1 << bit) for i in range(size)])  51.1 us
    ppermute x54, waiting for transfers between devices, exchange(): return lax.ppermute(array, axis, [(i, i ^ 1 << bit) for i in range(size)])  36.9 us
    pallas_call x25, Pallas kernels, small_call(): pl.pallas_call(kernel, grid=(1,) if stream else (), out_shape=[jax.ShapeD...  17.5 us
    all_to_all x1, blocking collectives, per_device(): message = lax.all_to_all(message, ('win', 'ch'), 0, 0, tiled=True)  10.1 us
  transfers between devices with their start and end apart: 54, of which 16 were waited for; matrix products, arithmetic and copies ran while one was open for 2% of the time, Pallas kernels for 36%

profile of v1, /device:TPU:0, one launch (start us, length us, event | category | flops | bytes accessed | tf_op | source)
XLA Modules:
  0.0 200.5 jit_solution(13171301719453566465)
XLA Ops:
  2.5 4.0 %collective-permute-start = (bf16[1,48,384]{2,1,0:T(8,128)(2,1)}, bf16[1,48,384]{2,1,0:T(8,128)(2,1)S(1)}, u32[]{:S(2)}, u32[]{:S(2)}) collective-permute-start(bf16[1,48,384]{2,1,0:T(8,128)(2,1)} %bitcast.77), channel_id=1, source_target_pairs={{0,16},{4,20},{8,24},{12,28},{16,0},{20,4},{24,8},{28,12},{1,17},{... | collective-permute-start | bytes 110600 | tf_op jit(solution)/shard_map/ppermute | solution.py:777
  12.0 2.0 %collective-permute-start.2 = (bf16[1,48,768]{2,1,0:T(8,128)(2,1)S(1)}, bf16[1,48,768]{2,1,0:T(8,128)(2,1)S(1)}, u32[]{:S(2)}, u32[]{:S(2)}) collective-permute-start(bf16[1,48,768]{2,1,0:T(8,128)(2,1)S(1)} %bitcast.75), channel_id=1, source_target_pairs={{0,16},{4,20},{8,24},{12,28},{16,0},{20,4},{24,8},{28,12},{1,17},{... | collective-permute-start | bytes 221192 | tf_op jit(solution)/shard_map/ppermute | solution.py:777
  15.5 2.5 %collective-permute-done.2.refs_3_ = bf16[1,48,768]{2,1,0:T(8,128)(2,1)S(1)} collective-permute-done((bf16[1,48,768]{2,1,0:T(8,128)(2,1)S(1)}, bf16[1,48,768]{2,1,0:T(8,128)(2,1)S(1)}, u32[]{:S(2)}, u32[]{:S(2)}) %collective-permute-start.2) | collective-permute-done | bytes 73760 | tf_op jit(solution)/shard_map/ppermute | solution.py:777
  23.2 3.0 %collective-permute-done.8.refs_1_ = bf16[1,48,1408]{2,1,0:T(8,128)(2,1)S(1)} collective-permute-done((bf16[1,48,1408]{2,1,0:T(8,128)(2,1)S(1)}, bf16[1,48,1408]{2,1,0:T(8,128)(2,1)S(1)}, u32[]{:S(2)}, u32[]{:S(2)}) %collective-permute-start.8) | collective-permute-done | bytes 135200 | tf_op jit(solution)/shard_map/ppermute | solution.py:777
  32.3 4.2 %collective-permute-done.7.refs_3_ = bf16[8,48,128]{2,1,0:T(8,128)(2,1)S(1)} collective-permute-done((bf16[8,48,128]{2,1,0:T(8,128)(2,1)S(1)}, bf16[8,48,128]{2,1,0:T(8,128)(2,1)S(1)}, u32[]{:S(2)}, u32[]{:S(2)}) %collective-permute-start.7) | collective-permute-done | bytes 98336 | tf_op jit(solution)/shard_map/ppermute | solution.py:777
  43.8 6.6 %attention_forward0_0.1 = (f32[2,208,384]{2,1,0:T(8,128)S(1)}, bf16[2,208,384]{2,1,0:T(8,128)(2,1)S(1)}, bf16[2,256,1152]{2,1,0:T(8,128)(2,1)S(1)}, bf16[2,4,3,6...) custom-call(bf16[2,384,256]{2,1,0:T(8,128)(2,1)S(1)} %bitcast.97, ...), custom_call_target="tpu_custom_call" | custom-call | flops 7851737088 | bytes 2731560 | tf_op jit(solution)/shard_map/attention_forward0_0/pallas_call | solution.py:758
  50.8 2.3 %collective-permute-done.18.refs_9_ = bf16[4,48,384]{2,1,0:T(8,128)(2,1)S(1)} collective-permute-done((bf16[4,48,384]{2,1,0:T(8,128)(2,1)S(1)}, bf16[4,48,384]{2,1,0:T(8,128)(2,1)S(1)}, u32[]{:S(2)}, u32[]{:S(2)}) %collective-permute-start.18) | collective-permute-done | bytes 147488 | tf_op jit(solution)/shard_map/ppermute | solution.py:777
  57.7 5.2 %attention_forward0_1.1 = (f32[2,208,384]{2,1,0:T(8,128)S(1)}, bf16[2,208,384]{2,1,0:T(8,128)(2,1)S(1)}, bf16[2,256,1152]{2,1,0:T(8,128)(2,1)S(1)}, bf16[2,4,3,6...) custom-call(bf16[4,208,384]{2,1,0:T(8,128)(2,1)S(1)} %pad.4.refs_5_.refs_0_.refs_7_, bf16[256,208]{1,0:T(8,128)(2,1)S(1)} %copy-done.29, ...), custom_call_target="tpu_custom_call" | custom-call | flops 7851737088 | bytes 2731552 | tf_op jit(solution)/shard_map/attention_forward0_1/pallas_call | solution.py:758
  64.6 6.0 %first_mlp.1 = (f32[4,208,384]{2,1,0:T(8,128)S(1)}, bf16[4,208,384]{2,1,0:T(8,128)(2,1)S(1)}, bf16[4,208,1536]{2,1,0:T(8,128)(2,1)S(1)}, bf16[4,208,1536]{2,1,0:...) custom-call(bf16[2,384,384]{2,1,0:T(8,128)(2,1)S(1)} %bitcast.87, ...), custom_call_target="tpu_custom_call" | custom-call | flops 15703474176 | bytes 3681800 | tf_op jit(solution)/shard_map/first_mlp/pallas_call | solution.py:758
  70.6 6.4 %attention_forward1_0.1 = (f32[2,208,384]{2,1,0:T(8,128)S(1)}, bf16[2,208,384]{2,1,0:T(8,128)(2,1)S(1)}, bf16[2,256,1152]{2,1,0:T(8,128)(2,1)S(1)}, bf16[2,4,3,6...) custom-call(bf16[2,384,384]{2,1,0:T(8,128)(2,1)S(1)} %bitcast.60, ...), custom_call_target="tpu_custom_call" | custom-call | flops 7851737088 | bytes 3370536 | tf_op jit(solution)/shard_map/attention_forward1_0/pallas_call | solution.py:758
  78.3 5.2 %attention_forward1_1.1 = (f32[2,208,384]{2,1,0:T(8,128)S(1)}, bf16[2,208,384]{2,1,0:T(8,128)(2,1)S(1)}, bf16[2,256,1152]{2,1,0:T(8,128)(2,1)S(1)}, bf16[2,4,3,6...) custom-call(f32[4,208,384]{2,1,0:T(8,128)S(1)} %get-tuple-element.359.refs_3_.refs_0_.refs_7_, ...), custom_call_target="tpu_custom_call" | custom-call | flops 7851737088 | bytes 3370528 | tf_op jit(solution)/shard_map/attention_forward1_1/pallas_call | solution.py:758
  83.6 14.8 %last_mlp.1 = (f32[4,208,384]{2,1,0:T(8,128)S(1)}, f32[8,384]{1,0:T(8,128)S(1)}, f32[1,1536]{1,0:T(1,128)S(1)}, f32[2,384]{1,0:T(2,128)S(1)}, f32[1,1024]{1,0:T(...) custom-call(bf16[2,384,640]{2,1,0:T(8,128)(2,1)S(1)} %bitcast.81, ...), custom_call_target="tpu_custom_call" | custom-call | flops 47110422528 | bytes 4470472 | tf_op jit(solution)/shard_map/last_mlp/pallas_call | solution.py:758
  99.0 5.3 %attention_backward1_0.1 = (f32[8,384]{1,0:T(8,128)S(1)}, f32[1,1152]{1,0:T(1,128)S(1)}, f32[3,64,256]{2,1,0:T(8,128)S(1)}, f32[2,208,384]{2,1,0:T(8,128)S(1)}, ...) custom-call(s32[2]{0:T(128)S(1)} %pad_add_fusion.me_ref.refs_4_.refs_2_.refs_0_, ...), custom_call_target="tpu_custom_call" | custom-call | flops 15703474176 | bytes 5959176 | tf_op jit(solution)/shard_map/attention_backward1_0/pallas_call | solution.py:758
  108.1 6.9 %attention_backward1_1.1 = (f32[8,384]{1,0:T(8,128)S(1)}, f32[1,1152]{1,0:T(1,128)S(1)}, f32[3,64,256]{2,1,0:T(8,128)S(1)}, f32[2,208,384]{2,1,0:T(8,128)S(1)}, ...) custom-call(s32[2]{0:T(128)S(1)} %pad_add_fusion.me_ref.refs_4_.refs_2_.refs_0_, ...), custom_call_target="tpu_custom_call" | custom-call | flops 15703474176 | bytes 8728584 | tf_op jit(solution)/shard_map/attention_backward1_1/pallas_call | solution.py:758
  115.1 4.8 %collective-permute-done.29.refs_1_ = bf16[8,48,640]{2,1,0:T(8,128)(2,1)S(1)} collective-permute-done((bf16[8,48,640]{2,1,0:T(8,128)(2,1)S(1)}, bf16[8,48,640]{2,1,0:T(8,128)(2,1)S(1)}, u32[]{:S(2)}, u32[]{:S(2)}) %collective-permute-start.29) | collective-permute-done | bytes 491552 | tf_op jit(solution)/shard_map/ppermute | solution.py:777
  123.0 7.9 %mlp_backward0.1 = (f32[4,208,384]{2,1,0:T(8,128)S(1)}, f32[8,384]{1,0:T(8,128)S(1)}, f32[1,1536]{1,0:T(1,128)S(1)}, bf16[2,384,384]{2,1,0:T(8,128)(2,1)S(1)}, b...) custom-call(s32[2]{0:T(128)S(1)} %pad_add_fusion.me_ref.refs_4_.refs_2_.refs_0_, ...), custom_call_target="tpu_custom_call" | custom-call | flops 31406948352 | bytes 10710536 | tf_op jit(solution)/shard_map/mlp_backward0/pallas_call | solution.py:758
  134.3 5.1 %attention_backward0_0.1 = (f32[8,384]{1,0:T(8,128)S(1)}, f32[1,1152]{1,0:T(1,128)S(1)}, f32[3,64,256]{2,1,0:T(8,128)S(1)}, bf16[416,1152]{1,0:T(8,128)(2,1)S(1)}, bf16[416,384]{1,0:T(8,128)(2,1)S(1)}) custom-call(s32[2]{0:T(128)S(1)} %pad_add_fusion.me_ref.refs_4_.refs_2_.refs_0_, bf16[384,1152]{1,0:T(8,128)(2,1)S(1)} %get-tuple-element.342.refs_9_.refs_1_, ...), custom_call_target="tpu_custom_call" | custom-call | flops 15703474176 | bytes 5320200 | tf_op jit(solution)/shard_map/attention_backward0_0/pallas_call | solution.py:758
  139.4 3.1 %collective-permute-done.34.refs_1_ = bf16[8,48,384]{2,1,0:T(8,128)(2,1)S(1)} collective-permute-done((bf16[8,48,384]{2,1,0:T(8,128)(2,1)S(1)}, bf16[8,48,384]{2,1,0:T(8,128)(2,1)S(1)}, u32[]{:S(2)}, u32[]{:S(2)}) %collective-permute-start.34) | collective-permute-done | bytes 294944 | tf_op jit(solution)/shard_map/ppermute | solution.py:777
  147.6 8.6 %attention_backward0_1.1 = (f32[8,384]{1,0:T(8,128)}, f32[1,1152]{1,0:T(1,128)}, f32[3,64,256]{2,1,0:T(8,128)}, bf16[2,384,256]{2,1,0:T(8,128)(2,1)S(1)}, bf16[2...) custom-call(s32[2]{0:T(128)S(1)} %pad_add_fusion.me_ref.refs_4_.refs_2_.refs_0_, ...), custom_call_target="tpu_custom_call" | custom-call | flops 15703474176 | bytes 8347656 | tf_op jit(solution)/shard_map/attention_backward0_1/pallas_call | solution.py:758
  163.4 2.2 %collective-permute-done.51.refs_3_ = bf16[4,48,384]{2,1,0:T(8,128)(2,1)S(1)} collective-permute-done((bf16[4,48,384]{2,1,0:T(8,128)(2,1)S(1)}, bf16[4,48,384]{2,1,0:T(8,128)(2,1)S(1)}, u32[]{:S(2)}, u32[]{:S(2)}) %collective-permute-start.51) | collective-permute-done | bytes 147488 | tf_op jit(solution)/shard_map/ppermute | solution.py:777
  171.8 2.4 %collective-permute-done.46.refs_1_ = bf16[4,48,256]{2,1,0:T(8,128)(2,1)S(1)} collective-permute-done((bf16[4,48,256]{2,1,0:T(8,128)(2,1)S(1)}, bf16[4,48,256]{2,1,0:T(8,128)(2,1)S(1)}, u32[]{:S(2)}, u32[]{:S(2)}) %collective-permute-start.46) | collective-permute-done | bytes 98336 | tf_op jit(solution)/shard_map/ppermute | solution.py:777
  178.2 3.6 %collective-permute-done.48.refs_1_ = bf16[2,48,512]{2,1,0:T(8,128)(2,1)S(1)} collective-permute-done((bf16[2,48,512]{2,1,0:T(8,128)(2,1)S(1)}, bf16[2,48,512]{2,1,0:T(8,128)(2,1)S(1)}, u32[]{:S(2)}, u32[]{:S(2)}) %collective-permute-start.48) | collective-permute-done | bytes 98336 | tf_op jit(solution)/shard_map/ppermute | solution.py:777
  184.9 3.1 %collective-permute-done.49.received = bf16[1,48,512]{2,1,0:T(8,128)(2,1)S(1)} collective-permute-done((bf16[1,48,512]{2,1,0:T(8,128)(2,1)S(1)}, bf16[1,48,512]{2,1,0:T(8,128)(2,1)S(1)}, u32[]{:S(2)}, u32[]{:S(2)}) %collective-permute-start.49) | collective-permute-done | bytes 49184 | tf_op jit(solution)/shard_map/ppermute | solution.py:777
  188.3 10.1 %all_to_all.11 = f32[32,1,768]{2,1,0:T(1,128)S(1)} all-to-all(f32[32,1,768]{2,1,0:T(1,128)S(1)} %copy.69), channel_id=1, replica_groups=mesh['win'=8,'ch'=4] {'win','ch'}, dimensions={0} | all-to-all | bytes 196608 | tf_op jit(solution)/shard_map/all_to_all | solution.py:1677
  (214 shorter events, 73.1 us)
Async XLA Ops:
  18.5 8.3 %collective-permute-start.5 = (bf16[2,48,768]{2,1,0:T(8,128)(2,1)S(1)}, bf16[2,48,768]{2,1,0:T(8,128)(2,1)S(1)}, u32[]{:S(2)}, u32[]{:S(2)}) collective-permute-start(bf16[2,48,768]{2,1,0:T(8,128)(2,1)S(1)} %get-tuple-element.296.refs_4_), channel_id=1, source_target_pairs={{0,8},{4,12},{8,0},{12,4},{16,24},{20,28},{24,16},{28,20},{1,9},{5... | collective-permute-start | bytes 442376 | tf_op jit(solution)/shard_map/ppermute | solution.py:777
  27.5 9.0 %collective-permute-start.11 = (bf16[2,48,1408]{2,1,0:T(8,128)(2,1)S(1)}, bf16[2,48,1408]{2,1,0:T(8,128)(2,1)S(1)}, u32[]{:S(2)}, u32[]{:S(2)}) collective-permute-start(bf16[2,48,1408]{2,1,0:T(8,128)(2,1)S(1)} %stack10.1.refs_0_), channel_id=1, source_target_pairs={{0,8},{4,12},{8,0},{12,4},{16,24},{20,28},{24,16},{28,20},{1,9},{5... | collective-permute-start | bytes 811016 | tf_op jit(solution)/shard_map/ppermute | solution.py:777
  28.3 8.2 %collective-permute-start.6 = (bf16[8,48,256]{2,1,0:T(8,128)(2,1)S(1)}, bf16[8,48,256]{2,1,0:T(8,128)(2,1)S(1)}, u32[]{:S(2)}, u32[]{:S(2)}) collective-permute-start(bf16[8,48,256]{2,1,0:T(8,128)(2,1)S(1)} %get-tuple-element.300.refs_0_), channel_id=1, source_target_pairs={{0,2},{1,3},{2,0},{3,1},{4,6},{5,7},{6,4},{7,5},{8,10},{9,11},{10,... | collective-permute-start | bytes 589832 | tf_op jit(solution)/shard_map/ppermute | solution.py:777
  37.8 12.6 %collective-permute-start.14 = (bf16[8,48,384]{2,1,0:T(8,128)(2,1)S(1)}, bf16[8,48,384]{2,1,0:T(8,128)(2,1)S(1)}, u32[]{:S(2)}, u32[]{:S(2)}) collective-permute-start(bf16[8,48,384]{2,1,0:T(8,128)(2,1)S(1)} %get-tuple-element.325.refs_0_), channel_id=1, source_target_pairs={{0,4},{4,0},{8,12},{12,8},{16,20},{20,16},{24,28},{28,24},{1,5},{5... | collective-permute-start | bytes 884744 | tf_op jit(solution)/shard_map/ppermute | solution.py:777
  39.0 11.4 %collective-permute-start.15 = (bf16[8,48,384]{2,1,0:T(8,128)(2,1)S(1)}, bf16[8,48,384]{2,1,0:T(8,128)(2,1)S(1)}, u32[]{:S(2)}, u32[]{:S(2)}) collective-permute-start(bf16[8,48,384]{2,1,0:T(8,128)(2,1)S(1)} %get-tuple-element.326.refs_2_), channel_id=1, source_target_pairs={{0,2},{1,3},{2,0},{3,1},{4,6},{5,7},{6,4},{7,5},{8,10},{9,11},{10,... | collective-permute-start | bytes 884744 | tf_op jit(solution)/shard_map/ppermute | solution.py:777
  41.1 9.7 %collective-permute-start.16 = (bf16[4,48,384]{2,1,0:T(8,128)(2,1)S(1)}, bf16[4,48,384]{2,1,0:T(8,128)(2,1)S(1)}, u32[]{:S(2)}, u32[]{:S(2)}) collective-permute-start(bf16[4,48,384]{2,1,0:T(8,128)(2,1)S(1)} %get-tuple-element.327.refs_4_), channel_id=1, source_target_pairs={{0,4},{4,0},{8,12},{12,8},{16,20},{20,16},{24,28},{28,24},{1,5},{5... | collective-permute-start | bytes 442376 | tf_op jit(solution)/shard_map/ppermute | solution.py:777
  41.9 11.1 %collective-permute-start.18 = (bf16[4,48,384]{2,1,0:T(8,128)(2,1)S(1)}, bf16[4,48,384]{2,1,0:T(8,128)(2,1)S(1)}, u32[]{:S(2)}, u32[]{:S(2)}) collective-permute-start(bf16[4,48,384]{2,1,0:T(8,128)(2,1)S(1)} %get-tuple-element.329.refs_8_), channel_id=1, source_target_pairs={{0,4},{4,0},{8,12},{12,8},{16,20},{20,16},{24,28},{28,24},{1,5},{5... | collective-permute-start | bytes 442376 | tf_op jit(solution)/shard_map/ppermute | solution.py:777
  43.2 9.9 %collective-permute-start.17 = (bf16[4,48,640]{2,1,0:T(8,128)(2,1)S(1)}, bf16[4,48,640]{2,1,0:T(8,128)(2,1)S(1)}, u32[]{:S(2)}, u32[]{:S(2)}) collective-permute-start(bf16[4,48,640]{2,1,0:T(8,128)(2,1)S(1)} %get-tuple-element.328.refs_6_), channel_id=1, source_target_pairs={{0,2},{1,3},{2,0},{3,1},{4,6},{5,7},{6,4},{7,5},{8,10},{9,11},{10,... | collective-permute-start | bytes 737288 | tf_op jit(solution)/shard_map/ppermute | solution.py:777
  53.8 10.0 %collective-permute-start.21 = (bf16[8,48,384]{2,1,0:T(8,128)(2,1)S(1)}, bf16[8,48,384]{2,1,0:T(8,128)(2,1)S(1)}, u32[]{:S(2)}, u32[]{:S(2)}) collective-permute-start(bf16[8,48,384]{2,1,0:T(8,128)(2,1)S(1)} %get-tuple-element.350.refs_0_), channel_id=1, source_target_pairs={{0,2},{1,3},{2,0},{3,1},{4,6},{5,7},{6,4},{7,5},{8,10},{9,11},{10,... | collective-permute-start | bytes 884744 | tf_op jit(solution)/shard_map/ppermute | solution.py:777
  55.4 21.6 %collective-permute-start.24 = (bf16[8,48,384]{2,1,0:T(8,128)(2,1)S(1)}, bf16[8,48,384]{2,1,0:T(8,128)(2,1)S(1)}, u32[]{:S(2)}, u32[]{:S(2)}) collective-permute-start(bf16[8,48,384]{2,1,0:T(8,128)(2,1)S(1)} %get-tuple-element.363.refs_2_), channel_id=1, source_target_pairs={{0,2},{1,3},{2,0},{3,1},{4,6},{5,7},{6,4},{7,5},{8,10},{9,11},{10,... | collective-permute-start | bytes 884744 | tf_op jit(solution)/shard_map/ppermute | solution.py:777
  55.9 21.1 %collective-permute-start.23 = (bf16[8,48,640]{2,1,0:T(8,128)(2,1)S(1)}, bf16[8,48,640]{2,1,0:T(8,128)(2,1)S(1)}, u32[]{:S(2)}, u32[]{:S(2)}) collective-permute-start(bf16[8,48,640]{2,1,0:T(8,128)(2,1)S(1)} %get-tuple-element.362.refs_0_), channel_id=1, source_target_pairs={{0,4},{4,0},{8,12},{12,8},{16,20},{20,16},{24,28},{28,24},{1,5},{5... | collective-permute-start | bytes 1474568 | tf_op jit(solution)/shard_map/ppermute | solution.py:777
  105.3 9.8 %collective-permute-start.30 = (bf16[8,48,384]{2,1,0:T(8,128)(2,1)S(1)}, bf16[8,48,384]{2,1,0:T(8,128)(2,1)S(1)}, u32[]{:S(2)}, u32[]{:S(2)}) collective-permute-start(bf16[8,48,384]{2,1,0:T(8,128)(2,1)S(1)} %get-tuple-element.406), channel_id=1, source_target_pairs={{0,4},{4,0},{8,12},{12,8},{16,20},{20,16},{24,28},{28,24},{1,5},{5... | collective-permute-start | bytes 884744 | tf_op jit(solution)/shard_map/ppermute | solution.py:777
  106.6 13.3 %collective-permute-start.29 = (bf16[8,48,640]{2,1,0:T(8,128)(2,1)S(1)}, bf16[8,48,640]{2,1,0:T(8,128)(2,1)S(1)}, u32[]{:S(2)}, u32[]{:S(2)}) collective-permute-start(bf16[8,48,640]{2,1,0:T(8,128)(2,1)S(1)} %get-tuple-element.405), channel_id=1, source_target_pairs={{0,2},{1,3},{2,0},{3,1},{4,6},{5,7},{6,4},{7,5},{8,10},{9,11},{10,... | collective-permute-start | bytes 1474568 | tf_op jit(solution)/shard_map/ppermute | solution.py:777
  115.0 16.4 %collective-permute-start.33 = (bf16[16,48,384]{2,1,0:T(8,128)(2,1)S(1)}, bf16[16,48,384]{2,1,0:T(8,128)(2,1)S(1)}, u32[]{:S(2)}, u32[]{:S(2)}) collective-permute-start(bf16[16,48,384]{2,1,0:T(8,128)(2,1)S(1)} %bitcast.84), channel_id=1, source_target_pairs={{0,1},{1,0},{2,3},{3,2},{4,5},{5,4},{6,7},{7,6},{8,9},{9,8},{10,11... | collective-permute-start | bytes 1769480 | tf_op jit(solution)/shard_map/ppermute | solution.py:777
  120.6 10.8 %collective-permute-start.32 = (bf16[4,48,384]{2,1,0:T(8,128)(2,1)S(1)}, bf16[4,48,384]{2,1,0:T(8,128)(2,1)S(1)}, u32[]{:S(2)}, u32[]{:S(2)}) collective-permute-start(bf16[4,48,384]{2,1,0:T(8,128)(2,1)S(1)} %get-tuple-element.422), channel_id=1, source_target_pairs={{0,2},{1,3},{2,0},{3,1},{4,6},{5,7},{6,4},{7,5},{8,10},{9,11},{10,... | collective-permute-start | bytes 442376 | tf_op jit(solution)/shard_map/ppermute | solution.py:777
  122.2 9.3 %collective-permute-start.31 = (bf16[4,48,640]{2,1,0:T(8,128)(2,1)S(1)}, bf16[4,48,640]{2,1,0:T(8,128)(2,1)S(1)}, u32[]{:S(2)}, u32[]{:S(2)}) collective-permute-start(bf16[4,48,640]{2,1,0:T(8,128)(2,1)S(1)} %get-tuple-element.421), channel_id=1, source_target_pairs={{0,4},{4,0},{8,12},{12,8},{16,20},{20,16},{24,28},{28,24},{1,5},{5... | collective-permute-start | bytes 737288 | tf_op jit(solution)/shard_map/ppermute | solution.py:777
  130.9 11.6 %collective-permute-start.35 = (bf16[16,48,384]{2,1,0:T(8,128)(2,1)S(1)}, bf16[16,48,384]{2,1,0:T(8,128)(2,1)S(1)}, u32[]{:S(2)}, u32[]{:S(2)}) collective-permute-start(bf16[16,48,384]{2,1,0:T(8,128)(2,1)S(1)} %bitcast.86), channel_id=1, source_target_pairs={{0,1},{1,0},{2,3},{3,2},{4,5},{5,4},{6,7},{7,6},{8,9},{9,8},{10,11... | collective-permute-start | bytes 1769480 | tf_op jit(solution)/shard_map/ppermute | solution.py:777
  131.0 11.6 %collective-permute-start.36 = (bf16[16,48,384]{2,1,0:T(8,128)(2,1)S(1)}, bf16[16,48,384]{2,1,0:T(8,128)(2,1)S(1)}, u32[]{:S(2)}, u32[]{:S(2)}) collective-permute-start(bf16[16,48,384]{2,1,0:T(8,128)(2,1)S(1)} %bitcast.85), channel_id=1, source_target_pairs={{0,1},{1,0},{2,3},{3,2},{4,5},{5,4},{6,7},{7,6},{8,9},{9,8},{10,11... | collective-permute-start | bytes 1769480 | tf_op jit(solution)/shard_map/ppermute | solution.py:777
  133.8 8.7 %collective-permute-start.34 = (bf16[8,48,384]{2,1,0:T(8,128)(2,1)S(1)}, bf16[8,48,384]{2,1,0:T(8,128)(2,1)S(1)}, u32[]{:S(2)}, u32[]{:S(2)}) collective-permute-start(bf16[8,48,384]{2,1,0:T(8,128)(2,1)S(1)} %get-tuple-element.440), channel_id=1, source_target_pairs={{0,2},{1,3},{2,0},{3,1},{4,6},{5,7},{6,4},{7,5},{8,10},{9,11},{10,... | collective-permute-start | bytes 884744 | tf_op jit(solution)/shard_map/ppermute | solution.py:777
  143.5 12.7 %collective-permute-start.41 = (bf16[1,48,1024]{2,1,0:T(8,128)(2,1)S(1)}, bf16[1,48,1024]{2,1,0:T(8,128)(2,1)S(1)}, u32[]{:S(2)}, u32[]{:S(2)}) collective-permute-start(bf16[1,48,1024]{2,1,0:T(8,128)(2,1)S(1)} %get-tuple-element.487), channel_id=1, source_target_pairs={{0,16},{4,20},{8,24},{12,28},{16,0},{20,4},{24,8},{28,12},{1,17},{... | collective-permute-start | bytes 294920 | tf_op jit(solution)/shard_map/ppermute | solution.py:777
  145.0 11.2 %collective-permute-start.38 = (bf16[4,48,384]{2,1,0:T(8,128)(2,1)S(1)}, bf16[4,48,384]{2,1,0:T(8,128)(2,1)S(1)}, u32[]{:S(2)}, u32[]{:S(2)}) collective-permute-start(bf16[4,48,384]{2,1,0:T(8,128)(2,1)S(1)} %get-tuple-element.484), channel_id=1, source_target_pairs={{0,4},{4,0},{8,12},{12,8},{16,20},{20,16},{24,28},{28,24},{1,5},{5... | collective-permute-start | bytes 442376 | tf_op jit(solution)/shard_map/ppermute | solution.py:777
  146.4 9.8 %collective-permute-start.39 = (bf16[8,48,384]{2,1,0:T(8,128)(2,1)S(1)}, bf16[8,48,384]{2,1,0:T(8,128)(2,1)S(1)}, u32[]{:S(2)}, u32[]{:S(2)}) collective-permute-start(bf16[8,48,384]{2,1,0:T(8,128)(2,1)S(1)} %get-tuple-element.485), channel_id=1, source_target_pairs={{0,2},{1,3},{2,0},{3,1},{4,6},{5,7},{6,4},{7,5},{8,10},{9,11},{10,... | collective-permute-start | bytes 884744 | tf_op jit(solution)/shard_map/ppermute | solution.py:777
  146.9 9.3 %collective-permute-start.40 = (bf16[8,48,384]{2,1,0:T(8,128)(2,1)S(1)}, bf16[8,48,384]{2,1,0:T(8,128)(2,1)S(1)}, u32[]{:S(2)}, u32[]{:S(2)}) collective-permute-start(bf16[8,48,384]{2,1,0:T(8,128)(2,1)S(1)} %get-tuple-element.486), channel_id=1, source_target_pairs={{0,4},{4,0},{8,12},{12,8},{16,20},{20,16},{24,28},{28,24},{1,5},{5... | collective-permute-start | bytes 884744 | tf_op jit(solution)/shard_map/ppermute | solution.py:777
  166.3 11.0 %collective-permute-start.52 = (bf16[2,48,1152]{2,1,0:T(8,128)(2,1)S(1)}, bf16[2,48,1152]{2,1,0:T(8,128)(2,1)S(1)}, u32[]{:S(2)}, u32[]{:S(2)}) collective-permute-start(bf16[2,48,1152]{2,1,0:T(8,128)(2,1)S(1)} %get-tuple-element.520), channel_id=1, source_target_pairs={{0,8},{4,12},{8,0},{12,4},{16,24},{20,28},{24,16},{28,20},{1,9},{5... | collective-permute-start | bytes 663560 | tf_op jit(solution)/shard_map/ppermute | solution.py:777
  (70 other events, 932.4 us)

commit v2 on v1

--- a/solution.py
+++ b/solution.py
@@ -157,10 +157,14 @@
     pltpu.make_async_copy(ref, ref, sem).wait()
 
 
+def sem_of(sems, number):
+    return sems[number] if isinstance(sems, list) else sems.at[number]
+
+
 def store_blocks(source, outs, width, sems, me_ref):
     for number, (ref, owners, start, source_start, size) in enumerate(outs):
         if owners is None:
-            copy = pltpu.make_async_copy(source, ref, sems.at[number])
+            copy = pltpu.make_async_copy(source, ref, sem_of(sems, number))
             copy.start()
             copy.wait()
             continue
@@ -168,7 +172,7 @@
             pltpu.make_async_copy(
                 owner_part(source, me_ref[1] ^ owner, width, source_start, size),
                 ref.at[n, :, start : start + size],
-                sems.at[number],
+                sem_of(sems, number),
             ).start()
 
 
@@ -501,7 +505,7 @@
     normed, middle = forward_attention(
         flat(k.field).astype(F32), group_sizes(k, plan.group), k.w_qkv, k.w_proj, k.perm, k.perm_t,
         k.row_limit, k.col_limit, k.bias, small, qkv_bias, k.qkv, k.prob, k.windowed,
-        k.mixed, k.attended, False,
+        k.mixed, k.attended, True,
     )
     put_rows(k.normed, normed)
     put_rows(k.middle, middle)
@@ -644,7 +648,10 @@
         owners, _, width = k.head_grad.shape
         for n in range(owners):
             k.head_grad[n] = total[:, n * width : (n + 1) * width]
-        store_blocks(k.head_grad, plan.outs(k, "head"), plan.widths["head"], k.sem_x, k.me)
+        store_blocks(
+            k.head_grad, plan.outs(k, "head"), plan.widths["head"],
+            [k.sem_x.at[0], k.sem_x.at[1], k.sem_y.at[0], k.sem_y.at[1]], k.me,
+        )
         wait_mlp_grads(k, plan)
 
 
@@ -986,8 +993,11 @@
         put(3, l, own[part][:, at : at + widths["down"]], LEARN_RATE)
         heads = table_rows // layers
         put(6, l, table_grad[l * heads : (l + 1) * heads], SMALL_RATE)
-    part, at = starts[-1]["head"]
-    put(4, None, own[part][:, at : at + outs[4][0].shape[1]], LEARN_RATE)
+    half = widths["head"] // 2
+    head_grad = jnp.concatenate(
+        [own[part][:, at : at + half] for part, at in starts[-1]["head"]], 1
+    )
+    put(4, None, head_grad[:, : outs[4][0].shape[1]], LEARN_RATE)
     put(5, None, vector_grad, SMALL_RATE)
 
 
@@ -1282,13 +1292,30 @@
                 )
         return outs
 
+    def halved_head_outputs(plan):
+        half = widths["head"] // 2
+        if not direct:
+            return grad_outputs(plan, x=["up", "head"], y=["down"])
+        outs, plan.targets["head"] = {}, []
+        for group, name, at in (("x", "up", 0), ("y", "down", half)):
+            plan.targets[name] = []
+            for kind, flip in (("keep", 0), ("send", 1)):
+                ref, places = f"{kind}_{group}", [owner ^ flip for owner in owners]
+                outs[ref] = (FAR, (len(owners), C, widths[name] + half), BF16)
+                plan.targets[name].append((ref, places, 0, 0, widths[name]))
+                plan.targets["head"].append((ref, places, widths[name], at, half))
+        return outs
+
     def chain_of(results, group, *members, pair_at=None):
         if direct:
             keep, send = results[f"keep_{group}"], results[f"send_{group}"]
         else:
             full = []
             for name in members:
+                name, *cut = name if isinstance(name, tuple) else (name,)
                 part = results[f"full_{name}"]
+                if cut:
+                    part = part[..., cut[0] : cut[1]]
                 if name in ("up", "down"):
                     part = part.reshape(C, ch_count, -1).transpose(1, 0, 2)
                 full.append(part)
@@ -1482,7 +1509,7 @@
         "final_rows": (whole((2, C)), (2, C), F32),
         "head_rows": (whole((1, head_classes)), (1, head_classes), F32),
         "loss": (whole((1, 128)), (1, 128), F32),
-        **grad_outputs(plan, x=["up", "head"], y=["down"]),
+        **halved_head_outputs(plan),
     }
     last = call(
         functools.partial(last_mlp_kernel, plan=plan, total_images=float(total_images)),
@@ -1554,7 +1581,9 @@
             2 * attn_flops * count // groups,
         )
 
-    x1, y1 = chain_of(last, "x", "up", "head"), chain_of(last, "y", "down")
+    half = widths["head"] // 2
+    x1 = chain_of(last, "x", "up", ("head", 0, half))
+    y1 = chain_of(last, "y", "down", ("head", half, 2 * half))
     if regular:
         start(x1, y1)
     grad_mid = last["grad_mid"]
@@ -1678,8 +1707,9 @@
     starts = [
         {"attn": (1, 0), "up": (2, 0), "down": (2, widths["up"])},
         {
-            "attn": (2, widths["up"] + widths["down"]), "up": (0, 0), "head": (0, widths["up"]),
-            "down": (0, widths["up"] + widths["head"]),
+            "attn": (2, widths["up"] + widths["down"]), "up": (0, 0),
+            "down": (0, widths["up"] + half),
+            "head": [(0, widths["up"]), (0, widths["up"] + half + widths["down"])],
         },
     ]
     arrays = [

time: 204 us -> 202 us (level)
  transfers between devices with their start and end apart: 54 -> 54, of which waited for: 16 -> 17; matrix products, arithmetic and copies ran while one was open for 2% -> 2% of each run, Pallas kernels for 36% -> 35%
where the time goes in v2:
time: 202 us; the launch traced here: 198 us
  Pallas kernels  93.9 us (46%)
  starting transfers between devices  52.3 us (26%)
  waiting for transfers between devices  35.5 us (18%)
  blocking collectives  9.51 us (5%)
  local copies, waits for them, and re-layouts  3.03 us (2%)
  between operations  2.05 us (1%)
    pallas_call x11, Pallas kernels, call(): pl.pallas_call(kernel, grid=(groups,), in_specs=[spec for spec, _ in ins....  76.5 us
    ppermute x54, starting transfers between devices, exchange(): return lax.ppermute(array, axis, [(i, i ^ 1 << bit) for i in range(size)])  52.3 us
    ppermute x54, waiting for transfers between devices, exchange(): return lax.ppermute(array, axis, [(i, i ^ 1 << bit) for i in range(size)])  35.5 us
    pallas_call x25, Pallas kernels, small_call(): pl.pallas_call(kernel, grid=(1,) if stream else (), out_shape=[jax.ShapeD...  17.4 us
    all_to_all x1, blocking collectives, per_device(): message = lax.all_to_all(message, ('win', 'ch'), 0, 0, tiled=True)  9.51 us
  transfers between devices with their start and end apart: 54, of which 17 were waited for; matrix products, arithmetic and copies ran while one was open for 2% of the time, Pallas kernels for 35%

profile of v2, /device:TPU:0, one launch (start us, length us, event | category | flops | bytes accessed | tf_op | source)
XLA Modules:
  0.0 198.2 jit_solution(5908139748861882210)
XLA Ops:
  0.7 1.8 pack.1
  2.5 4.0 %collective-permute-start = (bf16[1,48,384]{2,1,0:T(8,128)(2,1)}, bf16[1,48,384]{2,1,0:T(8,128)(2,1)S(1)}, u32[]{:S(2)}, u32[]{:S(2)}) collective-permute-start(bf16[1,48,384]{2,1,0:T(8,128)(2,1)} %bitcast.77), channel_id=1, source_target_pairs={{0,16},{4,20},{8,24},{12,28},{16,0},{20,4},{24,8},{28,12},{1,17},{... | collective-permute-start | bytes 110600 | tf_op jit(solution)/shard_map/ppermute | solution.py:784
  12.0 2.0 %collective-permute-start.2 = (bf16[1,48,768]{2,1,0:T(8,128)(2,1)S(1)}, bf16[1,48,768]{2,1,0:T(8,128)(2,1)S(1)}, u32[]{:S(2)}, u32[]{:S(2)}) collective-permute-start(bf16[1,48,768]{2,1,0:T(8,128)(2,1)S(1)} %bitcast.75), channel_id=1, source_target_pairs={{0,16},{4,20},{8,24},{12,28},{16,0},{20,4},{24,8},{28,12},{1,17},{... | collective-permute-start | bytes 221192 | tf_op jit(solution)/shard_map/ppermute | solution.py:784
  15.5 2.5 %collective-permute-done.2.refs_3_ = bf16[1,48,768]{2,1,0:T(8,128)(2,1)S(1)} collective-permute-done((bf16[1,48,768]{2,1,0:T(8,128)(2,1)S(1)}, bf16[1,48,768]{2,1,0:T(8,128)(2,1)S(1)}, u32[]{:S(2)}, u32[]{:S(2)}) %collective-permute-start.2) | collective-permute-done | bytes 73760 | tf_op jit(solution)/shard_map/ppermute | solution.py:784
  23.2 3.0 %collective-permute-done.8.refs_1_ = bf16[1,48,1408]{2,1,0:T(8,128)(2,1)S(1)} collective-permute-done((bf16[1,48,1408]{2,1,0:T(8,128)(2,1)S(1)}, bf16[1,48,1408]{2,1,0:T(8,128)(2,1)S(1)}, u32[]{:S(2)}, u32[]{:S(2)}) %collective-permute-start.8) | collective-permute-done | bytes 135200 | tf_op jit(solution)/shard_map/ppermute | solution.py:784
  32.3 4.2 %collective-permute-done.7.refs_3_ = bf16[8,48,128]{2,1,0:T(8,128)(2,1)S(1)} collective-permute-done((bf16[8,48,128]{2,1,0:T(8,128)(2,1)S(1)}, bf16[8,48,128]{2,1,0:T(8,128)(2,1)S(1)}, u32[]{:S(2)}, u32[]{:S(2)}) %collective-permute-start.7) | collective-permute-done | bytes 98336 | tf_op jit(solution)/shard_map/ppermute | solution.py:784
  43.8 5.8 %attention_forward0_0.1 = (f32[2,208,384]{2,1,0:T(8,128)S(1)}, bf16[2,208,384]{2,1,0:T(8,128)(2,1)S(1)}, bf16[2,256,1152]{2,1,0:T(8,128)(2,1)S(1)}, bf16[2,4,3,6...) custom-call(bf16[2,384,256]{2,1,0:T(8,128)(2,1)S(1)} %bitcast.97, ...), custom_call_target="tpu_custom_call" | custom-call | flops 7851737088 | bytes 2731560 | tf_op jit(solution)/shard_map/attention_forward0_0/pallas_call | solution.py:765
  50.8 2.3 %collective-permute-done.18.refs_9_ = bf16[4,48,384]{2,1,0:T(8,128)(2,1)S(1)} collective-permute-done((bf16[4,48,384]{2,1,0:T(8,128)(2,1)S(1)}, bf16[4,48,384]{2,1,0:T(8,128)(2,1)S(1)}, u32[]{:S(2)}, u32[]{:S(2)}) %collective-permute-start.18) | collective-permute-done | bytes 147488 | tf_op jit(solution)/shard_map/ppermute | solution.py:784
  57.7 4.8 %attention_forward0_1.1 = (f32[2,208,384]{2,1,0:T(8,128)S(1)}, bf16[2,208,384]{2,1,0:T(8,128)(2,1)S(1)}, bf16[2,256,1152]{2,1,0:T(8,128)(2,1)S(1)}, bf16[2,4,3,6...) custom-call(bf16[4,208,384]{2,1,0:T(8,128)(2,1)S(1)} %pad.4.refs_5_.refs_0_.refs_7_, bf16[256,208]{1,0:T(8,128)(2,1)S(1)} %copy-done.29, ...), custom_call_target="tpu_custom_call" | custom-call | flops 7851737088 | bytes 2731552 | tf_op jit(solution)/shard_map/attention_forward0_1/pallas_call | solution.py:765
  64.6 6.0 %first_mlp.1 = (f32[4,208,384]{2,1,0:T(8,128)S(1)}, bf16[4,208,384]{2,1,0:T(8,128)(2,1)S(1)}, bf16[4,208,1536]{2,1,0:T(8,128)(2,1)S(1)}, bf16[4,208,1536]{2,1,0:...) custom-call(bf16[2,384,384]{2,1,0:T(8,128)(2,1)S(1)} %bitcast.88, ...), custom_call_target="tpu_custom_call" | custom-call | flops 15703474176 | bytes 3681800 | tf_op jit(solution)/shard_map/first_mlp/pallas_call | solution.py:765
  70.6 6.0 %attention_forward1_0.1 = (f32[2,208,384]{2,1,0:T(8,128)S(1)}, bf16[2,208,384]{2,1,0:T(8,128)(2,1)S(1)}, bf16[2,256,1152]{2,1,0:T(8,128)(2,1)S(1)}, bf16[2,4,3,6...) custom-call(bf16[2,384,384]{2,1,0:T(8,128)(2,1)S(1)} %bitcast.61, ...), custom_call_target="tpu_custom_call" | custom-call | flops 7851737088 | bytes 3370536 | tf_op jit(solution)/shard_map/attention_forward1_0/pallas_call | solution.py:765
  77.9 4.8 %attention_forward1_1.1 = (f32[2,208,384]{2,1,0:T(8,128)S(1)}, bf16[2,208,384]{2,1,0:T(8,128)(2,1)S(1)}, bf16[2,256,1152]{2,1,0:T(8,128)(2,1)S(1)}, bf16[2,4,3,6...) custom-call(f32[4,208,384]{2,1,0:T(8,128)S(1)} %get-tuple-element.359.refs_3_.refs_0_.refs_7_, ...), custom_call_target="tpu_custom_call" | custom-call | flops 7851737088 | bytes 3370528 | tf_op jit(solution)/shard_map/attention_forward1_1/pallas_call | solution.py:765
  82.8 15.3 %last_mlp.1 = (f32[4,208,384]{2,1,0:T(8,128)S(1)}, f32[8,384]{1,0:T(8,128)S(1)}, f32[1,1536]{1,0:T(1,128)S(1)}, f32[2,384]{1,0:T(2,128)S(1)}, f32[1,1024]{1,0:T(...) custom-call(bf16[2,384,640]{2,1,0:T(8,128)(2,1)S(1)} %bitcast.81, ...), custom_call_target="tpu_custom_call" | custom-call | flops 47110422528 | bytes 4470472 | tf_op jit(solution)/shard_map/last_mlp/pallas_call | solution.py:765
  98.7 5.3 %attention_backward1_0.1 = (f32[8,384]{1,0:T(8,128)S(1)}, f32[1,1152]{1,0:T(1,128)S(1)}, f32[3,64,256]{2,1,0:T(8,128)S(1)}, f32[2,208,384]{2,1,0:T(8,128)S(1)}, ...) custom-call(s32[2]{0:T(128)S(1)} %pad_add_fusion.me_ref.refs_4_.refs_2_.refs_0_, ...), custom_call_target="tpu_custom_call" | custom-call | flops 15703474176 | bytes 5959176 | tf_op jit(solution)/shard_map/attention_backward1_0/pallas_call | solution.py:765
  107.7 7.0 %attention_backward1_1.1 = (f32[8,384]{1,0:T(8,128)S(1)}, f32[1,1152]{1,0:T(1,128)S(1)}, f32[3,64,256]{2,1,0:T(8,128)S(1)}, f32[2,208,384]{2,1,0:T(8,128)S(1)}, ...) custom-call(s32[2]{0:T(128)S(1)} %pad_add_fusion.me_ref.refs_4_.refs_2_.refs_0_, ...), custom_call_target="tpu_custom_call" | custom-call | flops 15703474176 | bytes 8728584 | tf_op jit(solution)/shard_map/attention_backward1_1/pallas_call | solution.py:765
  120.3 7.8 %mlp_backward0.1 = (f32[4,208,384]{2,1,0:T(8,128)S(1)}, f32[8,384]{1,0:T(8,128)S(1)}, f32[1,1536]{1,0:T(1,128)S(1)}, bf16[2,384,384]{2,1,0:T(8,128)(2,1)S(1)}, b...) custom-call(s32[2]{0:T(128)S(1)} %pad_add_fusion.me_ref.refs_4_.refs_2_.refs_0_, ...), custom_call_target="tpu_custom_call" | custom-call | flops 31406948352 | bytes 10710536 | tf_op jit(solution)/shard_map/mlp_backward0/pallas_call | solution.py:765
  132.6 5.1 %attention_backward0_0.1 = (f32[8,384]{1,0:T(8,128)S(1)}, f32[1,1152]{1,0:T(1,128)S(1)}, f32[3,64,256]{2,1,0:T(8,128)S(1)}, bf16[416,1152]{1,0:T(8,128)(2,1)S(1)}, bf16[416,384]{1,0:T(8,128)(2,1)S(1)}) custom-call(s32[2]{0:T(128)S(1)} %pad_add_fusion.me_ref.refs_4_.refs_2_.refs_0_, bf16[384,1152]{1,0:T(8,128)(2,1)S(1)} %get-tuple-element.342.refs_9_.refs_1_, ...), custom_call_target="tpu_custom_call" | custom-call | flops 15703474176 | bytes 5320200 | tf_op jit(solution)/shard_map/attention_backward0_0/pallas_call | solution.py:765
  137.7 2.1 %collective-permute-done.34.refs_1_ = bf16[8,48,384]{2,1,0:T(8,128)(2,1)S(1)} collective-permute-done((bf16[8,48,384]{2,1,0:T(8,128)(2,1)S(1)}, bf16[8,48,384]{2,1,0:T(8,128)(2,1)S(1)}, u32[]{:S(2)}, u32[]{:S(2)}) %collective-permute-start.34) | collective-permute-done | bytes 294944 | tf_op jit(solution)/shard_map/ppermute | solution.py:784
  145.8 8.7 %attention_backward0_1.1 = (f32[8,384]{1,0:T(8,128)}, f32[1,1152]{1,0:T(1,128)}, f32[3,64,256]{2,1,0:T(8,128)}, bf16[2,384,256]{2,1,0:T(8,128)(2,1)S(1)}, bf16[2...) custom-call(s32[2]{0:T(128)S(1)} %pad_add_fusion.me_ref.refs_4_.refs_2_.refs_0_, ...), custom_call_target="tpu_custom_call" | custom-call | flops 15703474176 | bytes 8347656 | tf_op jit(solution)/shard_map/attention_backward0_1/pallas_call | solution.py:765
  169.2 2.7 %collective-permute-done.46.refs_1_ = bf16[4,48,256]{2,1,0:T(8,128)(2,1)S(1)} collective-permute-done((bf16[4,48,256]{2,1,0:T(8,128)(2,1)S(1)}, bf16[4,48,256]{2,1,0:T(8,128)(2,1)S(1)}, u32[]{:S(2)}, u32[]{:S(2)}) %collective-permute-start.46) | collective-permute-done | bytes 98336 | tf_op jit(solution)/shard_map/ppermute | solution.py:784
  176.5 3.7 %collective-permute-done.48.refs_1_ = bf16[2,48,512]{2,1,0:T(8,128)(2,1)S(1)} collective-permute-done((bf16[2,48,512]{2,1,0:T(8,128)(2,1)S(1)}, bf16[2,48,512]{2,1,0:T(8,128)(2,1)S(1)}, u32[]{:S(2)}, u32[]{:S(2)}) %collective-permute-start.48) | collective-permute-done | bytes 98336 | tf_op jit(solution)/shard_map/ppermute | solution.py:784
  181.1 2.2 %collective-permute-done.53.received = bf16[1,48,1152]{2,1,0:T(8,128)(2,1)S(1)} collective-permute-done((bf16[1,48,1152]{2,1,0:T(8,128)(2,1)S(1)}, bf16[1,48,1152]{2,1,0:T(8,128)(2,1)S(1)}, u32[]{:S(2)}, u32[]{:S(2)}) %collective-permute-start.53) | collective-permute-done | bytes 110624 | tf_op jit(solution)/shard_map/ppermute | solution.py:784
  183.5 2.7 %collective-permute-done.49.received = bf16[1,48,512]{2,1,0:T(8,128)(2,1)S(1)} collective-permute-done((bf16[1,48,512]{2,1,0:T(8,128)(2,1)S(1)}, bf16[1,48,512]{2,1,0:T(8,128)(2,1)S(1)}, u32[]{:S(2)}, u32[]{:S(2)}) %collective-permute-start.49) | collective-permute-done | bytes 49184 | tf_op jit(solution)/shard_map/ppermute | solution.py:784
  186.4 9.5 %all_to_all.11 = f32[32,1,768]{2,1,0:T(1,128)S(1)} all-to-all(f32[32,1,768]{2,1,0:T(1,128)S(1)} %copy.69), channel_id=1, replica_groups=mesh['win'=8,'ch'=4] {'win','ch'}, dimensions={0} | all-to-all | bytes 196608 | tf_op jit(solution)/shard_map/all_to_all | solution.py:1706
  (214 shorter events, 76.8 us)
Async XLA Ops:
  18.5 8.3 %collective-permute-start.5 = (bf16[2,48,768]{2,1,0:T(8,128)(2,1)S(1)}, bf16[2,48,768]{2,1,0:T(8,128)(2,1)S(1)}, u32[]{:S(2)}, u32[]{:S(2)}) collective-permute-start(bf16[2,48,768]{2,1,0:T(8,128)(2,1)S(1)} %get-tuple-element.296.refs_4_), channel_id=1, source_target_pairs={{0,8},{4,12},{8,0},{12,4},{16,24},{20,28},{24,16},{28,20},{1,9},{5... | collective-permute-start | bytes 442376 | tf_op jit(solution)/shard_map/ppermute | solution.py:784
  27.5 9.0 %collective-permute-start.11 = (bf16[2,48,1408]{2,1,0:T(8,128)(2,1)S(1)}, bf16[2,48,1408]{2,1,0:T(8,128)(2,1)S(1)}, u32[]{:S(2)}, u32[]{:S(2)}) collective-permute-start(bf16[2,48,1408]{2,1,0:T(8,128)(2,1)S(1)} %stack10.1.refs_0_), channel_id=1, source_target_pairs={{0,8},{4,12},{8,0},{12,4},{16,24},{20,28},{24,16},{28,20},{1,9},{5... | collective-permute-start | bytes 811016 | tf_op jit(solution)/shard_map/ppermute | solution.py:784
  37.8 11.8 %collective-permute-start.14 = (bf16[8,48,384]{2,1,0:T(8,128)(2,1)S(1)}, bf16[8,48,384]{2,1,0:T(8,128)(2,1)S(1)}, u32[]{:S(2)}, u32[]{:S(2)}) collective-permute-start(bf16[8,48,384]{2,1,0:T(8,128)(2,1)S(1)} %get-tuple-element.325.refs_0_), channel_id=1, source_target_pairs={{0,4},{4,0},{8,12},{12,8},{16,20},{20,16},{24,28},{28,24},{1,5},{5... | collective-permute-start | bytes 884744 | tf_op jit(solution)/shard_map/ppermute | solution.py:784
  39.0 10.6 %collective-permute-start.15 = (bf16[8,48,384]{2,1,0:T(8,128)(2,1)S(1)}, bf16[8,48,384]{2,1,0:T(8,128)(2,1)S(1)}, u32[]{:S(2)}, u32[]{:S(2)}) collective-permute-start(bf16[8,48,384]{2,1,0:T(8,128)(2,1)S(1)} %get-tuple-element.326.refs_2_), channel_id=1, source_target_pairs={{0,2},{1,3},{2,0},{3,1},{4,6},{5,7},{6,4},{7,5},{8,10},{9,11},{10,... | collective-permute-start | bytes 884744 | tf_op jit(solution)/shard_map/ppermute | solution.py:784
  41.1 9.7 %collective-permute-start.16 = (bf16[4,48,384]{2,1,0:T(8,128)(2,1)S(1)}, bf16[4,48,384]{2,1,0:T(8,128)(2,1)S(1)}, u32[]{:S(2)}, u32[]{:S(2)}) collective-permute-start(bf16[4,48,384]{2,1,0:T(8,128)(2,1)S(1)} %get-tuple-element.327.refs_4_), channel_id=1, source_target_pairs={{0,4},{4,0},{8,12},{12,8},{16,20},{20,16},{24,28},{28,24},{1,5},{5... | collective-permute-start | bytes 442376 | tf_op jit(solution)/shard_map/ppermute | solution.py:784
  41.9 11.1 %collective-permute-start.18 = (bf16[4,48,384]{2,1,0:T(8,128)(2,1)S(1)}, bf16[4,48,384]{2,1,0:T(8,128)(2,1)S(1)}, u32[]{:S(2)}, u32[]{:S(2)}) collective-permute-start(bf16[4,48,384]{2,1,0:T(8,128)(2,1)S(1)} %get-tuple-element.329.refs_8_), channel_id=1, source_target_pairs={{0,4},{4,0},{8,12},{12,8},{16,20},{20,16},{24,28},{28,24},{1,5},{5... | collective-permute-start | bytes 442376 | tf_op jit(solution)/shard_map/ppermute | solution.py:784
  43.2 9.9 %collective-permute-start.17 = (bf16[4,48,640]{2,1,0:T(8,128)(2,1)S(1)}, bf16[4,48,640]{2,1,0:T(8,128)(2,1)S(1)}, u32[]{:S(2)}, u32[]{:S(2)}) collective-permute-start(bf16[4,48,640]{2,1,0:T(8,128)(2,1)S(1)} %get-tuple-element.328.refs_6_), channel_id=1, source_target_pairs={{0,2},{1,3},{2,0},{3,1},{4,6},{5,7},{6,4},{7,5},{8,10},{9,11},{10,... | collective-permute-start | bytes 737288 | tf_op jit(solution)/shard_map/ppermute | solution.py:784
  53.8 10.0 %collective-permute-start.21 = (bf16[8,48,384]{2,1,0:T(8,128)(2,1)S(1)}, bf16[8,48,384]{2,1,0:T(8,128)(2,1)S(1)}, u32[]{:S(2)}, u32[]{:S(2)}) collective-permute-start(bf16[8,48,384]{2,1,0:T(8,128)(2,1)S(1)} %get-tuple-element.350.refs_0_), channel_id=1, source_target_pairs={{0,2},{1,3},{2,0},{3,1},{4,6},{5,7},{6,4},{7,5},{8,10},{9,11},{10,... | collective-permute-start | bytes 884744 | tf_op jit(solution)/shard_map/ppermute | solution.py:784
  55.4 21.2 %collective-permute-start.24 = (bf16[8,48,384]{2,1,0:T(8,128)(2,1)S(1)}, bf16[8,48,384]{2,1,0:T(8,128)(2,1)S(1)}, u32[]{:S(2)}, u32[]{:S(2)}) collective-permute-start(bf16[8,48,384]{2,1,0:T(8,128)(2,1)S(1)} %get-tuple-element.363.refs_2_), channel_id=1, source_target_pairs={{0,2},{1,3},{2,0},{3,1},{4,6},{5,7},{6,4},{7,5},{8,10},{9,11},{10,... | collective-permute-start | bytes 884744 | tf_op jit(solution)/shard_map/ppermute | solution.py:784
  55.9 20.7 %collective-permute-start.23 = (bf16[8,48,640]{2,1,0:T(8,128)(2,1)S(1)}, bf16[8,48,640]{2,1,0:T(8,128)(2,1)S(1)}, u32[]{:S(2)}, u32[]{:S(2)}) collective-permute-start(bf16[8,48,640]{2,1,0:T(8,128)(2,1)S(1)} %get-tuple-element.362.refs_0_), channel_id=1, source_target_pairs={{0,4},{4,0},{8,12},{12,8},{16,20},{20,16},{24,28},{28,24},{1,5},{5... | collective-permute-start | bytes 1474568 | tf_op jit(solution)/shard_map/ppermute | solution.py:784
  104.9 11.5 %collective-permute-start.29 = (bf16[8,48,512]{2,1,0:T(8,128)(2,1)S(1)}, bf16[8,48,512]{2,1,0:T(8,128)(2,1)S(1)}, u32[]{:S(2)}, u32[]{:S(2)}) collective-permute-start(bf16[8,48,512]{2,1,0:T(8,128)(2,1)S(1)} %get-tuple-element.405), channel_id=1, source_target_pairs={{0,2},{1,3},{2,0},{3,1},{4,6},{5,7},{6,4},{7,5},{8,10},{9,11},{10,... | collective-permute-start | bytes 1179656 | tf_op jit(solution)/shard_map/ppermute | solution.py:784
  106.5 11.2 %collective-permute-start.30 = (bf16[8,48,512]{2,1,0:T(8,128)(2,1)S(1)}, bf16[8,48,512]{2,1,0:T(8,128)(2,1)S(1)}, u32[]{:S(2)}, u32[]{:S(2)}) collective-permute-start(bf16[8,48,512]{2,1,0:T(8,128)(2,1)S(1)} %get-tuple-element.406), channel_id=1, source_target_pairs={{0,4},{4,0},{8,12},{12,8},{16,20},{20,16},{24,28},{28,24},{1,5},{5... | collective-permute-start | bytes 1179656 | tf_op jit(solution)/shard_map/ppermute | solution.py:784
  114.8 13.9 %collective-permute-start.33 = (bf16[16,48,384]{2,1,0:T(8,128)(2,1)S(1)}, bf16[16,48,384]{2,1,0:T(8,128)(2,1)S(1)}, u32[]{:S(2)}, u32[]{:S(2)}) collective-permute-start(bf16[16,48,384]{2,1,0:T(8,128)(2,1)S(1)} %bitcast.85), channel_id=1, source_target_pairs={{0,1},{1,0},{2,3},{3,2},{4,5},{5,4},{6,7},{7,6},{8,9},{9,8},{10,11... | collective-permute-start | bytes 1769480 | tf_op jit(solution)/shard_map/ppermute | solution.py:784
  118.4 10.3 %collective-permute-start.31 = (bf16[4,48,512]{2,1,0:T(8,128)(2,1)S(1)}, bf16[4,48,512]{2,1,0:T(8,128)(2,1)S(1)}, u32[]{:S(2)}, u32[]{:S(2)}) collective-permute-start(bf16[4,48,512]{2,1,0:T(8,128)(2,1)S(1)} %get-tuple-element.421), channel_id=1, source_target_pairs={{0,4},{4,0},{8,12},{12,8},{16,20},{20,16},{24,28},{28,24},{1,5},{5... | collective-permute-start | bytes 589832 | tf_op jit(solution)/shard_map/ppermute | solution.py:784
  119.7 8.9 %collective-permute-start.32 = (bf16[4,48,512]{2,1,0:T(8,128)(2,1)S(1)}, bf16[4,48,512]{2,1,0:T(8,128)(2,1)S(1)}, u32[]{:S(2)}, u32[]{:S(2)}) collective-permute-start(bf16[4,48,512]{2,1,0:T(8,128)(2,1)S(1)} %get-tuple-element.422), channel_id=1, source_target_pairs={{0,2},{1,3},{2,0},{3,1},{4,6},{5,7},{6,4},{7,5},{8,10},{9,11},{10,... | collective-permute-start | bytes 589832 | tf_op jit(solution)/shard_map/ppermute | solution.py:784
  128.1 11.7 %collective-permute-start.35 = (bf16[16,48,384]{2,1,0:T(8,128)(2,1)S(1)}, bf16[16,48,384]{2,1,0:T(8,128)(2,1)S(1)}, u32[]{:S(2)}, u32[]{:S(2)}) collective-permute-start(bf16[16,48,384]{2,1,0:T(8,128)(2,1)S(1)} %bitcast.87), channel_id=1, source_target_pairs={{0,1},{1,0},{2,3},{3,2},{4,5},{5,4},{6,7},{7,6},{8,9},{9,8},{10,11... | collective-permute-start | bytes 1769480 | tf_op jit(solution)/shard_map/ppermute | solution.py:784
  128.1 11.6 %collective-permute-start.36 = (bf16[16,48,384]{2,1,0:T(8,128)(2,1)S(1)}, bf16[16,48,384]{2,1,0:T(8,128)(2,1)S(1)}, u32[]{:S(2)}, u32[]{:S(2)}) collective-permute-start(bf16[16,48,384]{2,1,0:T(8,128)(2,1)S(1)} %bitcast.86), channel_id=1, source_target_pairs={{0,1},{1,0},{2,3},{3,2},{4,5},{5,4},{6,7},{7,6},{8,9},{9,8},{10,11... | collective-permute-start | bytes 1769480 | tf_op jit(solution)/shard_map/ppermute | solution.py:784
  131.1 8.7 %collective-permute-start.34 = (bf16[8,48,384]{2,1,0:T(8,128)(2,1)S(1)}, bf16[8,48,384]{2,1,0:T(8,128)(2,1)S(1)}, u32[]{:S(2)}, u32[]{:S(2)}) collective-permute-start(bf16[8,48,384]{2,1,0:T(8,128)(2,1)S(1)} %get-tuple-element.440), channel_id=1, source_target_pairs={{0,2},{1,3},{2,0},{3,1},{4,6},{5,7},{6,4},{7,5},{8,10},{9,11},{10,... | collective-permute-start | bytes 884744 | tf_op jit(solution)/shard_map/ppermute | solution.py:784
  140.7 13.8 %collective-permute-start.41 = (bf16[1,48,1024]{2,1,0:T(8,128)(2,1)S(1)}, bf16[1,48,1024]{2,1,0:T(8,128)(2,1)S(1)}, u32[]{:S(2)}, u32[]{:S(2)}) collective-permute-start(bf16[1,48,1024]{2,1,0:T(8,128)(2,1)S(1)} %get-tuple-element.487), channel_id=1, source_target_pairs={{0,16},{4,20},{8,24},{12,28},{16,0},{20,4},{24,8},{28,12},{1,17},{... | collective-permute-start | bytes 294920 | tf_op jit(solution)/shard_map/ppermute | solution.py:784
  142.3 12.2 %collective-permute-start.38 = (bf16[4,48,384]{2,1,0:T(8,128)(2,1)S(1)}, bf16[4,48,384]{2,1,0:T(8,128)(2,1)S(1)}, u32[]{:S(2)}, u32[]{:S(2)}) collective-permute-start(bf16[4,48,384]{2,1,0:T(8,128)(2,1)S(1)} %get-tuple-element.484), channel_id=1, source_target_pairs={{0,4},{4,0},{8,12},{12,8},{16,20},{20,16},{24,28},{28,24},{1,5},{5... | collective-permute-start | bytes 442376 | tf_op jit(solution)/shard_map/ppermute | solution.py:784
  143.0 11.5 %collective-permute-start.39 = (bf16[8,48,384]{2,1,0:T(8,128)(2,1)S(1)}, bf16[8,48,384]{2,1,0:T(8,128)(2,1)S(1)}, u32[]{:S(2)}, u32[]{:S(2)}) collective-permute-start(bf16[8,48,384]{2,1,0:T(8,128)(2,1)S(1)} %get-tuple-element.485), channel_id=1, source_target_pairs={{0,2},{1,3},{2,0},{3,1},{4,6},{5,7},{6,4},{7,5},{8,10},{9,11},{10,... | collective-permute-start | bytes 884744 | tf_op jit(solution)/shard_map/ppermute | solution.py:784
  144.5 10.1 %collective-permute-start.40 = (bf16[8,48,384]{2,1,0:T(8,128)(2,1)S(1)}, bf16[8,48,384]{2,1,0:T(8,128)(2,1)S(1)}, u32[]{:S(2)}, u32[]{:S(2)}) collective-permute-start(bf16[8,48,384]{2,1,0:T(8,128)(2,1)S(1)} %get-tuple-element.486), channel_id=1, source_target_pairs={{0,4},{4,0},{8,12},{12,8},{16,20},{20,16},{24,28},{28,24},{1,5},{5... | collective-permute-start | bytes 884744 | tf_op jit(solution)/shard_map/ppermute | solution.py:784
  157.8 8.5 %collective-permute-start.44 = (bf16[8,48,256]{2,1,0:T(8,128)(2,1)S(1)}, bf16[8,48,256]{2,1,0:T(8,128)(2,1)S(1)}, u32[]{:S(2)}, u32[]{:S(2)}) collective-permute-start(bf16[8,48,256]{2,1,0:T(8,128)(2,1)S(1)} %get-tuple-element.502), channel_id=1, source_target_pairs={{0,2},{1,3},{2,0},{3,1},{4,6},{5,7},{6,4},{7,5},{8,10},{9,11},{10,... | collective-permute-start | bytes 589832 | tf_op jit(solution)/shard_map/ppermute | solution.py:784
  164.0 11.6 %collective-permute-start.52 = (bf16[2,48,1152]{2,1,0:T(8,128)(2,1)S(1)}, bf16[2,48,1152]{2,1,0:T(8,128)(2,1)S(1)}, u32[]{:S(2)}, u32[]{:S(2)}) collective-permute-start(bf16[2,48,1152]{2,1,0:T(8,128)(2,1)S(1)} %get-tuple-element.520), channel_id=1, source_target_pairs={{0,8},{4,12},{8,0},{12,4},{16,24},{20,28},{24,16},{28,20},{1,9},{5... | collective-permute-start | bytes 663560 | tf_op jit(solution)/shard_map/ppermute | solution.py:784
  (70 other events, 925.8 us)

commit v3 on v2

--- a/solution.py
+++ b/solution.py
@@ -43,7 +43,7 @@
 TN = (((0,), (0,)), ((), ()))
 VMEM_LIMIT = 24 * 1024 * 1024
 GROUP = 2
-CHUNK = 512
+CHUNK = 768
 
 
 def dot(a, b, dims=NN):

time: 202 us -> 201 us (level)
  no operation moved by 1% of the time
where the time goes in v3:
time: 201 us; the launch traced here: 197 us
  Pallas kernels  93.2 us (46%)
  starting transfers between devices  52.2 us (26%)
  waiting for transfers between devices  35.5 us (18%)
  blocking collectives  9.51 us (5%)
  local copies, waits for them, and re-layouts  3.03 us (2%)
  between operations  2.05 us (1%)
    pallas_call x11, Pallas kernels, call(): pl.pallas_call(kernel, grid=(groups,), in_specs=[spec for spec, _ in ins....  75.7 us
    ppermute x54, starting transfers between devices, exchange(): return lax.ppermute(array, axis, [(i, i ^ 1 << bit) for i in range(size)])  52.2 us
    ppermute x54, waiting for transfers between devices, exchange(): return lax.ppermute(array, axis, [(i, i ^ 1 << bit) for i in range(size)])  35.5 us
    pallas_call x25, Pallas kernels, small_call(): pl.pallas_call(kernel, grid=(1,) if stream else (), out_shape=[jax.ShapeD...  17.4 us
    all_to_all x1, blocking collectives, per_device(): message = lax.all_to_all(message, ('win', 'ch'), 0, 0, tiled=True)  9.51 us
  transfers between devices with their start and end apart: 54, of which 17 were waited for; matrix products, arithmetic and copies ran while one was open for 2% of the time, Pallas kernels for 35%

profile of v3, /device:TPU:0, one launch (start us, length us, event | category | flops | bytes accessed | tf_op | source)
XLA Modules:
  0.0 197.4 jit_solution(9415846701742058308)
XLA Ops:
  0.7 1.8 pack.1
  2.5 4.0 %collective-permute-start = (bf16[1,48,384]{2,1,0:T(8,128)(2,1)}, bf16[1,48,384]{2,1,0:T(8,128)(2,1)S(1)}, u32[]{:S(2)}, u32[]{:S(2)}) collective-permute-start(bf16[1,48,384]{2,1,0:T(8,128)(2,1)} %bitcast.77), channel_id=1, source_target_pairs={{0,16},{4,20},{8,24},{12,28},{16,0},{20,4},{24,8},{28,12},{1,17},{... | collective-permute-start | bytes 110600 | tf_op jit(solution)/shard_map/ppermute | solution.py:784
  12.0 2.0 %collective-permute-start.2 = (bf16[1,48,768]{2,1,0:T(8,128)(2,1)S(1)}, bf16[1,48,768]{2,1,0:T(8,128)(2,1)S(1)}, u32[]{:S(2)}, u32[]{:S(2)}) collective-permute-start(bf16[1,48,768]{2,1,0:T(8,128)(2,1)S(1)} %bitcast.75), channel_id=1, source_target_pairs={{0,16},{4,20},{8,24},{12,28},{16,0},{20,4},{24,8},{28,12},{1,17},{... | collective-permute-start | bytes 221192 | tf_op jit(solution)/shard_map/ppermute | solution.py:784
  15.5 2.5 %collective-permute-done.2.refs_3_ = bf16[1,48,768]{2,1,0:T(8,128)(2,1)S(1)} collective-permute-done((bf16[1,48,768]{2,1,0:T(8,128)(2,1)S(1)}, bf16[1,48,768]{2,1,0:T(8,128)(2,1)S(1)}, u32[]{:S(2)}, u32[]{:S(2)}) %collective-permute-start.2) | collective-permute-done | bytes 73760 | tf_op jit(solution)/shard_map/ppermute | solution.py:784
  23.2 3.0 %collective-permute-done.8.refs_1_ = bf16[1,48,1408]{2,1,0:T(8,128)(2,1)S(1)} collective-permute-done((bf16[1,48,1408]{2,1,0:T(8,128)(2,1)S(1)}, bf16[1,48,1408]{2,1,0:T(8,128)(2,1)S(1)}, u32[]{:S(2)}, u32[]{:S(2)}) %collective-permute-start.8) | collective-permute-done | bytes 135200 | tf_op jit(solution)/shard_map/ppermute | solution.py:784
  32.3 4.2 %collective-permute-done.7.refs_3_ = bf16[8,48,128]{2,1,0:T(8,128)(2,1)S(1)} collective-permute-done((bf16[8,48,128]{2,1,0:T(8,128)(2,1)S(1)}, bf16[8,48,128]{2,1,0:T(8,128)(2,1)S(1)}, u32[]{:S(2)}, u32[]{:S(2)}) %collective-permute-start.7) | collective-permute-done | bytes 98336 | tf_op jit(solution)/shard_map/ppermute | solution.py:784
  43.8 5.8 %attention_forward0_0.1 = (f32[2,208,384]{2,1,0:T(8,128)S(1)}, bf16[2,208,384]{2,1,0:T(8,128)(2,1)S(1)}, bf16[2,256,1152]{2,1,0:T(8,128)(2,1)S(1)}, bf16[2,4,3,6...) custom-call(bf16[2,384,256]{2,1,0:T(8,128)(2,1)S(1)} %bitcast.97, ...), custom_call_target="tpu_custom_call" | custom-call | flops 7851737088 | bytes 2731560 | tf_op jit(solution)/shard_map/attention_forward0_0/pallas_call | solution.py:765
  50.8 2.3 %collective-permute-done.18.refs_9_ = bf16[4,48,384]{2,1,0:T(8,128)(2,1)S(1)} collective-permute-done((bf16[4,48,384]{2,1,0:T(8,128)(2,1)S(1)}, bf16[4,48,384]{2,1,0:T(8,128)(2,1)S(1)}, u32[]{:S(2)}, u32[]{:S(2)}) %collective-permute-start.18) | collective-permute-done | bytes 147488 | tf_op jit(solution)/shard_map/ppermute | solution.py:784
  57.7 4.8 %attention_forward0_1.1 = (f32[2,208,384]{2,1,0:T(8,128)S(1)}, bf16[2,208,384]{2,1,0:T(8,128)(2,1)S(1)}, bf16[2,256,1152]{2,1,0:T(8,128)(2,1)S(1)}, bf16[2,4,3,6...) custom-call(bf16[4,208,384]{2,1,0:T(8,128)(2,1)S(1)} %pad.4.refs_5_.refs_0_.refs_7_, bf16[256,208]{1,0:T(8,128)(2,1)S(1)} %copy-done.29, ...), custom_call_target="tpu_custom_call" | custom-call | flops 7851737088 | bytes 2731552 | tf_op jit(solution)/shard_map/attention_forward0_1/pallas_call | solution.py:765
  64.6 5.6 %first_mlp.1 = (f32[4,208,384]{2,1,0:T(8,128)S(1)}, bf16[4,208,384]{2,1,0:T(8,128)(2,1)S(1)}, bf16[4,208,1536]{2,1,0:T(8,128)(2,1)S(1)}, bf16[4,208,1536]{2,1,0:...) custom-call(bf16[2,384,384]{2,1,0:T(8,128)(2,1)S(1)} %bitcast.88, ...), custom_call_target="tpu_custom_call" | custom-call | flops 15703474176 | bytes 3681800 | tf_op jit(solution)/shard_map/first_mlp/pallas_call | solution.py:765
  70.2 6.0 %attention_forward1_0.1 = (f32[2,208,384]{2,1,0:T(8,128)S(1)}, bf16[2,208,384]{2,1,0:T(8,128)(2,1)S(1)}, bf16[2,256,1152]{2,1,0:T(8,128)(2,1)S(1)}, bf16[2,4,3,6...) custom-call(bf16[2,384,384]{2,1,0:T(8,128)(2,1)S(1)} %bitcast.61, ...), custom_call_target="tpu_custom_call" | custom-call | flops 7851737088 | bytes 3370536 | tf_op jit(solution)/shard_map/attention_forward1_0/pallas_call | solution.py:765
  77.5 4.8 %attention_forward1_1.1 = (f32[2,208,384]{2,1,0:T(8,128)S(1)}, bf16[2,208,384]{2,1,0:T(8,128)(2,1)S(1)}, bf16[2,256,1152]{2,1,0:T(8,128)(2,1)S(1)}, bf16[2,4,3,6...) custom-call(f32[4,208,384]{2,1,0:T(8,128)S(1)} %get-tuple-element.359.refs_3_.refs_0_.refs_7_, ...), custom_call_target="tpu_custom_call" | custom-call | flops 7851737088 | bytes 3370528 | tf_op jit(solution)/shard_map/attention_forward1_1/pallas_call | solution.py:765
  82.3 15.1 %last_mlp.1 = (f32[4,208,384]{2,1,0:T(8,128)S(1)}, f32[8,384]{1,0:T(8,128)S(1)}, f32[1,1536]{1,0:T(1,128)S(1)}, f32[2,384]{1,0:T(2,128)S(1)}, f32[1,1024]{1,0:T(...) custom-call(bf16[2,384,640]{2,1,0:T(8,128)(2,1)S(1)} %bitcast.81, ...), custom_call_target="tpu_custom_call" | custom-call | flops 47110422528 | bytes 4470472 | tf_op jit(solution)/shard_map/last_mlp/pallas_call | solution.py:765
  98.1 5.3 %attention_backward1_0.1 = (f32[8,384]{1,0:T(8,128)S(1)}, f32[1,1152]{1,0:T(1,128)S(1)}, f32[3,64,256]{2,1,0:T(8,128)S(1)}, f32[2,208,384]{2,1,0:T(8,128)S(1)}, ...) custom-call(s32[2]{0:T(128)S(1)} %pad_add_fusion.me_ref.refs_4_.refs_2_.refs_0_, ...), custom_call_target="tpu_custom_call" | custom-call | flops 15703474176 | bytes 5959176 | tf_op jit(solution)/shard_map/attention_backward1_0/pallas_call | solution.py:765
  107.1 7.0 %attention_backward1_1.1 = (f32[8,384]{1,0:T(8,128)S(1)}, f32[1,1152]{1,0:T(1,128)S(1)}, f32[3,64,256]{2,1,0:T(8,128)S(1)}, f32[2,208,384]{2,1,0:T(8,128)S(1)}, ...) custom-call(s32[2]{0:T(128)S(1)} %pad_add_fusion.me_ref.refs_4_.refs_2_.refs_0_, ...), custom_call_target="tpu_custom_call" | custom-call | flops 15703474176 | bytes 8728584 | tf_op jit(solution)/shard_map/attention_backward1_1/pallas_call | solution.py:765
  119.6 7.7 %mlp_backward0.1 = (f32[4,208,384]{2,1,0:T(8,128)S(1)}, f32[8,384]{1,0:T(8,128)S(1)}, f32[1,1536]{1,0:T(1,128)S(1)}, bf16[2,384,384]{2,1,0:T(8,128)(2,1)S(1)}, b...) custom-call(s32[2]{0:T(128)S(1)} %pad_add_fusion.me_ref.refs_4_.refs_2_.refs_0_, ...), custom_call_target="tpu_custom_call" | custom-call | flops 31406948352 | bytes 10710536 | tf_op jit(solution)/shard_map/mlp_backward0/pallas_call | solution.py:765
  131.8 5.1 %attention_backward0_0.1 = (f32[8,384]{1,0:T(8,128)S(1)}, f32[1,1152]{1,0:T(1,128)S(1)}, f32[3,64,256]{2,1,0:T(8,128)S(1)}, bf16[416,1152]{1,0:T(8,128)(2,1)S(1)}, bf16[416,384]{1,0:T(8,128)(2,1)S(1)}) custom-call(s32[2]{0:T(128)S(1)} %pad_add_fusion.me_ref.refs_4_.refs_2_.refs_0_, bf16[384,1152]{1,0:T(8,128)(2,1)S(1)} %get-tuple-element.342.refs_9_.refs_1_, ...), custom_call_target="tpu_custom_call" | custom-call | flops 15703474176 | bytes 5320200 | tf_op jit(solution)/shard_map/attention_backward0_0/pallas_call | solution.py:765
  136.9 2.1 %collective-permute-done.34.refs_1_ = bf16[8,48,384]{2,1,0:T(8,128)(2,1)S(1)} collective-permute-done((bf16[8,48,384]{2,1,0:T(8,128)(2,1)S(1)}, bf16[8,48,384]{2,1,0:T(8,128)(2,1)S(1)}, u32[]{:S(2)}, u32[]{:S(2)}) %collective-permute-start.34) | collective-permute-done | bytes 294944 | tf_op jit(solution)/shard_map/ppermute | solution.py:784
  145.0 8.7 %attention_backward0_1.1 = (f32[8,384]{1,0:T(8,128)}, f32[1,1152]{1,0:T(1,128)}, f32[3,64,256]{2,1,0:T(8,128)}, bf16[2,384,256]{2,1,0:T(8,128)(2,1)S(1)}, bf16[2...) custom-call(s32[2]{0:T(128)S(1)} %pad_add_fusion.me_ref.refs_4_.refs_2_.refs_0_, ...), custom_call_target="tpu_custom_call" | custom-call | flops 15703474176 | bytes 8347656 | tf_op jit(solution)/shard_map/attention_backward0_1/pallas_call | solution.py:765
  168.4 2.7 %collective-permute-done.46.refs_1_ = bf16[4,48,256]{2,1,0:T(8,128)(2,1)S(1)} collective-permute-done((bf16[4,48,256]{2,1,0:T(8,128)(2,1)S(1)}, bf16[4,48,256]{2,1,0:T(8,128)(2,1)S(1)}, u32[]{:S(2)}, u32[]{:S(2)}) %collective-permute-start.46) | collective-permute-done | bytes 98336 | tf_op jit(solution)/shard_map/ppermute | solution.py:784
  175.7 3.7 %collective-permute-done.48.refs_1_ = bf16[2,48,512]{2,1,0:T(8,128)(2,1)S(1)} collective-permute-done((bf16[2,48,512]{2,1,0:T(8,128)(2,1)S(1)}, bf16[2,48,512]{2,1,0:T(8,128)(2,1)S(1)}, u32[]{:S(2)}, u32[]{:S(2)}) %collective-permute-start.48) | collective-permute-done | bytes 98336 | tf_op jit(solution)/shard_map/ppermute | solution.py:784
  180.3 2.2 %collective-permute-done.53.received = bf16[1,48,1152]{2,1,0:T(8,128)(2,1)S(1)} collective-permute-done((bf16[1,48,1152]{2,1,0:T(8,128)(2,1)S(1)}, bf16[1,48,1152]{2,1,0:T(8,128)(2,1)S(1)}, u32[]{:S(2)}, u32[]{:S(2)}) %collective-permute-start.53) | collective-permute-done | bytes 110624 | tf_op jit(solution)/shard_map/ppermute | solution.py:784
  182.7 2.7 %collective-permute-done.49.received = bf16[1,48,512]{2,1,0:T(8,128)(2,1)S(1)} collective-permute-done((bf16[1,48,512]{2,1,0:T(8,128)(2,1)S(1)}, bf16[1,48,512]{2,1,0:T(8,128)(2,1)S(1)}, u32[]{:S(2)}, u32[]{:S(2)}) %collective-permute-start.49) | collective-permute-done | bytes 49184 | tf_op jit(solution)/shard_map/ppermute | solution.py:784
  185.7 9.5 %all_to_all.11 = f32[32,1,768]{2,1,0:T(1,128)S(1)} all-to-all(f32[32,1,768]{2,1,0:T(1,128)S(1)} %copy.69), channel_id=1, replica_groups=mesh['win'=8,'ch'=4] {'win','ch'}, dimensions={0} | all-to-all | bytes 196608 | tf_op jit(solution)/shard_map/all_to_all | solution.py:1706
  (214 shorter events, 76.7 us)
Async XLA Ops:
  18.5 8.3 %collective-permute-start.5 = (bf16[2,48,768]{2,1,0:T(8,128)(2,1)S(1)}, bf16[2,48,768]{2,1,0:T(8,128)(2,1)S(1)}, u32[]{:S(2)}, u32[]{:S(2)}) collective-permute-start(bf16[2,48,768]{2,1,0:T(8,128)(2,1)S(1)} %get-tuple-element.296.refs_4_), channel_id=1, source_target_pairs={{0,8},{4,12},{8,0},{12,4},{16,24},{20,28},{24,16},{28,20},{1,9},{5... | collective-permute-start | bytes 442376 | tf_op jit(solution)/shard_map/ppermute | solution.py:784
  27.5 9.0 %collective-permute-start.11 = (bf16[2,48,1408]{2,1,0:T(8,128)(2,1)S(1)}, bf16[2,48,1408]{2,1,0:T(8,128)(2,1)S(1)}, u32[]{:S(2)}, u32[]{:S(2)}) collective-permute-start(bf16[2,48,1408]{2,1,0:T(8,128)(2,1)S(1)} %stack10.1.refs_0_), channel_id=1, source_target_pairs={{0,8},{4,12},{8,0},{12,4},{16,24},{20,28},{24,16},{28,20},{1,9},{5... | collective-permute-start | bytes 811016 | tf_op jit(solution)/shard_map/ppermute | solution.py:784
  37.8 11.8 %collective-permute-start.14 = (bf16[8,48,384]{2,1,0:T(8,128)(2,1)S(1)}, bf16[8,48,384]{2,1,0:T(8,128)(2,1)S(1)}, u32[]{:S(2)}, u32[]{:S(2)}) collective-permute-start(bf16[8,48,384]{2,1,0:T(8,128)(2,1)S(1)} %get-tuple-element.325.refs_0_), channel_id=1, source_target_pairs={{0,4},{4,0},{8,12},{12,8},{16,20},{20,16},{24,28},{28,24},{1,5},{5... | collective-permute-start | bytes 884744 | tf_op jit(solution)/shard_map/ppermute | solution.py:784
  39.0 10.6 %collective-permute-start.15 = (bf16[8,48,384]{2,1,0:T(8,128)(2,1)S(1)}, bf16[8,48,384]{2,1,0:T(8,128)(2,1)S(1)}, u32[]{:S(2)}, u32[]{:S(2)}) collective-permute-start(bf16[8,48,384]{2,1,0:T(8,128)(2,1)S(1)} %get-tuple-element.326.refs_2_), channel_id=1, source_target_pairs={{0,2},{1,3},{2,0},{3,1},{4,6},{5,7},{6,4},{7,5},{8,10},{9,11},{10,... | collective-permute-start | bytes 884744 | tf_op jit(solution)/shard_map/ppermute | solution.py:784
  41.1 9.7 %collective-permute-start.16 = (bf16[4,48,384]{2,1,0:T(8,128)(2,1)S(1)}, bf16[4,48,384]{2,1,0:T(8,128)(2,1)S(1)}, u32[]{:S(2)}, u32[]{:S(2)}) collective-permute-start(bf16[4,48,384]{2,1,0:T(8,128)(2,1)S(1)} %get-tuple-element.327.refs_4_), channel_id=1, source_target_pairs={{0,4},{4,0},{8,12},{12,8},{16,20},{20,16},{24,28},{28,24},{1,5},{5... | collective-permute-start | bytes 442376 | tf_op jit(solution)/shard_map/ppermute | solution.py:784
  41.9 11.1 %collective-permute-start.18 = (bf16[4,48,384]{2,1,0:T(8,128)(2,1)S(1)}, bf16[4,48,384]{2,1,0:T(8,128)(2,1)S(1)}, u32[]{:S(2)}, u32[]{:S(2)}) collective-permute-start(bf16[4,48,384]{2,1,0:T(8,128)(2,1)S(1)} %get-tuple-element.329.refs_8_), channel_id=1, source_target_pairs={{0,4},{4,0},{8,12},{12,8},{16,20},{20,16},{24,28},{28,24},{1,5},{5... | collective-permute-start | bytes 442376 | tf_op jit(solution)/shard_map/ppermute | solution.py:784
  43.2 9.9 %collective-permute-start.17 = (bf16[4,48,640]{2,1,0:T(8,128)(2,1)S(1)}, bf16[4,48,640]{2,1,0:T(8,128)(2,1)S(1)}, u32[]{:S(2)}, u32[]{:S(2)}) collective-permute-start(bf16[4,48,640]{2,1,0:T(8,128)(2,1)S(1)} %get-tuple-element.328.refs_6_), channel_id=1, source_target_pairs={{0,2},{1,3},{2,0},{3,1},{4,6},{5,7},{6,4},{7,5},{8,10},{9,11},{10,... | collective-permute-start | bytes 737288 | tf_op jit(solution)/shard_map/ppermute | solution.py:784
  53.8 10.0 %collective-permute-start.21 = (bf16[8,48,384]{2,1,0:T(8,128)(2,1)S(1)}, bf16[8,48,384]{2,1,0:T(8,128)(2,1)S(1)}, u32[]{:S(2)}, u32[]{:S(2)}) collective-permute-start(bf16[8,48,384]{2,1,0:T(8,128)(2,1)S(1)} %get-tuple-element.350.refs_0_), channel_id=1, source_target_pairs={{0,2},{1,3},{2,0},{3,1},{4,6},{5,7},{6,4},{7,5},{8,10},{9,11},{10,... | collective-permute-start | bytes 884744 | tf_op jit(solution)/shard_map/ppermute | solution.py:784
  55.4 20.8 %collective-permute-start.24 = (bf16[8,48,384]{2,1,0:T(8,128)(2,1)S(1)}, bf16[8,48,384]{2,1,0:T(8,128)(2,1)S(1)}, u32[]{:S(2)}, u32[]{:S(2)}) collective-permute-start(bf16[8,48,384]{2,1,0:T(8,128)(2,1)S(1)} %get-tuple-element.363.refs_2_), channel_id=1, source_target_pairs={{0,2},{1,3},{2,0},{3,1},{4,6},{5,7},{6,4},{7,5},{8,10},{9,11},{10,... | collective-permute-start | bytes 884744 | tf_op jit(solution)/shard_map/ppermute | solution.py:784
  55.9 20.3 %collective-permute-start.23 = (bf16[8,48,640]{2,1,0:T(8,128)(2,1)S(1)}, bf16[8,48,640]{2,1,0:T(8,128)(2,1)S(1)}, u32[]{:S(2)}, u32[]{:S(2)}) collective-permute-start(bf16[8,48,640]{2,1,0:T(8,128)(2,1)S(1)} %get-tuple-element.362.refs_0_), channel_id=1, source_target_pairs={{0,4},{4,0},{8,12},{12,8},{16,20},{20,16},{24,28},{28,24},{1,5},{5... | collective-permute-start | bytes 1474568 | tf_op jit(solution)/shard_map/ppermute | solution.py:784
  104.3 11.5 %collective-permute-start.29 = (bf16[8,48,512]{2,1,0:T(8,128)(2,1)S(1)}, bf16[8,48,512]{2,1,0:T(8,128)(2,1)S(1)}, u32[]{:S(2)}, u32[]{:S(2)}) collective-permute-start(bf16[8,48,512]{2,1,0:T(8,128)(2,1)S(1)} %get-tuple-element.405), channel_id=1, source_target_pairs={{0,2},{1,3},{2,0},{3,1},{4,6},{5,7},{6,4},{7,5},{8,10},{9,11},{10,... | collective-permute-start | bytes 1179656 | tf_op jit(solution)/shard_map/ppermute | solution.py:784
  105.8 11.2 %collective-permute-start.30 = (bf16[8,48,512]{2,1,0:T(8,128)(2,1)S(1)}, bf16[8,48,512]{2,1,0:T(8,128)(2,1)S(1)}, u32[]{:S(2)}, u32[]{:S(2)}) collective-permute-start(bf16[8,48,512]{2,1,0:T(8,128)(2,1)S(1)} %get-tuple-element.406), channel_id=1, source_target_pairs={{0,4},{4,0},{8,12},{12,8},{16,20},{20,16},{24,28},{28,24},{1,5},{5... | collective-permute-start | bytes 1179656 | tf_op jit(solution)/shard_map/ppermute | solution.py:784
  114.1 13.8 %collective-permute-start.33 = (bf16[16,48,384]{2,1,0:T(8,128)(2,1)S(1)}, bf16[16,48,384]{2,1,0:T(8,128)(2,1)S(1)}, u32[]{:S(2)}, u32[]{:S(2)}) collective-permute-start(bf16[16,48,384]{2,1,0:T(8,128)(2,1)S(1)} %bitcast.85), channel_id=1, source_target_pairs={{0,1},{1,0},{2,3},{3,2},{4,5},{5,4},{6,7},{7,6},{8,9},{9,8},{10,11... | collective-permute-start | bytes 1769480 | tf_op jit(solution)/shard_map/ppermute | solution.py:784
  117.7 10.2 %collective-permute-start.31 = (bf16[4,48,512]{2,1,0:T(8,128)(2,1)S(1)}, bf16[4,48,512]{2,1,0:T(8,128)(2,1)S(1)}, u32[]{:S(2)}, u32[]{:S(2)}) collective-permute-start(bf16[4,48,512]{2,1,0:T(8,128)(2,1)S(1)} %get-tuple-element.421), channel_id=1, source_target_pairs={{0,4},{4,0},{8,12},{12,8},{16,20},{20,16},{24,28},{28,24},{1,5},{5... | collective-permute-start | bytes 589832 | tf_op jit(solution)/shard_map/ppermute | solution.py:784
  119.1 8.8 %collective-permute-start.32 = (bf16[4,48,512]{2,1,0:T(8,128)(2,1)S(1)}, bf16[4,48,512]{2,1,0:T(8,128)(2,1)S(1)}, u32[]{:S(2)}, u32[]{:S(2)}) collective-permute-start(bf16[4,48,512]{2,1,0:T(8,128)(2,1)S(1)} %get-tuple-element.422), channel_id=1, source_target_pairs={{0,2},{1,3},{2,0},{3,1},{4,6},{5,7},{6,4},{7,5},{8,10},{9,11},{10,... | collective-permute-start | bytes 589832 | tf_op jit(solution)/shard_map/ppermute | solution.py:784
  127.3 11.7 %collective-permute-start.35 = (bf16[16,48,384]{2,1,0:T(8,128)(2,1)S(1)}, bf16[16,48,384]{2,1,0:T(8,128)(2,1)S(1)}, u32[]{:S(2)}, u32[]{:S(2)}) collective-permute-start(bf16[16,48,384]{2,1,0:T(8,128)(2,1)S(1)} %bitcast.87), channel_id=1, source_target_pairs={{0,1},{1,0},{2,3},{3,2},{4,5},{5,4},{6,7},{7,6},{8,9},{9,8},{10,11... | collective-permute-start | bytes 1769480 | tf_op jit(solution)/shard_map/ppermute | solution.py:784
  127.4 11.6 %collective-permute-start.36 = (bf16[16,48,384]{2,1,0:T(8,128)(2,1)S(1)}, bf16[16,48,384]{2,1,0:T(8,128)(2,1)S(1)}, u32[]{:S(2)}, u32[]{:S(2)}) collective-permute-start(bf16[16,48,384]{2,1,0:T(8,128)(2,1)S(1)} %bitcast.86), channel_id=1, source_target_pairs={{0,1},{1,0},{2,3},{3,2},{4,5},{5,4},{6,7},{7,6},{8,9},{9,8},{10,11... | collective-permute-start | bytes 1769480 | tf_op jit(solution)/shard_map/ppermute | solution.py:784
  130.3 8.7 %collective-permute-start.34 = (bf16[8,48,384]{2,1,0:T(8,128)(2,1)S(1)}, bf16[8,48,384]{2,1,0:T(8,128)(2,1)S(1)}, u32[]{:S(2)}, u32[]{:S(2)}) collective-permute-start(bf16[8,48,384]{2,1,0:T(8,128)(2,1)S(1)} %get-tuple-element.440), channel_id=1, source_target_pairs={{0,2},{1,3},{2,0},{3,1},{4,6},{5,7},{6,4},{7,5},{8,10},{9,11},{10,... | collective-permute-start | bytes 884744 | tf_op jit(solution)/shard_map/ppermute | solution.py:784
  140.0 13.8 %collective-permute-start.41 = (bf16[1,48,1024]{2,1,0:T(8,128)(2,1)S(1)}, bf16[1,48,1024]{2,1,0:T(8,128)(2,1)S(1)}, u32[]{:S(2)}, u32[]{:S(2)}) collective-permute-start(bf16[1,48,1024]{2,1,0:T(8,128)(2,1)S(1)} %get-tuple-element.487), channel_id=1, source_target_pairs={{0,16},{4,20},{8,24},{12,28},{16,0},{20,4},{24,8},{28,12},{1,17},{... | collective-permute-start | bytes 294920 | tf_op jit(solution)/shard_map/ppermute | solution.py:784
  141.5 12.2 %collective-permute-start.38 = (bf16[4,48,384]{2,1,0:T(8,128)(2,1)S(1)}, bf16[4,48,384]{2,1,0:T(8,128)(2,1)S(1)}, u32[]{:S(2)}, u32[]{:S(2)}) collective-permute-start(bf16[4,48,384]{2,1,0:T(8,128)(2,1)S(1)} %get-tuple-element.484), channel_id=1, source_target_pairs={{0,4},{4,0},{8,12},{12,8},{16,20},{20,16},{24,28},{28,24},{1,5},{5... | collective-permute-start | bytes 442376 | tf_op jit(solution)/shard_map/ppermute | solution.py:784
  142.2 11.5 %collective-permute-start.39 = (bf16[8,48,384]{2,1,0:T(8,128)(2,1)S(1)}, bf16[8,48,384]{2,1,0:T(8,128)(2,1)S(1)}, u32[]{:S(2)}, u32[]{:S(2)}) collective-permute-start(bf16[8,48,384]{2,1,0:T(8,128)(2,1)S(1)} %get-tuple-element.485), channel_id=1, source_target_pairs={{0,2},{1,3},{2,0},{3,1},{4,6},{5,7},{6,4},{7,5},{8,10},{9,11},{10,... | collective-permute-start | bytes 884744 | tf_op jit(solution)/shard_map/ppermute | solution.py:784
  143.7 10.0 %collective-permute-start.40 = (bf16[8,48,384]{2,1,0:T(8,128)(2,1)S(1)}, bf16[8,48,384]{2,1,0:T(8,128)(2,1)S(1)}, u32[]{:S(2)}, u32[]{:S(2)}) collective-permute-start(bf16[8,48,384]{2,1,0:T(8,128)(2,1)S(1)} %get-tuple-element.486), channel_id=1, source_target_pairs={{0,4},{4,0},{8,12},{12,8},{16,20},{20,16},{24,28},{28,24},{1,5},{5... | collective-permute-start | bytes 884744 | tf_op jit(solution)/shard_map/ppermute | solution.py:784
  157.1 8.5 %collective-permute-start.44 = (bf16[8,48,256]{2,1,0:T(8,128)(2,1)S(1)}, bf16[8,48,256]{2,1,0:T(8,128)(2,1)S(1)}, u32[]{:S(2)}, u32[]{:S(2)}) collective-permute-start(bf16[8,48,256]{2,1,0:T(8,128)(2,1)S(1)} %get-tuple-element.502), channel_id=1, source_target_pairs={{0,2},{1,3},{2,0},{3,1},{4,6},{5,7},{6,4},{7,5},{8,10},{9,11},{10,... | collective-permute-start | bytes 589832 | tf_op jit(solution)/shard_map/ppermute | solution.py:784
  163.2 11.6 %collective-permute-start.52 = (bf16[2,48,1152]{2,1,0:T(8,128)(2,1)S(1)}, bf16[2,48,1152]{2,1,0:T(8,128)(2,1)S(1)}, u32[]{:S(2)}, u32[]{:S(2)}) collective-permute-start(bf16[2,48,1152]{2,1,0:T(8,128)(2,1)S(1)} %get-tuple-element.520), channel_id=1, source_target_pairs={{0,8},{4,12},{8,0},{12,4},{16,24},{20,28},{24,16},{28,20},{1,9},{5... | collective-permute-start | bytes 663560 | tf_op jit(solution)/shard_map/ppermute | solution.py:784
  (70 other events, 923.9 us)
